TPU v7x, 256 devices: a whole 4x4x8 slice. The times are simulated.
256 devices in a mesh: row: 16 (over y, x), col: 16 (over z, core).
Axes of the slice: x: 4, y: 4, z: 8, core: 2. Of those that a mesh axis runs over, the one named last changes fastest.
Arguments:
- kernel_matrix: float32 [16384, 16384], P('row', 'col'), may hold values from -2 to 2, as said below
Outputs:
- factored: float32 [16384, 16384], P('row', 'col')
Inputs may be any that keep to these rules, and one draw needn't show every extreme that they name: `kernel_matrix`: the block of A's first 512 rows and columns is positive definite, read by its symmetric part.
All inputs are finite; a program needn't handle non-finite values.
Results may differ from a plain program's by a relative error of at most 0.0003.
Values sent between devices are 32-bit elements; how exact they have to be, the bound alone decides.
No kernel may reach another device: no remote copies, remote signals or barrier semaphores. Data moves between devices by JAX's collectives and lax.ppermute only.
A program may use at most 128 MiB of HBM per device.

v0:
```python
import jax
import jax.numpy as jnp
from jax import lax
from jax.sharding import PartitionSpec as P

NB = 256


def from_root(shard, axis, root):
    mine = lax.axis_index(axis) == root
    return lax.psum(jnp.where(mine, shard, jnp.zeros_like(shard)), axis)


def panel_step(tiles, step, prow, pcol, grid_c, row_nat):
    local_r = step // prow
    local_c = step // pcol
    tile = from_root(tiles[local_r, :, local_c, :], "row", step % prow)
    owner = grid_c == step % pcol
    tile = jnp.where(owner, tile, jnp.eye(NB, dtype=jnp.float32))
    lower = jnp.linalg.cholesky(tile)
    inverse = jax.scipy.linalg.solve_triangular(lower, jnp.eye(NB, dtype=jnp.float32), lower=True)
    column = tiles[:, :, local_c, :]
    panel = jnp.einsum("lia,ja->lij", column, inverse, precision=lax.Precision.HIGHEST)
    panel = jnp.where(row_nat[:, None, None] == step, lower[None], panel)
    panel = jnp.where(row_nat[:, None, None] < step, jnp.float32(0.0), panel)
    panel = jnp.where(owner, panel, jnp.float32(0.0))
    panel = from_root(panel, "col", step % pcol)
    ncols = tiles.shape[2]
    selected = panel.reshape(ncols, pcol // prow, NB, NB)
    picked = lax.dynamic_index_in_dim(selected, grid_c // prow, 1, keepdims=False)
    across = jnp.stack([from_root(picked[m], "row", grid_c % prow) for m in range(ncols)])
    return (panel, across)


def update_range(tiles, panel, across, first, last):
    product = jnp.einsum("lia,mja->limj", panel, across, precision=lax.Precision.HIGHEST)
    return tiles.at[:, :, first:last, :].set(tiles - product)


def per_device(kernel_matrix):
    prow = lax.axis_size("row")
    pcol = lax.axis_size("col")
    grid_r = lax.axis_index("row")
    grid_c = lax.axis_index("col")
    nrows = kernel_matrix.shape[0] // NB
    ncols = kernel_matrix.shape[1] // NB
    tiles = kernel_matrix.reshape(nrows, NB, ncols, NB)
    row_nat = jnp.arange(nrows, dtype=jnp.int32) * prow + grid_r
    col_nat = jnp.arange(ncols, dtype=jnp.int32) * pcol + grid_c
    panel0, across0 = panel_step(tiles, 0, prow, pcol, grid_c, row_nat)
    tiles = update_range(tiles, panel0, across0, 0, ncols)
    panel1, across1 = panel_step(tiles, 1, prow, pcol, grid_c, row_nat)
    tiles = update_range(tiles, panel1, across1, 0, ncols)
    rows_b = row_nat[:, None, None, None]
    cols_b = col_nat[None, None, :, None]
    trailing = jnp.where(rows_b >= cols_b, tiles, jnp.float32(0.0))
    result = jnp.where(cols_b == 1, panel1[:, :, None, :], trailing)
    result = jnp.where(cols_b == 0, panel0[:, :, None, :], result)
    return result.reshape(nrows * NB, ncols * NB)


def solution(mesh):
    return jax.shard_map(
        per_device,
        mesh=mesh,
        in_specs=(P("row", "col"),),
        out_specs=P("row", "col"),
        check_vma=False,
    )
```

profile of v0, /device:TPU:8, one launch (start us, length us, event | category | flops | bytes accessed | tf_op | source)
XLA Modules:
  0.0 800.8 jit_solution(2083935464988667970)
XLA Ops:
  6.5 5.6 reshape.215
  12.1 5.2 copy.17
  17.4 1.7 fusion.22
  19.2 96.8 %all-reduce.10.cloned.1.call-done = f32[256,256]{0,1:T(8,128)} async-done(((f32[256,256]{0,1:T(8,128)}), f32[256,256]{0,1:T(8,128)}) %all-reduce.10.cloned.1.call-update) | async-done | bytes 262160 | tf_op jit(solution)/shard_map/psum | solution.py:11
  118.2 11.7 %cholesky.130 = f32[128,128]{1,0:T(8,128)S(1)} custom-call(f32[128,128]{1,0:T(8,128)S(1)} %cholesky.194), custom_call_target="Cholesky" | custom-call | tf_op jit(solution)/shard_map/jit(cholesky)/cholesky | solution.py:20
  129.9 9.8 %custom-call.13 = f32[1,128,128]{1,2,0:T(8,128)S(1)} custom-call(f32[1,128,128]{2,1,0:T(8,128)S(1)} %get-tuple-element.110), custom_call_target="InvertDiagBlocksLowerTriangular" | custom-call | tf_op jit(solution)/shard_map/jit(cholesky)/cholesky | solution.py:20
  140.3 11.7 %cholesky.147 = f32[128,128]{1,0:T(8,128)S(1)} custom-call(f32[128,128]{1,0:T(8,128)S(1)} %convolution_subtract_fusion.4), custom_call_target="Cholesky" | custom-call | tf_op jit(solution)/shard_map/jit(cholesky)/cholesky | solution.py:20
  154.2 4.4 while.8
  155.3 1.3 bitcast_dynamic-update-slice_fusion.4
  158.6 19.7 %custom-call.14 = f32[2,128,128]{1,2,0:T(8,128)S(1)} custom-call(f32[2,128,128]{2,1,0:T(8,128)S(1)} %get-tuple-element.61), custom_call_target="InvertDiagBlocksLowerTriangular" | custom-call | tf_op jit(solution)/shard_map/jit(_solve_triangular)/triangular_solve | solution.py:21
  179.4 2.1 fusion.6
  181.6 109.6 %all-reduce.12.cloned.1.call-done = f32[4,256,256]{1,2,0:T(8,128)} async-done(((f32[4,256,256]{1,2,0:T(8,128)}), f32[4,256,256]{1,2,0:T(8,128)}) %all-reduce.12.cloned.1.call-update) | async-done | bytes 1048592 | tf_op jit(solution)/shard_map/psum | solution.py:11
  291.1 2.2 slice_select_fusion.8
  293.4 98.4 %all-reduce.20.cloned.1.call-done = (f32[1,256,256]{1,2,0:T(8,128)}, f32[1,256,256]{1,2,0:T(8,128)}, f32[1,256,256]{1,2,0:T(8,128)}, f32[1,256,256]{1,2,0:T(8,128)}) async-done(((f32[1,256,256]{1,2,0:T(8,128)}, f32[1,256,256]{1,2,0:T(8,128)}, f32[1,256,256]{1,2,0:T(8,128)}, f32[1,256,256]{1,2,0:T(8,128)}), (f32[1,256,256]{1,2,0:T(8,128)}, f32[1,256,256]{1,2,0:T(8,128)}, f32[1,256,256]{1,2,0:T(8,128)}, ...) | async-done | bytes 1048592 | tf_op jit(solution)/shard_map/psum | solution.py:11
  391.8 7.0 convolution_subtract_fusion
  398.8 1.9 copy-done
  401.7 93.9 %all-reduce.14.cloned.1.call-done = f32[256,256]{0,1:T(8,128)} async-done(((f32[256,256]{0,1:T(8,128)}), f32[256,256]{0,1:T(8,128)}) %all-reduce.14.cloned.1.call-update) | async-done | bytes 262160 | tf_op jit(solution)/shard_map/psum | solution.py:11
  495.8 11.7 %cholesky.164 = f32[128,128]{1,0:T(8,128)S(1)} custom-call(f32[128,128]{1,0:T(8,128)S(1)} %cholesky.197), custom_call_target="Cholesky" | custom-call | tf_op jit(solution)/shard_map/jit(cholesky)/cholesky | solution.py:20
  508.2 9.8 %custom-call.15 = f32[1,128,128]{1,2,0:T(8,128)S(1)} custom-call(f32[1,128,128]{2,1,0:T(8,128)S(1)} %get-tuple-element.106), custom_call_target="InvertDiagBlocksLowerTriangular" | custom-call | tf_op jit(solution)/shard_map/jit(cholesky)/cholesky | solution.py:20
  518.6 11.7 %cholesky.181 = f32[128,128]{1,0:T(8,128)S(1)} custom-call(f32[128,128]{1,0:T(8,128)S(1)} %convolution_subtract_fusion.3), custom_call_target="Cholesky" | custom-call | tf_op jit(solution)/shard_map/jit(cholesky)/cholesky | solution.py:20
  532.4 4.1 while.9
  536.5 19.7 %custom-call.16 = f32[2,128,128]{1,2,0:T(8,128)S(1)} custom-call(f32[2,128,128]{2,1,0:T(8,128)S(1)} %get-tuple-element.62), custom_call_target="InvertDiagBlocksLowerTriangular" | custom-call | tf_op jit(solution)/shard_map/jit(_solve_triangular)/triangular_solve | solution.py:21
  557.2 3.4 fusion.2
  560.6 111.3 %all-reduce.16.cloned.1.call-done = f32[4,256,256]{1,2,0:T(8,128)} async-done(((f32[4,256,256]{1,2,0:T(8,128)}), f32[4,256,256]{1,2,0:T(8,128)}) %all-reduce.16.cloned.1.call-update) | async-done | bytes 1048592 | tf_op jit(solution)/shard_map/psum | solution.py:11
  671.9 2.2 slice_select_fusion.3
  675.5 3.0 copy.50
  679.6 3.0 copy.51
  682.6 89.8 %all-reduce.18.cloned.1.call-done = (f32[1,256,256]{1,2,0:T(8,128)}, f32[1,256,256]{1,2,0:T(8,128)}, f32[1,256,256]{1,2,0:T(8,128)}, f32[1,256,256]{1,2,0:T(8,128)}) async-done(((f32[1,256,256]{1,2,0:T(8,128)}, f32[1,256,256]{1,2,0:T(8,128)}, f32[1,256,256]{1,2,0:T(8,128)}, f32[1,256,256]{1,2,0:T(8,128)}), (f32[1,256,256]{1,2,0:T(8,128)}, f32[1,256,256]{1,2,0:T(8,128)}, f32[1,256,256]{1,2,0:T(8,128)}, ...) | async-done | bytes 1048592 | tf_op jit(solution)/shard_map/psum | solution.py:11
  772.4 7.7 subtract_select_fusion
  780.1 5.2 copy.34
  785.3 3.4 copy.52
  790.0 3.5 select_select_fusion
  (85 shorter events, 19.2 us)
Async XLA Ops:
  6.5 109.5 %all-reduce.10.cloned.1.call-start = ((), (), s32[]{:S(2)}) async-start(), calls=%async_computation | async-start | bytes 524288 | tf_op jit(solution)/shard_map/psum | solution.py:11
  19.1 272.0 %all-reduce.12.cloned.1.call-start = ((), (), s32[]{:S(2)}) async-start(), calls=%async_computation.1 | async-start | bytes 2097152 | tf_op jit(solution)/shard_map/psum | solution.py:11
  19.2 160.2 %slice-start = ((f32[4,256,4,256]{3,2,1,0:T(4,128)}), f32[4,256,1,256]{3,2,1,0:T(1,128)S(1)}, s32[]{:S(2)}) async-start(f32[4,256,4,256]{3,2,1,0:T(4,128)} %reshape.215), calls=%async_computation.6 | async-start | bytes 2097152 | tf_op jit(solution)/shard_map/slice | solution.py:22
  181.5 210.3 %all-reduce.20.cloned.1.call-start = ((), (), s32[]{:S(2)}) async-start(), calls=%async_computation.5 | async-start | bytes 2097152 | tf_op jit(solution)/shard_map/psum | solution.py:11
  293.3 202.3 %all-reduce.14.cloned.1.call-start = ((), (), s32[]{:S(2)}) async-start(), calls=%async_computation.2 | async-start | bytes 524288 | tf_op jit(solution)/shard_map/psum | solution.py:11
  398.8 1.9 copy-start
  401.4 270.5 %all-reduce.16.cloned.1.call-start = ((), (), s32[]{:S(2)}) async-start(), calls=%async_computation.3 | async-start | bytes 2097152 | tf_op jit(solution)/shard_map/psum | solution.py:11
  536.4 138.0 %copy-start.3 = (f32[4,256,256]{1,2,0:T(8,128)S(1)}, f32[4,256,256]{1,2,0:T(8,128)}, u32[]{:S(2)}) copy-start(f32[4,256,256]{1,2,0:T(8,128)} %all-reduce.12.cloned.1.call-done) | copy-start | bytes 3145732
  560.6 211.8 %all-reduce.18.cloned.1.call-start = ((), (), s32[]{:S(2)}) async-start(), calls=%async_computation.4 | async-start | bytes 2097152 | tf_op jit(solution)/shard_map/psum | solution.py:11
  675.5 3.0 copy-start.4
  785.3 3.4 copy-start.1
  785.3 4.7 copy-start.2
Sparse Core Ops, SparseCore 0:
  19.2 96.7 all-reduce.9
  181.6 109.4 all-reduce.11
  294.6 97.1 all-reduce.19
  401.6 93.9 all-reduce.13
  560.7 111.1 all-reduce.15
  675.2 97.1 all-reduce.17
where the time goes:
time: 810 us; the launch traced here: 801 us
  waiting for transfers between devices  600 us (74%)
  other arithmetic  121 us (15%)
  local copies, waits for them, and re-layouts  39.3 us (5%)
  matrix products  23.1 us (3%)
  between operations  16.7 us (2%)
    psum x6, waiting for transfers between devices, from_root(): return lax.psum(jnp.where(mine, shard, jnp.zeros_like(shard)), axis)  600 us
    another operation x13, other arithmetic, panel_step(): lower = jnp.linalg.cholesky(tile)  68.6 us
    another operation x5, other arithmetic, panel_step(): jax.scipy.linalg.solve_triangular(lower, jnp.eye(NB, dtype=jnp.float32),...  39.4 us
  transfers between devices with their start and end apart: 6, of which 6 were waited for; matrix products, arithmetic and copies ran while one was open for 1% of the time, Pallas kernels for 0%

commit v1 on v0

v1 whole, which is shorter than its diff:
```python
import jax
import jax.numpy as jnp
from jax import lax
from jax.experimental import pallas as pl
from jax.experimental.pallas import tpu as pltpu
from jax.sharding import PartitionSpec as P

NB = 256
HB = 128
HIGH = lax.Precision.HIGHEST


def dot_nt(a, b):
    return lax.dot_general(a, b, (((1,), (1,)), ((), ())), precision=HIGH, preferred_element_type=jnp.float32)


def dot_nn(a, b):
    return lax.dot_general(a, b, (((1,), (0,)), ((), ())), precision=HIGH, preferred_element_type=jnp.float32)


def dot_tn(a, b):
    return lax.dot_general(a, b, (((0,), (0,)), ((), ())), precision=HIGH, preferred_element_type=jnp.float32)


def factor_half(m_ref):
    sub = lax.broadcasted_iota(jnp.int32, (8, HB), 0)
    for b in range(HB // 8):
        lo = 8 * b
        s = m_ref[lo:lo + 8, :HB]
        v = m_ref[lo:lo + 8, HB:]
        cols = [jnp.broadcast_to(s[:, lo + j:lo + j + 1], (8, HB)) for j in range(8)]
        diag = jnp.ones((8, HB), jnp.float32)
        for j in range(8):
            d = jnp.broadcast_to(cols[j][j:j + 1, :], (8, HB))
            diag = jnp.where(sub == j, d, diag)
            if j < 7:
                f = jnp.where(sub > j, cols[j] / d, 0.0)
                for i in range(j + 1, 8):
                    cols[i] = cols[i] - f * jnp.broadcast_to(cols[i][j:j + 1, :], (8, HB))
                s = s - f * jnp.broadcast_to(s[j:j + 1, :], (8, HB))
                v = v - f * jnp.broadcast_to(v[j:j + 1, :], (8, HB))
        root = 1.0 / jnp.sqrt(diag)
        lane = lax.broadcasted_iota(jnp.int32, (8, HB), 1)
        s = jnp.where(lane >= lo + sub, s * root, 0.0)
        v = v * root
        uw = jnp.concatenate([s, v], axis=1)
        m_ref[lo:lo + 8, :] = uw
        if lo + 8 < HB:
            full = dot_tn(s, uw)
            m_ref[lo + 8:, :] = m_ref[lo + 8:, :] - full[lo + 8:, :]


def factor_kernel(a_ref, l0_ref, w0_ref, l10_ref, l1_ref, w1_ref, s_ref, m_ref):
    a00 = a_ref[0]
    a10 = a_ref[1]
    a11 = a_ref[2]
    n = 2 * NB
    s_ref[:NB, :NB] = (a00 + a00.T) * 0.5
    s_ref[:NB, NB:] = a10.T
    s_ref[NB:, NB:] = (a11 + a11.T) * 0.5
    eye = (lax.broadcasted_iota(jnp.int32, (HB, HB), 0) == lax.broadcasted_iota(jnp.int32, (HB, HB), 1)).astype(jnp.float32)
    zero = jnp.zeros((HB, HB), jnp.float32)
    outs = ((l0_ref, w0_ref), (l1_ref, w1_ref))
    for k in range(4):
        lo = k * HB
        m_ref[:, :HB] = s_ref[lo:lo + HB, lo:lo + HB]
        m_ref[:, HB:] = eye
        factor_half(m_ref)
        u = m_ref[:, :HB]
        w = m_ref[:, HB:]
        l_ref, w_ref = outs[k // 2]
        h = (k % 2) * HB
        l_ref[h:h + HB, h:h + HB] = u.T
        w_ref[h:h + HB, h:h + HB] = w
        if k < 3:
            row = dot_nn(w, s_ref[lo:lo + HB, lo + HB:])
            s_ref[lo:lo + HB, lo + HB:] = row
            s_ref[lo + HB:, lo + HB:] = s_ref[lo + HB:, lo + HB:] - dot_tn(row, row)
        if k % 2 == 1:
            cross = s_ref[lo - HB:lo, lo:lo + HB].T
            l_ref[HB:, :HB] = cross
            l_ref[:HB, HB:] = zero
            w_ref[:HB, HB:] = zero
            w_ref[HB:, :HB] = -dot_nn(w, dot_nn(cross, w_ref[:HB, :HB]))
    l10_ref[...] = s_ref[:NB, NB:n].T


def factor(lead):
    block = jax.ShapeDtypeStruct((NB, NB), jnp.float32)
    return pl.pallas_call(
        factor_kernel,
        out_shape=[block] * 5,
        in_specs=[pl.BlockSpec(memory_space=pltpu.VMEM)],
        out_specs=[pl.BlockSpec(memory_space=pltpu.VMEM)] * 5,
        scratch_shapes=[pltpu.VMEM((2 * NB, 2 * NB), jnp.float32), pltpu.VMEM((HB, 2 * HB), jnp.float32)],
        compiler_params=pltpu.CompilerParams(vmem_limit_bytes=32 * 2**20),
        cost_estimate=pl.CostEstimate(flops=200_000_000, bytes_accessed=4_000_000, transcendentals=0),
        name="factor_lead",
    )(lead)


def update_kernel(pos_ref, a_ref, gr_ref, gc_ref, l0_ref, w0_ref, l10_ref, l1_ref, w1_ref, o_ref, pc_ref, pr_ref):
    step = pl.program_id(0)
    r = pos_ref[0]
    c = pos_ref[1]
    w0 = w0_ref[...]
    w1 = w1_ref[...]
    l10 = l10_ref[...]

    def solve(g0, g1):
        p0 = dot_nt(g0, w0)
        p1 = dot_nt(g1 - dot_nt(p0, l10), w1)
        return p0, p1

    @pl.when(step == 0)
    def _():
        for m in range(4):
            g0 = gc_ref[:, 0, m].reshape(NB, NB)
            g1 = gc_ref[:, 1, m].reshape(NB, NB)
            p0, p1 = solve(g0, g1)
            pc_ref[m, :, :NB] = p0
            pc_ref[m, :, NB:] = p1

    p0, p1 = solve(gr_ref[:, 0].reshape(NB, NB), gr_ref[:, 1].reshape(NB, NB))
    pr_ref[:, :NB] = p0
    pr_ref[:, NB:] = p1
    row = r + 16 * step

    @pl.when(row == 0)
    def _():
        pr_ref[:, :NB] = l0_ref[...]
        pr_ref[:, NB:] = jnp.zeros((NB, NB), jnp.float32)

    @pl.when(row == 1)
    def _():
        pr_ref[:, NB:] = l1_ref[...]

    for m in range(4):
        col = c + 16 * m

        @pl.when(row < col)
        def _():
            o_ref[:, m * NB:(m + 1) * NB] = jnp.zeros((NB, NB), jnp.float32)

        @pl.when(row >= col)
        def _():
            o_ref[:, m * NB:(m + 1) * NB] = a_ref[:, m * NB:(m + 1) * NB] - dot_nt(pr_ref[...], pc_ref[m])

    @pl.when(c == 0)
    def _():
        o_ref[:, :NB] = pr_ref[:, :NB]

    @pl.when(c == 1)
    def _():
        o_ref[:, :NB] = pr_ref[:, NB:]


def update(pos, a, gr, gc, l0, w0, l10, l1, w1):
    whole = pl.BlockSpec(memory_space=pltpu.VMEM)
    return pl.pallas_call(
        update_kernel,
        grid=(4,),
        out_shape=jax.ShapeDtypeStruct((4 * NB, 4 * NB), jnp.float32),
        in_specs=[
            pl.BlockSpec(memory_space=pltpu.SMEM),
            pl.BlockSpec((NB, 4 * NB), lambda i: (i, 0)),
            pl.BlockSpec((2, 2, HB, NB), lambda i: (i, 0, 0, 0)),
            whole, whole, whole, whole, whole, whole,
        ],
        out_specs=pl.BlockSpec((NB, 4 * NB), lambda i: (i, 0)),
        scratch_shapes=[pltpu.VMEM((4, NB, 2 * NB), jnp.float32), pltpu.VMEM((NB, 2 * NB), jnp.float32)],
        compiler_params=pltpu.CompilerParams(vmem_limit_bytes=48 * 2**20),
        cost_estimate=pl.CostEstimate(flops=8_000_000_000, bytes_accessed=13_000_000, transcendentals=0),
        name="solve_update",
    )(pos, a, gr, gc, l0, w0, l10, l1, w1)


def per_device(a):
    r = lax.axis_index("row").astype(jnp.int32)
    c = lax.axis_index("col").astype(jnp.int32)
    z, core = c // 2, c % 2
    x = a[:, :NB]
    pieces = x.reshape(4, 16, 16, NB).transpose(1, 0, 2, 3)
    spread = lax.all_to_all(pieces, "row", 0, 0, tiled=True)
    lead = spread[0:2, 0].reshape(32, NB)

    def payload(k):
        return jnp.concatenate([spread[2 * k:2 * k + 2].reshape(HB, NB), x[k * HB:(k + 1) * HB], lead], axis=0)

    got = jnp.where(z == 0, payload(0), 0.0)
    for k in range(1, 8):
        got = got + lax.ppermute(payload(k), "col", [(h, 2 * k + h) for h in range(2)])
    col_piece = got[:HB].reshape(2, 64, NB)
    row_piece = got[HB:2 * HB]
    lead = got[2 * HB:].reshape(2, 16, NB)

    swap = [(i, i ^ 1) for i in range(16)]
    mine = lax.dynamic_index_in_dim(col_piece, core, 0, keepdims=False)
    other = lax.ppermute(lax.dynamic_index_in_dim(col_piece, 1 - core, 0, keepdims=False), "col", swap)
    col_piece = jnp.where(core == 0, jnp.stack([mine, other]), jnp.stack([other, mine]))
    gc = lax.all_gather(col_piece.reshape(2, 4, 16, NB), "row")
    gr = lax.all_gather(row_piece, "col").reshape(8, 2, HB, NB)

    lead = lax.all_to_all(jnp.broadcast_to(lead[None], (16, 2, 16, NB)), "row", 0, 0, tiled=True)
    lead = lead.transpose(1, 0, 2, 3).reshape(2, NB, NB)
    theirs = lax.ppermute(lead, "col", swap)
    lane0 = jnp.where(core == 0, lead, theirs)
    lane1 = jnp.where(core == 0, theirs, lead)
    factors = factor(jnp.concatenate([lane0, lane1[1:]], axis=0))
    return update(jnp.stack([r, c]), a, gr, gc, *factors)


def solution(mesh):
    return jax.shard_map(
        per_device,
        mesh=mesh,
        in_specs=(P("row", "col"),),
        out_specs=P("row", "col"),
        check_vma=False,
    )
```

time: 810 us -> 188 us (0.23); the launches traced: 801 us -> 188 us
  waiting for transfers between devices: 600 us -> 66.2 us
  other arithmetic: 121 us -> 2.35 us
  Pallas kernels: 0 us -> 56.4 us
  local copies, waits for them, and re-layouts: 39.3 us -> 7.79 us
  starting transfers between devices: 0.38 us -> 25.6 us
  matrix products: 23.1 us -> 0 us
  blocking collectives: 0 us -> 15.9 us
    psum x6 -> x0, waiting for transfers between devices: 600 us -> none  [from_root(): return lax.psum(jnp.where(mine, shard, jnp.zeros_like(shard)), axis)]
    another operation x18 -> x1, other arithmetic: 108 us -> 0.08 us  [per_device(): return update(jnp.stack([r, c]), a, gr, gc, *factors)]
    pallas_call x0 -> x2, Pallas kernels: none -> 56.4 us  [the longest x1 37.5 us: factor(): pl.pallas_call(factor_kernel, out_shape=[block] * 5, in_specs=[pl.BlockSp...]
    all_gather x0 -> x2, waiting for transfers between devices: none -> 34.7 us  [the longest x1 34.7 us: per_device(): gc = lax.all_gather(col_piece.reshape(2, 4, 16, NB), 'row')]
    dot_general x4 -> x0, matrix products: 20.2 us -> none  [the longest x2 14.7 us: update_range(): jnp.einsum('lia,mja->limj', panel, across, precision=lax.Precision.HIGHEST)]
    ppermute x0 -> x9, waiting for transfers between devices: none -> 18.3 us  [the longest x7 15.3 us: per_device(): lax.ppermute(payload(k), 'col', [(h, 2 * k + h) for h in range(2)])]
    ppermute x0 -> x9, starting transfers between devices: none -> 18.1 us  [the longest x7 17.7 us: per_device(): lax.ppermute(payload(k), 'col', [(h, 2 * k + h) for h in range(2)])]
    all_to_all x0 -> x1, blocking collectives: none -> 15.9 us  [per_device(): lax.all_to_all(jnp.broadcast_to(lead[None], (16, 2, 16, NB)), 'row', 0, 0...]
  transfers between devices with their start and end apart: 6 -> 12, of which waited for: 6 -> 8; matrix products, arithmetic and copies ran while one was open for 1% -> 1% of each run, Pallas kernels for 0% -> 20%
where the time goes in v1:
time: 188 us
  waiting for transfers between devices  66.2 us (35%)
  Pallas kernels  56.4 us (30%)
  starting transfers between devices  25.6 us (14%)
  blocking collectives  15.9 us (8%)
  between operations  13.6 us (7%)
  local copies, waits for them, and re-layouts  7.79 us (4%)
  other arithmetic  2.35 us (1%)
    pallas_call x1, Pallas kernels, factor(): pl.pallas_call(factor_kernel, out_shape=[block] * 5, in_specs=[pl.BlockSp...  37.5 us
    all_gather x1, waiting for transfers between devices, per_device(): gc = lax.all_gather(col_piece.reshape(2, 4, 16, NB), 'row')  34.7 us
    pallas_call x1, Pallas kernels, update(): pl.pallas_call(update_kernel, grid=(4,), out_shape=jax.ShapeDtypeStruct((...  18.9 us
    ppermute x7, starting transfers between devices, per_device(): lax.ppermute(payload(k), 'col', [(h, 2 * k + h) for h in range(2)])  17.7 us
    all_to_all x1, blocking collectives, per_device(): lax.all_to_all(jnp.broadcast_to(lead[None], (16, 2, 16, NB)), 'row', 0, 0...  15.9 us
    ppermute x7, waiting for transfers between devices, per_device(): lax.ppermute(payload(k), 'col', [(h, 2 * k + h) for h in range(2)])  15.3 us
    all_to_all x1, waiting for transfers between devices, per_device(): spread = lax.all_to_all(pieces, 'row', 0, 0, tiled=True)  13.1 us
    all_to_all x1, starting transfers between devices, per_device(): spread = lax.all_to_all(pieces, 'row', 0, 0, tiled=True)  7.39 us
  transfers between devices with their start and end apart: 12, of which 8 were waited for; matrix products, arithmetic and copies ran while one was open for 1% of the time, Pallas kernels for 20%

profile of v1, /device:TPU:8, one launch (start us, length us, event | category | flops | bytes accessed | tf_op | source)
XLA Modules:
  0.0 187.8 jit_solution(12111640484554746549)
XLA Ops:
  6.5 1.3 slice.74
  7.8 1.1 copy.11
  8.9 7.4 %all-to-all-start = ((f32[16,4,16,256]{3,2,1,0:T(8,128)}), f32[16,4,16,256]{3,2,1,0:T(8,128)S(1)}, u32[]{:S(2)}, u32[]{:S(2)}) async-start(f32[16,4,16,256]{3,2,1,0:T(8,128)} %copy.11), calls=%async_computation | async-start | bytes 2097152 | tf_op jit(solution)/shard_map/all_to_all | solution.py:184
  16.3 1.4 fusion.8
  17.7 13.1 %all-to-all-done = f32[16,4,16,256]{3,2,1,0:T(8,128)S(1)} async-done(((f32[16,4,16,256]{3,2,1,0:T(8,128)}), f32[16,4,16,256]{3,2,1,0:T(8,128)S(1)}, u32[]{:S(2)}, u32[]{:S(2)}) %all-to-all-start) | async-done | bytes 1048608 | tf_op jit(solution)/shard_map/all_to_all | solution.py:184
  30.9 0.1 fusion.9
  31.0 7.8 %collective-permute-start.6 = (f32[288,256]{1,0:T(8,128)S(1)}, f32[288,256]{1,0:T(8,128)S(1)}, u32[]{:S(2)}, u32[]{:S(2)}) collective-permute-start(f32[288,256]{1,0:T(8,128)S(1)} %pad_maximum_fusion), channel_id=1, source_target_pairs={{0,14},{1,15},{16,30},{17,31},{32,46},{33,47},{48,62},{49,63},{64,... | collective-permute-start | bytes 884744 | tf_op jit(solution)/shard_map/ppermute | solution.py:192
  38.8 0.1 pad_maximum_fusion.6
  38.9 1.3 collective-permute-start
  40.2 1.3 collective-permute-start.1
  41.5 1.3 collective-permute-start.2
  42.8 2.0 %collective-permute-start.3 = (f32[288,256]{1,0:T(8,128)S(1)}, f32[288,256]{1,0:T(8,128)}, u32[]{:S(2)}, u32[]{:S(2)}) collective-permute-start(f32[288,256]{1,0:T(8,128)S(1)} %get-tuple-element.38), channel_id=1, source_target_pairs={{0,8},{1,9},{16,24},{17,25},{32,40},{33,41},{48,56},{49,57},{64,72... | collective-permute-start | bytes 884744 | tf_op jit(solution)/shard_map/ppermute | solution.py:192
  44.9 2.0 %collective-permute-start.4 = (f32[288,256]{1,0:T(8,128)S(1)}, f32[288,256]{1,0:T(8,128)}, u32[]{:S(2)}, u32[]{:S(2)}) collective-permute-start(f32[288,256]{1,0:T(8,128)S(1)} %get-tuple-element.39), channel_id=1, source_target_pairs={{0,10},{1,11},{16,26},{17,27},{32,42},{33,43},{48,58},{49,59},{64,... | collective-permute-start | bytes 884744 | tf_op jit(solution)/shard_map/ppermute | solution.py:192
  46.9 0.8 collective-permute-done
  47.6 2.0 %collective-permute-start.5 = (f32[288,256]{1,0:T(8,128)S(1)}, f32[288,256]{1,0:T(8,128)}, u32[]{:S(2)}, u32[]{:S(2)}) collective-permute-start(f32[288,256]{1,0:T(8,128)S(1)} %get-tuple-element.40), channel_id=1, source_target_pairs={{0,12},{1,13},{16,28},{17,29},{32,44},{33,45},{48,60},{49,61},{64,... | collective-permute-start | bytes 884744 | tf_op jit(solution)/shard_map/ppermute | solution.py:192
  49.6 4.3 %collective-permute-done.1 = f32[288,256]{1,0:T(8,128)S(1)} collective-permute-done((f32[288,256]{1,0:T(8,128)S(1)}, f32[288,256]{1,0:T(8,128)S(1)}, u32[]{:S(2)}, u32[]{:S(2)}) %collective-permute-start.1) | collective-permute-done | bytes 294944 | tf_op jit(solution)/shard_map/ppermute | solution.py:192
  54.0 6.3 %collective-permute-done.2 = f32[288,256]{1,0:T(8,128)S(1)} collective-permute-done((f32[288,256]{1,0:T(8,128)S(1)}, f32[288,256]{1,0:T(8,128)S(1)}, u32[]{:S(2)}, u32[]{:S(2)}) %collective-permute-start.2) | collective-permute-done | bytes 294944 | tf_op jit(solution)/shard_map/ppermute | solution.py:192
  60.3 3.9 %collective-permute-done.3 = f32[288,256]{1,0:T(8,128)} collective-permute-done((f32[288,256]{1,0:T(8,128)S(1)}, f32[288,256]{1,0:T(8,128)}, u32[]{:S(2)}, u32[]{:S(2)}) %collective-permute-start.3) | collective-permute-done | bytes 294944 | tf_op jit(solution)/shard_map/ppermute | solution.py:192
  64.2 1.3 fusion.7
  65.5 0.7 fusion.10
  66.2 0.1 collective-permute-start.7
  66.4 1.2 collective-permute-done.7
  67.6 0.7 maximum_select_fusion
  68.4 15.9 %all_to_all.10 = f32[16,2,16,256]{3,2,1,0:T(8,128)S(1)} all-to-all(f32[16,2,16,256]{3,2,1,0:T(8,128)S(1)} %broadcast_in_dim.13), channel_id=1, replica_groups=mesh['row'=16,'col'=16] {'row'}, dimensions={0} | all-to-all | bytes 1048576 | tf_op jit(solution)/shard_map/all_to_all | solution.py:204
  84.3 0.3 collective-permute-start.8
  84.6 0.1 pad_add_fusion.pos_ref
  84.7 1.8 collective-permute-done.8
  86.7 37.5 %factor_lead.1 = (f32[256,256]{1,0:T(8,128)S(1)}, f32[256,256]{1,0:T(8,128)S(1)}, f32[256,256]{1,0:T(8,128)S(1)}, f32[256,256]{1,0:T(8,128)S(1)}, f32[256,256]{1,0:T(8,128)S(1)}) custom-call(f32[3,256,256]{2,1,0:T(8,128)S(1)} %pad_maximum_fusion.8.a_ref), custom_call_target="tpu_custom_call" | custom-call | flops 200000000 | bytes 4000000 | tf_op jit(solution)/shard_map/factor_lead/pallas_call | solution.py:90
  124.2 34.7 %all-gather.4.cloned.1.call-done.gc_ref = f32[16,2,4,16,256]{4,3,2,1,0:T(8,128)} async-done(((f32[1,2,4,16,256]{4,3,2,1,0:T(8,128)}), f32[16,2,4,16,256]{4,3,2,1,0:T(8,128)}) %all-gather.4.cloned.1.call-update) | async-done | bytes 2097168 | tf_op jit(solution)/shard_map/all_gather | solution.py:201
  158.9 1.6 copy-done
  160.5 1.6 copy-done.1
  162.1 18.9 %solve_update.1 = f32[1024,1024]{1,0:T(8,128)} custom-call(s32[2]{0:T(128)S(1)} %pad_add_fusion.pos_ref, f32[1024,1024]{1,0:T(8,128)} %a_ref.1, f32[8,2,128,256]{3,2,1,0:T(8,128)S(1)} %bitcast.24, f32[16,2,4,16,256]{4,3,2,1,0:T(8,128)S(1)} %copy-done.1, f32[256,256]{1,0:T(8,128)S(1)} %get-tuple-element.10.l0_ref, f32[256,256]{1,0:T(8,128)S(1)} %get-tuple-element.11.w0_ref, ...), custom_call_target="tpu_custom_call" | custom-call | flops 8000000000 | bytes 13000000 | tf_op jit(solution)/shard_map/solve_update/pallas_call | solution.py:160
  (19 shorter events, 0.4 us)
Async XLA Ops:
  8.9 22.0 %all-to-all-start = ((f32[16,4,16,256]{3,2,1,0:T(8,128)}), f32[16,4,16,256]{3,2,1,0:T(8,128)S(1)}, u32[]{:S(2)}, u32[]{:S(2)}) async-start(f32[16,4,16,256]{3,2,1,0:T(8,128)} %copy.11), calls=%async_computation | async-start | bytes 2097152 | tf_op jit(solution)/shard_map/all_to_all | solution.py:184
  16.3 107.9 %all-gather.6.cloned.1.call-start = ((), (), s32[]{:S(2)}) async-start(), calls=%async_computation.3 | async-start | bytes 2228224 | tf_op jit(solution)/shard_map/all_gather | solution.py:202
  31.0 13.9 %collective-permute-start.6 = (f32[288,256]{1,0:T(8,128)S(1)}, f32[288,256]{1,0:T(8,128)S(1)}, u32[]{:S(2)}, u32[]{:S(2)}) collective-permute-start(f32[288,256]{1,0:T(8,128)S(1)} %pad_maximum_fusion), channel_id=1, source_target_pairs={{0,14},{1,15},{16,30},{17,31},{32,46},{33,47},{48,62},{49,63},{64,... | collective-permute-start | bytes 884744 | tf_op jit(solution)/shard_map/ppermute | solution.py:192
  38.9 8.7 %collective-permute-start = (f32[288,256]{1,0:T(8,128)S(1)}, f32[288,256]{1,0:T(8,128)S(1)}, u32[]{:S(2)}, u32[]{:S(2)}) collective-permute-start(f32[288,256]{1,0:T(8,128)S(1)} %get-tuple-element.35), channel_id=1, source_target_pairs={{0,2},{1,3},{16,18},{17,19},{32,34},{33,35},{48,50},{49,51},{64,66... | collective-permute-start | bytes 884744 | tf_op jit(solution)/shard_map/ppermute | solution.py:192
  40.2 13.8 %collective-permute-start.1 = (f32[288,256]{1,0:T(8,128)S(1)}, f32[288,256]{1,0:T(8,128)S(1)}, u32[]{:S(2)}, u32[]{:S(2)}) collective-permute-start(f32[288,256]{1,0:T(8,128)S(1)} %get-tuple-element.36), channel_id=1, source_target_pairs={{0,4},{1,5},{16,20},{17,21},{32,36},{33,37},{48,52},{49,53},{64,68... | collective-permute-start | bytes 884744 | tf_op jit(solution)/shard_map/ppermute | solution.py:192
  41.5 18.8 %collective-permute-start.2 = (f32[288,256]{1,0:T(8,128)S(1)}, f32[288,256]{1,0:T(8,128)S(1)}, u32[]{:S(2)}, u32[]{:S(2)}) collective-permute-start(f32[288,256]{1,0:T(8,128)S(1)} %get-tuple-element.37), channel_id=1, source_target_pairs={{0,6},{1,7},{16,22},{17,23},{32,38},{33,39},{48,54},{49,55},{64,70... | collective-permute-start | bytes 884744 | tf_op jit(solution)/shard_map/ppermute | solution.py:192
  42.8 21.3 %collective-permute-start.3 = (f32[288,256]{1,0:T(8,128)S(1)}, f32[288,256]{1,0:T(8,128)}, u32[]{:S(2)}, u32[]{:S(2)}) collective-permute-start(f32[288,256]{1,0:T(8,128)S(1)} %get-tuple-element.38), channel_id=1, source_target_pairs={{0,8},{1,9},{16,24},{17,25},{32,40},{33,41},{48,56},{49,57},{64,72... | collective-permute-start | bytes 884744 | tf_op jit(solution)/shard_map/ppermute | solution.py:192
  44.9 19.3 %collective-permute-start.4 = (f32[288,256]{1,0:T(8,128)S(1)}, f32[288,256]{1,0:T(8,128)}, u32[]{:S(2)}, u32[]{:S(2)}) collective-permute-start(f32[288,256]{1,0:T(8,128)S(1)} %get-tuple-element.39), channel_id=1, source_target_pairs={{0,10},{1,11},{16,26},{17,27},{32,42},{33,43},{48,58},{49,59},{64,... | collective-permute-start | bytes 884744 | tf_op jit(solution)/shard_map/ppermute | solution.py:192
  47.6 16.5 %collective-permute-start.5 = (f32[288,256]{1,0:T(8,128)S(1)}, f32[288,256]{1,0:T(8,128)}, u32[]{:S(2)}, u32[]{:S(2)}) collective-permute-start(f32[288,256]{1,0:T(8,128)S(1)} %get-tuple-element.40), channel_id=1, source_target_pairs={{0,12},{1,13},{16,28},{17,29},{32,44},{33,45},{48,60},{49,61},{64,... | collective-permute-start | bytes 884744 | tf_op jit(solution)/shard_map/ppermute | solution.py:192
  66.2 92.7 %all-gather.4.cloned.1.call-start = ((), (), s32[]{:S(2)}) async-start(), calls=%async_computation.2 | async-start | bytes 2228224 | tf_op jit(solution)/shard_map/all_gather | solution.py:201
  66.2 1.3 collective-permute-start.7
  84.3 2.2 %collective-permute-start.8 = (f32[2,256,256]{2,1,0:T(8,128)S(1)}, f32[2,256,256]{2,1,0:T(8,128)S(1)}, u32[]{:S(2)}, u32[]{:S(2)}) collective-permute-start(f32[2,256,256]{2,1,0:T(8,128)S(1)} %bitcast.26), channel_id=1, source_target_pairs={{0,1},{1,0},{2,3},{3,2},{4,5},{5,4},{6,7},{7,6},{8,9},{9,8},{10,11... | collective-permute-start | bytes 1572872 | tf_op jit(solution)/shard_map/ppermute | solution.py:206
  158.9 1.6 copy-start
  160.5 1.6 copy-start.1
Sparse Core Ops, SparseCore 0:
  66.3 41.5 all-gather.5
  110.3 48.5 all-gather.3

commit v2 on v0

v2 whole, which is shorter than its diff:
```python
import jax
import jax.numpy as jnp
from jax import lax
from jax.experimental import pallas as pl
from jax.experimental.pallas import tpu as pltpu
from jax.sharding import PartitionSpec as P

NB = 256
HB = 128
STEP = 16
HIGH = lax.Precision.HIGHEST
F32 = jnp.float32
BF16 = jnp.bfloat16
VMEM = pl.BlockSpec(memory_space=pltpu.VMEM)
SMEM = pl.BlockSpec(memory_space=pltpu.SMEM)


def dot_nt(a, b):
    return lax.dot_general(a, b, (((1,), (1,)), ((), ())), precision=HIGH, preferred_element_type=F32)


def dot_nn(a, b):
    return lax.dot_general(a, b, (((1,), (0,)), ((), ())), precision=HIGH, preferred_element_type=F32)


def dot_tn(a, b):
    return lax.dot_general(a, b, (((0,), (0,)), ((), ())), precision=HIGH, preferred_element_type=F32)


def dot_nt_16(a, b):
    return lax.dot_general(a, b, (((1,), (1,)), ((), ())), preferred_element_type=F32)


def split3(x):
    hi = x.astype(BF16).astype(F32)
    rest = x - hi
    mid = rest.astype(BF16).astype(F32)
    return hi, mid, rest - mid


def dot_tn_short(a, b):
    ah, am, al = split3(a)
    bh, bm, bl = split3(b)
    left = jnp.concatenate([ah, ah, am, ah, al, am], axis=0).astype(BF16)
    right = jnp.concatenate([bh, bm, bh, bl, bh, bm], axis=0).astype(BF16)
    return lax.dot_general(left, right, (((0,), (0,)), ((), ())), preferred_element_type=F32)


def reciprocal(x):
    r = pl.reciprocal(x, approx=True)
    return r * (2.0 - x * r)


def inverse_root(x):
    r = lax.rsqrt(x)
    return r * (1.5 - 0.5 * x * r * r)


def factor_half(m_ref):
    sub = lax.broadcasted_iota(jnp.int32, (STEP, HB), 0)
    lane = lax.broadcasted_iota(jnp.int32, (STEP, HB), 1)
    odd = (sub & 1) == 1

    def spread(x, i):
        return jnp.broadcast_to(x[i:i + 1, :], (STEP, HB))

    for lo in range(0, HB, STEP):
        s = m_ref[lo:lo + STEP, :HB]
        v = m_ref[lo:lo + STEP, HB:]
        cols = [jnp.broadcast_to(s[:, lo + j:lo + j + 1], (STEP, HB)) for j in range(STEP)]
        first = jnp.ones((STEP, HB), F32)
        dets = first
        cross = first
        for j in range(0, STEP, 2):
            a, b, c = spread(cols[j], j), spread(cols[j], j + 1), spread(cols[j + 1], j + 1)
            det = a * c - b * b
            pair = (sub == j) | (sub == j + 1)
            first = jnp.where(pair, a, first)
            dets = jnp.where(pair, det, dets)
            cross = jnp.where(pair, b, cross)
            if j < STEP - 2:
                r = reciprocal(det)
                below = sub > j + 1
                f0 = jnp.where(below, (cols[j] * c - cols[j + 1] * b) * r, 0.0)
                f1 = jnp.where(below, (cols[j + 1] * a - cols[j] * b) * r, 0.0)
                for i in range(j + 2, STEP):
                    cols[i] = cols[i] - (f0 * spread(cols[i], j) + f1 * spread(cols[i], j + 1))
                s = s - (f0 * spread(s, j) + f1 * spread(s, j + 1))
                v = v - (f0 * spread(v, j) + f1 * spread(v, j + 1))
        ra = inverse_root(first)
        scale = jnp.where(odd, first * ra * inverse_root(dets), ra)
        mult = jnp.where(odd, cross * ra * ra, 0.0)
        s = jnp.where(lane >= lo + sub, (s - mult * pltpu.roll(s, 1, 0)) * scale, 0.0)
        v = (v - mult * pltpu.roll(v, 1, 0)) * scale
        uw = jnp.concatenate([s, v], axis=1)
        m_ref[lo:lo + STEP, :] = uw
        if lo + STEP < HB:
            full = dot_tn_short(s, uw)
            m_ref[lo + STEP:, :] = m_ref[lo + STEP:, :] - full[lo + STEP:, :]


def factor_kernel(pos_ref, mine_ref, theirs_ref, l_ref, w_ref, a_ref, s_ref, m_ref):
    lane0 = pos_ref[1] % 2 == 0
    for k in range(16):
        at = slice(16 * k, 16 * k + 16)
        mine = mine_ref[k]
        theirs = theirs_ref[k]
        a_ref[0, at, :] = jnp.where(lane0, mine[0], theirs[0])
        a_ref[1, at, :] = jnp.where(lane0, mine[1], theirs[1])
        a_ref[2, at, :] = jnp.where(lane0, theirs[1], mine[1])
    a00 = a_ref[0]
    a11 = a_ref[2]
    s_ref[:NB, :NB] = (a00 + a00.T) * 0.5
    s_ref[:NB, NB:] = a_ref[1].T
    s_ref[NB:, NB:] = (a11 + a11.T) * 0.5
    eye = (lax.broadcasted_iota(jnp.int32, (HB, HB), 0) == lax.broadcasted_iota(jnp.int32, (HB, HB), 1)).astype(F32)
    l_ref[...] = jnp.zeros((2 * NB, 2 * NB), F32)
    w_ref[...] = jnp.zeros((2 * NB, 2 * NB), F32)
    for k in range(4):
        lo = k * HB
        hi = lo + HB
        m_ref[:, :HB] = s_ref[lo:hi, lo:hi]
        m_ref[:, HB:] = eye
        factor_half(m_ref)
        w = m_ref[:, HB:]
        l_ref[lo:hi, lo:hi] = m_ref[:, :HB].T
        w_ref[lo:hi, lo:hi] = w
        if k < 3:
            row = dot_nn(w, s_ref[lo:hi, hi:])
            s_ref[lo:hi, hi:] = row
            s_ref[hi:, hi:] = s_ref[hi:, hi:] - dot_tn(row, row)
            l_ref[hi:, lo:hi] = row.T
        if k % 2 == 1:
            w_ref[lo:hi, lo - HB:lo] = -dot_nn(w, dot_nn(l_ref[lo:hi, lo - HB:lo], w_ref[lo - HB:lo, lo - HB:lo]))
    w_ref[NB:, :NB] = -dot_nn(w_ref[NB:, NB:], dot_nn(l_ref[NB:, :NB], w_ref[:NB, :NB]))


def factor(pos, mine, theirs):
    both = jax.ShapeDtypeStruct((2 * NB, 2 * NB), F32)
    return pl.pallas_call(
        factor_kernel,
        out_shape=[both] * 2,
        in_specs=[SMEM, VMEM, VMEM],
        out_specs=[VMEM] * 2,
        scratch_shapes=[
            pltpu.VMEM((3, NB, NB), F32),
            pltpu.VMEM((2 * NB, 2 * NB), F32),
            pltpu.VMEM((HB, 2 * HB), F32),
        ],
        compiler_params=pltpu.CompilerParams(vmem_limit_bytes=16 * 2**20),
        cost_estimate=pl.CostEstimate(flops=15_000_000_000, bytes_accessed=4_000_000, transcendentals=0),
        name="factor_lead",
    )(pos, mine, theirs)


def meanwhile(pos):
    def kernel(x_ref, o_ref):
        o_ref[0] = x_ref[0]
        o_ref[1] = x_ref[1]

    return pl.pallas_call(
        kernel,
        out_shape=jax.ShapeDtypeStruct(pos.shape, pos.dtype),
        in_specs=[SMEM],
        out_specs=SMEM,
        cost_estimate=pl.CostEstimate(flops=40_000_000_000, bytes_accessed=100_000_000, transcendentals=0),
        name="meanwhile",
    )(pos)


def rows_kernel(pos_ref, mine_ref, other_ref, l_ref, w_ref, p_hbm, q_hbm, p_ref, q_ref, p_sem, q_sem):
    r = pos_ref[0]
    c = pos_ref[1]
    n = 2 * NB
    lane0 = c % 2 == 0
    copies = []
    for k in range(4):
        at = slice(k * NB, (k + 1) * NB)
        mine = mine_ref[at, :]
        other = other_ref[at, :]
        g0 = jnp.where(lane0, mine, other)
        g1 = jnp.where(lane0, other, mine)
        p0 = dot_nt(g0, w_ref[:NB, :NB])
        p1 = dot_nt(jnp.concatenate([g0, g1], axis=1), w_ref[NB:, :])
        q0 = dot_nn(jnp.concatenate([p0, p1], axis=1), w_ref[:, :NB])
        q1 = dot_nn(p1, w_ref[NB:, NB:])
        for h, part in enumerate(split3(jnp.concatenate([q0, q1], axis=1))):
            q_ref[at, h * n:(h + 1) * n] = part.astype(BF16)
        copies.append(pltpu.make_async_copy(q_ref.at[at], q_hbm.at[at], q_sem.at[k]))
        copies[-1].start()
        p = jnp.where(c == 0, p0, p1)
        if k == 0:
            zero = jnp.zeros((NB, NB), F32)
            p = jnp.where(r == 0, jnp.where(c == 0, l_ref[:NB, :NB], zero), p)
            p = jnp.where(r == 1, jnp.where(c == 0, l_ref[NB:, :NB], l_ref[NB:, NB:]), p)
        p_ref[at, :] = p
    copies.append(pltpu.make_async_copy(p_ref, p_hbm, p_sem))
    copies[-1].start()
    for copy in copies:
        copy.wait()


def solve_rows(pos, mine, other, factors):
    hbm = pl.BlockSpec(memory_space=pltpu.HBM)
    p = jax.ShapeDtypeStruct((4 * NB, NB), F32)
    q = jax.ShapeDtypeStruct((4 * NB, 6 * NB), BF16)
    return pl.pallas_call(
        rows_kernel,
        out_shape=[p, q],
        in_specs=[SMEM] + [VMEM] * 4,
        out_specs=[hbm] * 2,
        scratch_shapes=[
            pltpu.VMEM(p.shape, F32),
            pltpu.VMEM(q.shape, BF16),
            pltpu.SemaphoreType.DMA(()),
            pltpu.SemaphoreType.DMA((4,)),
        ],
        compiler_params=pltpu.CompilerParams(vmem_limit_bytes=20 * 2**20),
        cost_estimate=pl.CostEstimate(flops=9_000_000_000, bytes_accessed=5_000_000, transcendentals=0),
        name="solve_rows",
    )(pos, mine, other, *factors)


def update_kernel(pos_ref, a_hbm, p_hbm, q_hbm, gc_ref, o_hbm, a_ref, p_ref, q_ref, g_ref, o_ref, sems):
    r = pos_ref[0]
    c = pos_ref[1]
    n = 2 * NB
    order = (3, 2, 1, 0)
    rows = [slice(k * NB, (k + 1) * NB) for k in range(4)]
    loads = {}
    for k in order:
        loads[k] = [
            pltpu.make_async_copy(q_hbm.at[rows[k]], q_ref.at[rows[k]], sems.at[0, k]),
            pltpu.make_async_copy(a_hbm.at[rows[k]], a_ref.at[rows[k]], sems.at[1, k]),
            pltpu.make_async_copy(p_hbm.at[rows[k]], p_ref.at[rows[k]], sems.at[2, k]),
        ]
        for copy in loads[k]:
            copy.start()

    core = c % 2
    for h, lane in enumerate((core, 1 - core)):
        for m in range(4):
            hi, mid, lo = split3(gc_ref[:, lane, m].reshape(NB, NB))
            for k, part in enumerate((lo, mid, hi)):
                g_ref[rows[m], k * n + h * NB:k * n + (h + 1) * NB] = part.astype(BF16)

    stores = []
    for k in order:
        for copy in loads[k]:
            copy.wait()
        row = r + 16 * k
        for m in range(4):
            col = c + 16 * m

            @pl.when(row < col)
            def _():
                o_ref[rows[k], rows[m]] = jnp.zeros((NB, NB), F32)

            @pl.when(row >= col)
            def _():
                small = dot_nt_16(q_ref[rows[k], :], g_ref[rows[m], :])
                small += dot_nt_16(q_ref[rows[k], :2 * n], g_ref[rows[m], n:])
                o_ref[rows[k], rows[m]] = a_ref[rows[k], rows[m]] - (
                    small + dot_nt_16(q_ref[rows[k], :n], g_ref[rows[m], 2 * n:])
                )

        @pl.when(c < 2)
        def _():
            o_ref[rows[k], :NB] = p_ref[rows[k], :]

        stores.append(pltpu.make_async_copy(o_ref.at[rows[k]], o_hbm.at[rows[k]], sems.at[3, k]))
        stores[-1].start()
    for copy in stores:
        copy.wait()


def update(pos, a, p, q, gc):
    hbm = pl.BlockSpec(memory_space=pltpu.HBM)
    return pl.pallas_call(
        update_kernel,
        out_shape=jax.ShapeDtypeStruct(a.shape, F32),
        in_specs=[SMEM, hbm, hbm, hbm, VMEM],
        out_specs=hbm,
        scratch_shapes=[
            pltpu.VMEM(a.shape, F32),
            pltpu.VMEM(p.shape, F32),
            pltpu.VMEM(q.shape, BF16),
            pltpu.VMEM(q.shape, BF16),
            pltpu.VMEM(a.shape, F32),
            pltpu.SemaphoreType.DMA((4, 4)),
        ],
        compiler_params=pltpu.CompilerParams(vmem_limit_bytes=32 * 2**20),
        cost_estimate=pl.CostEstimate(flops=8_000_000_000, bytes_accessed=13_000_000, transcendentals=0),
        name="update",
    )(pos, a, p, q, gc)


TREE = (
    tuple(((0, d or 4),) for d in range(8)),
    (
        ((0, 6), (4, 2)), ((0, 6), (1, 3)), ((0, 6), (2, 4)), ((0, 6), (3, 5)),
        ((0, 2), (4, 6)), ((0, 2), (5, 3)), ((0, 2), (6, 4)), ((0, 2), (7, 5)),
    ),
    (
        ((0, 7), (6, 5), (4, 3), (2, 1)), ((0, 7), (1, 2), (3, 4), (6, 5)),
        ((0, 1), (2, 3), (4, 5), (6, 7)), ((0, 1), (3, 2), (5, 4), (6, 7)),
        ((0, 1), (2, 3), (4, 5), (6, 7)), ((0, 7), (2, 1), (3, 4), (5, 6)),
        ((0, 1), (2, 3), (4, 5), (6, 7)), ((0, 1), (2, 3), (5, 4), (7, 6)),
    ),
)


LEAD = (((0, 5),), ((0, 7), (5, 3)), ((7, 6), (5, 4), (3, 2)), ((2, 1),))


def along_z(x, moves):
    pairs = [(16 * r + 2 * a + h, 16 * r + 2 * b + h) for r in range(16) for a, b in moves(r // 2) for h in range(2)]
    return lax.ppermute(x, ("row", "col"), pairs)


def per_device(a):
    r = lax.axis_index("row").astype(jnp.int32)
    c = lax.axis_index("col").astype(jnp.int32)
    pos = jnp.stack([r, c])
    swap = [(i, i ^ 1) for i in range(16)]
    x = a[:, :NB]
    here = c < 2

    lead = lax.all_to_all(x[:NB].reshape(16, 16, NB), "row", 0, 0, tiled=True)[0:2].reshape(32, NB)
    lead = jnp.where(here, lead, 0.0)
    for moves in LEAD:
        lead += along_z(lead, lambda d: moves if d < 5 else [((8 - s) % 8, (8 - t) % 8) for s, t in moves])
    panel = jnp.where(here, x, 0.0)
    panel += along_z(panel, lambda d: TREE[0][d])
    lead, panel, pos = lax.optimization_barrier((lead, panel, pos))

    pieces = panel.reshape(4, 16, 16, NB).transpose(1, 0, 2, 3).reshape(16, 64, NB)
    pieces = jnp.concatenate([pieces, jnp.broadcast_to(lead[None], (16, 32, NB))], axis=1)
    held = lax.all_to_all(pieces, "row", 0, 0, tiled=True)
    arrived = along_z(panel, lambda d: TREE[1][d])
    held, arrived, pos = lax.optimization_barrier((held, arrived, meanwhile(pos)))
    panel += arrived

    lead = held[:, 64:].reshape(16, 2, 16, NB)
    theirs = lax.ppermute(lead, "col", swap)
    mine = lax.dynamic_index_in_dim(held, c, 0, keepdims=False)[:64]
    other = lax.ppermute(lax.dynamic_index_in_dim(held, c ^ 1, 0, keepdims=False)[:64], "col", swap)
    mine, other, lead, theirs, panel = lax.optimization_barrier((mine, other, lead, theirs, panel))
    gc = jnp.stack([mine, other]).reshape(2, 4, 16, NB)
    gc = lax.all_to_all(jnp.broadcast_to(gc[None], (16, 2, 4, 16, NB)), "row", 0, 0, tiled=True)
    arrived = along_z(panel, lambda d: TREE[2][d])
    *factors, arrived = lax.optimization_barrier((*factor(pos, lead, theirs), arrived))
    panel += arrived
    p, q = solve_rows(pos, panel, lax.ppermute(panel, "col", swap), factors)
    return update(pos, a, p, q, gc)


def solution(mesh):
    return jax.shard_map(
        per_device,
        mesh=mesh,
        in_specs=(P("row", "col"),),
        out_specs=P("row", "col"),
        check_vma=False,
    )
```

time: 810 us -> 132 us (0.16)
  waiting for transfers between devices: 600 us -> 21.7 us
  other arithmetic: 121 us -> 7.32 us
  starting transfers between devices: 0.38 us -> 38.2 us
  Pallas kernels: 0 us -> 35.4 us
  local copies, waits for them, and re-layouts: 39.3 us -> 10.4 us
  matrix products: 23.1 us -> 0 us
  blocking collectives: 0 us -> 17.5 us
  between operations: 16.7 us -> 0.38 us
    psum x6 -> x0, waiting for transfers between devices: 600 us -> none  [from_root(): return lax.psum(jnp.where(mine, shard, jnp.zeros_like(shard)), axis)]
    another operation x18 -> x1, other arithmetic: 108 us -> 0.59 us  [per_device(): pos = jnp.stack([r, c])]
    pallas_call x0 -> x4, Pallas kernels: none -> 35.4 us  [the longest x1 17.7 us: factor(): pl.pallas_call(factor_kernel, out_shape=[both] * 2, in_specs=[SMEM, VMEM,...]
    ppermute x0 -> x10, starting transfers between devices: none -> 24.6 us  [the longest x7 23.6 us: along_z(): return lax.ppermute(x, ('row', 'col'), pairs)]
    dot_general x4 -> x0, matrix products: 20.2 us -> none  [the longest x2 14.7 us: update_range(): jnp.einsum('lia,mja->limj', panel, across, precision=lax.Precision.HIGHEST)]
    all_to_all x0 -> x1, blocking collectives: none -> 17.5 us  [per_device(): lax.all_to_all(x[:NB].reshape(16, 16, NB), 'row', 0, 0, tiled=True)[0:2]]
    all_to_all x0 -> x2, starting transfers between devices: none -> 13.6 us  [the longest x1 8.62 us: per_device(): held = lax.all_to_all(pieces, 'row', 0, 0, tiled=True)]
    ppermute x0 -> x10, waiting for transfers between devices: none -> 12.6 us  [the longest x7 9.98 us: along_z(): return lax.ppermute(x, ('row', 'col'), pairs)]
  transfers between devices with their start and end apart: 6 -> 12, of which waited for: 6 -> 5; matrix products, arithmetic and copies ran while one was open for 1% -> 6% of each run, Pallas kernels for 0% -> 20%
where the time goes in v2:
time: 132 us; the launch traced here: 131 us
  starting transfers between devices  38.2 us (29%)
  Pallas kernels  35.4 us (27%)
  waiting for transfers between devices  21.7 us (16%)
  blocking collectives  17.5 us (13%)
  local copies, waits for them, and re-layouts  10.4 us (8%)
  other arithmetic  7.32 us (6%)
    ppermute x7, starting transfers between devices, along_z(): return lax.ppermute(x, ('row', 'col'), pairs)  23.6 us
    pallas_call x1, Pallas kernels, factor(): pl.pallas_call(factor_kernel, out_shape=[both] * 2, in_specs=[SMEM, VMEM,...  17.7 us
    all_to_all x1, blocking collectives, per_device(): lax.all_to_all(x[:NB].reshape(16, 16, NB), 'row', 0, 0, tiled=True)[0:2]  17.5 us
    ppermute x7, waiting for transfers between devices, along_z(): return lax.ppermute(x, ('row', 'col'), pairs)  9.98 us
    all_to_all x1, waiting for transfers between devices, per_device(): held = lax.all_to_all(pieces, 'row', 0, 0, tiled=True)  9.08 us
    pallas_call x1, Pallas kernels, update(): pl.pallas_call(update_kernel, out_shape=jax.ShapeDtypeStruct(a.shape, F32...  9.03 us
    all_to_all x1, starting transfers between devices, per_device(): held = lax.all_to_all(pieces, 'row', 0, 0, tiled=True)  8.62 us
    pallas_call x1, Pallas kernels, solve_rows(): pl.pallas_call(rows_kernel, out_shape=[p, q], in_specs=[SMEM] + [VMEM] *...  7.5 us
  transfers between devices with their start and end apart: 12, of which 5 were waited for; matrix products, arithmetic and copies ran while one was open for 6% of the time, Pallas kernels for 20%

profile of v2, /device:TPU:8, one launch (start us, length us, event | category | flops | bytes accessed | tf_op | source)
XLA Modules:
  0.0 130.9 jit_solution(11906378472010940419)
XLA Ops:
  0.0 1.3 slice_select_fusion
  1.3 5.2 %collective-permute-start.4 = (f32[1024,256]{1,0:T(8,128)S(1)}, f32[1024,256]{1,0:T(8,128)S(1)}, u32[]{:S(2)}, u32[]{:S(2)}) collective-permute-start(f32[1024,256]{1,0:T(8,128)S(1)} %slice_select_fusion), channel_id=1, source_target_pairs={{0,8},{1,9},{16,24},{17,25},{32,34},{33,35},{48,50},{49,51},{64,68... | collective-permute-start | bytes 3145736 | tf_op jit(solution)/shard_map/ppermute | solution.py:318
  6.5 1.0 slice.25
  7.5 17.5 %all_to_all.15 = f32[16,16,256]{2,1,0:T(8,128)S(1)} all-to-all(f32[16,16,256]{2,1,0:T(8,128)S(1)} %bitcast.22), channel_id=1, replica_groups=mesh['row'=16,'col'=16] {'row'}, dimensions={0} | all-to-all | bytes 524288 | tf_op jit(solution)/shard_map/all_to_all | solution.py:329
  25.0 1.4 %collective-permute-start = (f32[32,256]{1,0:T(8,128)S(1)}, f32[32,256]{1,0:T(8,128)S(1)}, u32[]{:S(2)}, u32[]{:S(2)}) collective-permute-start(f32[32,256]{1,0:T(8,128)S(1)} %bitcast.24), channel_id=1, source_target_pairs={{0,10},{1,11},{16,26},{17,27},{32,42},{33,43},{48,58},{49,59},{64,... | collective-permute-start | bytes 98312 | tf_op jit(solution)/shard_map/ppermute | solution.py:318
  26.4 1.6 %collective-permute-done = f32[32,256]{1,0:T(8,128)S(1)} collective-permute-done((f32[32,256]{1,0:T(8,128)S(1)}, f32[32,256]{1,0:T(8,128)S(1)}, u32[]{:S(2)}, u32[]{:S(2)}) %collective-permute-start) | collective-permute-done | bytes 32800 | tf_op jit(solution)/shard_map/ppermute | solution.py:318
  28.0 1.3 collective-permute-start.1
  29.3 1.6 %collective-permute-done.1 = f32[32,256]{1,0:T(8,128)S(1)} collective-permute-done((f32[32,256]{1,0:T(8,128)S(1)}, f32[32,256]{1,0:T(8,128)S(1)}, u32[]{:S(2)}, u32[]{:S(2)}) %collective-permute-start.1) | collective-permute-done | bytes 32800 | tf_op jit(solution)/shard_map/ppermute | solution.py:318
  30.8 0.7 collective-permute-start.2
  31.5 0.7 collective-permute-start.3
  32.2 0.6 pad_add_fusion.x_ref
  32.8 1.4 %fusion = f32[1024,256]{1,0:T(8,128)S(1)} fusion(f32[1024,256]{1,0:T(8,128)S(1)} %collective-permute-done.4, f32[1024,1024]{1,0:T(8,128)} %a_hbm.1, pred[]{:T(512)S(6)} %lt.10), kind=kLoop, calls=%fused_computation.8 | loop fusion | flops 524288 | bytes 3145729 | tf_op jit(solution)/shard_map/add | solution.py:334
  34.2 9.4 %collective-permute-start.5 = (f32[1024,256]{1,0:T(8,128)S(1)}, f32[1024,256]{1,0:T(8,128)S(1)}, u32[]{:S(2)}, u32[]{:S(2)}) collective-permute-start(f32[1024,256]{1,0:T(8,128)S(1)} %fusion), channel_id=1, source_target_pairs={{0,12},{1,13},{8,4},{9,5},{16,28},{17,29},{24,20},{25,21},{32,44},... | collective-permute-start | bytes 3145736 | tf_op jit(solution)/shard_map/ppermute | solution.py:318
  43.7 1.2 pad_maximum_fusion
  45.0 8.6 %all-to-all-start.1 = ((f32[16,96,256]{2,1,0:T(8,128)}), f32[16,96,256]{2,1,0:T(8,128)}, u32[]{:S(2)}, u32[]{:S(2)}) async-start(f32[16,96,256]{2,1,0:T(8,128)} %pad_maximum_fusion), calls=%async_computation.1 | async-start | bytes 3145728 | tf_op jit(solution)/shard_map/all_to_all | solution.py:339
  53.6 1.2 meanwhile.1.pos_ref
  54.8 6.8 %collective-permute-done.5 = f32[1024,256]{1,0:T(8,128)S(1)} collective-permute-done((f32[1024,256]{1,0:T(8,128)S(1)}, f32[1024,256]{1,0:T(8,128)S(1)}, u32[]{:S(2)}, u32[]{:S(2)}) %collective-permute-start.5) | collective-permute-done | bytes 1048608 | tf_op jit(solution)/shard_map/ppermute | solution.py:318
  61.6 9.1 %all-to-all-done.1 = f32[16,96,256]{2,1,0:T(8,128)} async-done(((f32[16,96,256]{2,1,0:T(8,128)}), f32[16,96,256]{2,1,0:T(8,128)}, u32[]{:S(2)}, u32[]{:S(2)}) %all-to-all-start.1) | async-done | bytes 1572896 | tf_op jit(solution)/shard_map/all_to_all | solution.py:339
  70.7 1.1 slice.32
  71.9 0.9 dynamic-slice_bitcast_fusion
  73.4 1.1 add.35
  74.5 5.0 %collective-permute-start.8 = (f32[1024,256]{1,0:T(8,128)}, f32[1024,256]{1,0:T(8,128)}, u32[]{:S(2)}, u32[]{:S(2)}) collective-permute-start(f32[1024,256]{1,0:T(8,128)} %add.35), channel_id=1, source_target_pairs={{0,14},{1,15},{12,10},{13,11},{8,6},{9,7},{4,2},{5,3},{16,30},{17,... | collective-permute-start | bytes 3145736 | tf_op jit(solution)/shard_map/ppermute | solution.py:318
  79.4 1.6 %broadcast_in_dim.25 = f32[16,2,4,16,256]{4,3,2,1,0:T(8,128)} broadcast(f32[2,4,16,256]{3,2,1,0:T(8,128)S(1)} %maximum_bitcast_fusion), dimensions={1,2,3,4} | broadcast | bytes 2228224 | tf_op jit(solution)/shard_map/broadcast_in_dim | solution.py:350
  81.0 5.0 %all-to-all-start.2 = ((f32[16,2,4,16,256]{4,3,2,1,0:T(8,128)}), f32[16,2,4,16,256]{4,3,2,1,0:T(8,128)S(1)}, u32[]{:S(2)}, u32[]{:S(2)}) async-start(f32[16,2,4,16,256]{4,3,2,1,0:T(8,128)} %broadcast_in_dim.25), calls=%async_computation.2 | async-start | bytes 4194304 | tf_op jit(solution)/shard_map/all_to_all | solution.py:350
  86.0 17.7 %factor_lead.1 = (f32[512,512]{1,0:T(8,128)S(1)}, f32[512,512]{1,0:T(8,128)S(1)}) custom-call(s32[2]{0:T(128)S(1)} %copy-done.3, f32[16,2,16,256]{3,2,1,0:T(8,128)S(1)} %bitcast.19, f32[16,2,16,256]{3,2,1,0:T(8,128)S(1)} %collective-permute-done.7.theirs_ref), custom_call_target="tpu_custom_call" | custom-call | flops 15000000512 | bytes 4000000 | tf_op jit(solution)/shard_map/factor_lead/pallas_call | solution.py:140
  103.7 1.7 %add.36.mine_ref = f32[1024,256]{1,0:T(8,128)S(1)} add(f32[1024,256]{1,0:T(8,128)} %add.35, f32[1024,256]{1,0:T(8,128)} %collective-permute-done.8) | non-fusion elementwise | flops 262144 | bytes 3145728 | tf_op jit(solution)/shard_map/add | solution.py:353
  105.7 2.6 %collective-permute-done.9.other_ref = f32[1024,256]{1,0:T(8,128)S(1)} collective-permute-done((f32[1024,256]{1,0:T(8,128)S(1)}, f32[1024,256]{1,0:T(8,128)S(1)}, u32[]{:S(2)}, u32[]{:S(2)}) %collective-permute-start.9) | collective-permute-done | bytes 1048608 | tf_op jit(solution)/shard_map/ppermute | solution.py:354
  108.4 7.5 %solve_rows.1 = (f32[1024,256]{1,0:T(8,128)S(1)}, bf16[1024,1536]{1,0:T(8,128)(2,1)S(1)}) custom-call(s32[2]{0:T(128)S(1)} %copy-done.3, f32[1024,256]{1,0:T(8,128)S(1)} %add.36.mine_ref, f32[1024,256]{1,0:T(8,128)S(1)} %collective-permute-done.9.other_ref, f32[512,512]{1,0:T(8,128)S(1)} %get-tuple-element.35.l_ref, f32[512,512]{1,0:T(8,128)S(1)} %get-tuple-element.36.w_ref), custom_call_target="tpu_custom_call" | custom-call | flops 8999999488 | bytes 5000000 | tf_op jit(solution)/shard_map/solve_rows/pallas_call | solution.py:207
  115.9 1.7 %copy-done.1 = bf16[1024,1536]{1,0:T(8,128)(2,1)} copy-done((bf16[1024,1536]{1,0:T(8,128)(2,1)}, bf16[1024,1536]{1,0:T(8,128)(2,1)S(1)}, u32[]{:S(2)}) %copy-start.1) | copy-done | bytes 3145752
  117.6 2.2 %copy-done = f32[1024,1024]{1,0:T(8,128)S(1)} copy-done((f32[1024,1024]{1,0:T(8,128)S(1)}, f32[1024,1024]{1,0:T(8,128)}, u32[]{:S(2)}) %copy-start) | copy-done | bytes 4194328
  119.8 1.9 %copy-done.2 = bf16[1024,1536]{1,0:T(8,128)(2,1)S(1)} copy-done((bf16[1024,1536]{1,0:T(8,128)(2,1)S(1)}, bf16[1024,1536]{1,0:T(8,128)(2,1)}, u32[]{:S(2)}) %copy-start.2) | copy-done | bytes 3145752
  121.6 9.0 %update.1 = f32[1024,1024]{1,0:T(8,128)} custom-call(s32[2]{0:T(128)S(1)} %copy-done.3, f32[1024,1024]{1,0:T(8,128)S(1)} %copy-done, f32[1024,256]{1,0:T(8,128)S(1)} %get-tuple-element.37.p_hbm, bf16[1024,1536]{1,0:T(8,128)(2,1)S(1)} %copy-done.2, f32[16,2,4,16,256]{4,3,2,1,0:T(8,128)S(1)} %all-to-all-done.2.gc_ref), custom_call_target="tpu_custom_call" | custom-call | flops 8000000000 | bytes 13000000 | tf_op jit(solution)/shard_map/update/pallas_call | solution.py:279
  (23 shorter events, 1.2 us)
Async XLA Ops:
  1.3 31.5 %collective-permute-start.4 = (f32[1024,256]{1,0:T(8,128)S(1)}, f32[1024,256]{1,0:T(8,128)S(1)}, u32[]{:S(2)}, u32[]{:S(2)}) collective-permute-start(f32[1024,256]{1,0:T(8,128)S(1)} %slice_select_fusion), channel_id=1, source_target_pairs={{0,8},{1,9},{16,24},{17,25},{32,34},{33,35},{48,50},{49,51},{64,68... | collective-permute-start | bytes 3145736 | tf_op jit(solution)/shard_map/ppermute | solution.py:318
  25.0 3.0 %collective-permute-start = (f32[32,256]{1,0:T(8,128)S(1)}, f32[32,256]{1,0:T(8,128)S(1)}, u32[]{:S(2)}, u32[]{:S(2)}) collective-permute-start(f32[32,256]{1,0:T(8,128)S(1)} %bitcast.24), channel_id=1, source_target_pairs={{0,10},{1,11},{16,26},{17,27},{32,42},{33,43},{48,58},{49,59},{64,... | collective-permute-start | bytes 98312 | tf_op jit(solution)/shard_map/ppermute | solution.py:318
  28.0 2.9 %collective-permute-start.1 = (f32[32,256]{1,0:T(8,128)S(1)}, f32[32,256]{1,0:T(8,128)S(1)}, u32[]{:S(2)}, u32[]{:S(2)}) collective-permute-start(f32[32,256]{1,0:T(8,128)S(1)} %bitcast_add_fusion), channel_id=1, source_target_pairs={{0,14},{1,15},{10,6},{11,7},{16,30},{17,31},{26,22},{27,23},{32,46... | collective-permute-start | bytes 98312 | tf_op jit(solution)/shard_map/ppermute | solution.py:318
  30.8 0.7 collective-permute-start.2
  31.5 1.3 collective-permute-start.3
  34.2 27.4 %collective-permute-start.5 = (f32[1024,256]{1,0:T(8,128)S(1)}, f32[1024,256]{1,0:T(8,128)S(1)}, u32[]{:S(2)}, u32[]{:S(2)}) collective-permute-start(f32[1024,256]{1,0:T(8,128)S(1)} %fusion), channel_id=1, source_target_pairs={{0,12},{1,13},{8,4},{9,5},{16,28},{17,29},{24,20},{25,21},{32,44},... | collective-permute-start | bytes 3145736 | tf_op jit(solution)/shard_map/ppermute | solution.py:318
  45.0 25.7 %all-to-all-start.1 = ((f32[16,96,256]{2,1,0:T(8,128)}), f32[16,96,256]{2,1,0:T(8,128)}, u32[]{:S(2)}, u32[]{:S(2)}) async-start(f32[16,96,256]{2,1,0:T(8,128)} %pad_maximum_fusion), calls=%async_computation.1 | async-start | bytes 3145728 | tf_op jit(solution)/shard_map/all_to_all | solution.py:339
  71.8 2.7 %collective-permute-start.7 = (f32[16,2,16,256]{3,2,1,0:T(8,128)S(1)}, f32[16,2,16,256]{3,2,1,0:T(8,128)S(1)}, u32[]{:S(2)}, u32[]{:S(2)}) collective-permute-start(f32[16,2,16,256]{3,2,1,0:T(8,128)S(1)} %bitcast.18), channel_id=1, source_target_pairs={{0,1},{1,0},{2,3},{3,2},{4,5},{5,4},{6,7},{7,6},{8,9},{9,8},{10,11... | collective-permute-start | bytes 1572872 | tf_op jit(solution)/shard_map/ppermute | solution.py:345
  72.8 1.7 %collective-permute-start.6 = (f32[64,256]{1,0:T(8,128)S(1)}, f32[64,256]{1,0:T(8,128)S(1)}, u32[]{:S(2)}, u32[]{:S(2)}) collective-permute-start(f32[64,256]{1,0:T(8,128)S(1)} %get-tuple-element.41), channel_id=1, source_target_pairs={{0,1},{1,0},{2,3},{3,2},{4,5},{5,4},{6,7},{7,6},{8,9},{9,8},{10,11... | collective-permute-start | bytes 196616 | tf_op jit(solution)/shard_map/ppermute | solution.py:347
  74.5 29.3 %collective-permute-start.8 = (f32[1024,256]{1,0:T(8,128)}, f32[1024,256]{1,0:T(8,128)}, u32[]{:S(2)}, u32[]{:S(2)}) collective-permute-start(f32[1024,256]{1,0:T(8,128)} %add.35), channel_id=1, source_target_pairs={{0,14},{1,15},{12,10},{13,11},{8,6},{9,7},{4,2},{5,3},{16,30},{17,... | collective-permute-start | bytes 3145736 | tf_op jit(solution)/shard_map/ppermute | solution.py:318
  81.0 5.0 %copy-start.3 = (s32[2]{0:T(128)S(1)}, s32[2]{0:T(128)}, u32[]{:S(2)}) copy-start(s32[2]{0:T(128)} %meanwhile.1.pos_ref) | copy-start | bytes 28
  81.0 36.5 %all-to-all-start.2 = ((f32[16,2,4,16,256]{4,3,2,1,0:T(8,128)}), f32[16,2,4,16,256]{4,3,2,1,0:T(8,128)S(1)}, u32[]{:S(2)}, u32[]{:S(2)}) async-start(f32[16,2,4,16,256]{4,3,2,1,0:T(8,128)} %broadcast_in_dim.25), calls=%async_computation.2 | async-start | bytes 4194304 | tf_op jit(solution)/shard_map/all_to_all | solution.py:350
  105.4 3.0 %collective-permute-start.9 = (f32[1024,256]{1,0:T(8,128)S(1)}, f32[1024,256]{1,0:T(8,128)S(1)}, u32[]{:S(2)}, u32[]{:S(2)}) collective-permute-start(f32[1024,256]{1,0:T(8,128)S(1)} %add.36.mine_ref), channel_id=1, source_target_pairs={{0,1},{1,0},{2,3},{3,2},{4,5},{5,4},{6,7},{7,6},{8,9},{9,8},{10,11... | collective-permute-start | bytes 3145736 | tf_op jit(solution)/shard_map/ppermute | solution.py:354
  115.9 1.7 %copy-start.1 = (bf16[1024,1536]{1,0:T(8,128)(2,1)}, bf16[1024,1536]{1,0:T(8,128)(2,1)S(1)}, u32[]{:S(2)}) copy-start(bf16[1024,1536]{1,0:T(8,128)(2,1)S(1)} %get-tuple-element.38.q_hbm) | copy-start | bytes 9437188
  117.6 2.2 %copy-start = (f32[1024,1024]{1,0:T(8,128)S(1)}, f32[1024,1024]{1,0:T(8,128)}, u32[]{:S(2)}) copy-start(f32[1024,1024]{1,0:T(8,128)} %a_hbm.1) | copy-start | bytes 12582916
  119.7 1.9 %copy-start.2 = (bf16[1024,1536]{1,0:T(8,128)(2,1)S(1)}, bf16[1024,1536]{1,0:T(8,128)(2,1)}, u32[]{:S(2)}) copy-start(bf16[1024,1536]{1,0:T(8,128)(2,1)} %copy-done.1) | copy-start | bytes 9437188

commit v3 on v2

--- a/solution.py
+++ b/solution.py
@@ -206,7 +206,7 @@
     q = jax.ShapeDtypeStruct((4 * NB, 6 * NB), BF16)
     return pl.pallas_call(
         rows_kernel,
-        out_shape=[p, q],
+        out_shape=[pltpu.HBM(p.shape, F32), pltpu.HBM(q.shape, BF16)],
         in_specs=[SMEM] + [VMEM] * 4,
         out_specs=[hbm] * 2,
         scratch_shapes=[
@@ -310,7 +310,7 @@
 )
 
 
-LEAD = (((0, 5),), ((0, 7), (5, 3)), ((7, 6), (5, 4), (3, 2)), ((2, 1),))
+LEAD = (((0, 5),), ((0, 6), (5, 2)), ((0, 7), (6, 3), (5, 4), (2, 1)))
 
 
 def along_z(x, moves):
@@ -352,6 +352,7 @@
     *factors, arrived = lax.optimization_barrier((*factor(pos, lead, theirs), arrived))
     panel += arrived
     p, q = solve_rows(pos, panel, lax.ppermute(panel, "col", swap), factors)
+    a, p, q = (pltpu.with_memory_space_constraint(v, pltpu.HBM) for v in (a, p, q))
     return update(pos, a, p, q, gc)
 
 

time: 132 us -> 125 us (0.947)
  local copies, waits for them, and re-layouts: 10.4 us -> 4.63 us
  starting transfers between devices: 38.2 us -> 33.4 us
  waiting for transfers between devices: 21.7 us -> 25.4 us
    unnamed x8 -> x2, local copies, waits for them, and re-layouts: 5.74 us -> 0.01 us
    ppermute x7 -> x6, starting transfers between devices: 23.6 us -> 20.1 us  [along_z(): return lax.ppermute(x, ('row', 'col'), pairs)]
    ppermute x7 -> x6, waiting for transfers between devices: 9.98 us -> 12.8 us  [along_z(): return lax.ppermute(x, ('row', 'col'), pairs)]
    all_to_all x1, starting transfers between devices: 8.62 us -> 7.02 us  [per_device(): held = lax.all_to_all(pieces, 'row', 0, 0, tiled=True)]
    all_to_all x1, waiting for transfers between devices: 0.01 us -> 1.37 us  [per_device(): lax.all_to_all(jnp.broadcast_to(gc[None], (16, 2, 4, 16, NB)), 'row', 0,...]
  transfers between devices with their start and end apart: 12 -> 11, of which waited for: 5 -> 7; matrix products, arithmetic and copies ran while one was open for 6% -> 7% of each run, Pallas kernels for 20% -> 21%
where the time goes in v3:
time: 125 us
  Pallas kernels  35.9 us (29%)
  starting transfers between devices  33.4 us (27%)
  waiting for transfers between devices  25.4 us (20%)
  blocking collectives  17.5 us (14%)
  other arithmetic  7.38 us (6%)
  local copies, waits for them, and re-layouts  4.63 us (4%)
    ppermute x6, starting transfers between devices, along_z(): return lax.ppermute(x, ('row', 'col'), pairs)  20.1 us
    pallas_call x1, Pallas kernels, factor(): pl.pallas_call(factor_kernel, out_shape=[both] * 2, in_specs=[SMEM, VMEM,...  17.7 us
    all_to_all x1, blocking collectives, per_device(): lax.all_to_all(x[:NB].reshape(16, 16, NB), 'row', 0, 0, tiled=True)[0:2]  17.5 us
    ppermute x6, waiting for transfers between devices, along_z(): return lax.ppermute(x, ('row', 'col'), pairs)  12.8 us
    pallas_call x1, Pallas kernels, update(): pl.pallas_call(update_kernel, out_shape=jax.ShapeDtypeStruct(a.shape, F32...  9.43 us
    all_to_all x1, waiting for transfers between devices, per_device(): held = lax.all_to_all(pieces, 'row', 0, 0, tiled=True)  8.64 us
    pallas_call x1, Pallas kernels, solve_rows(): pl.pallas_call(rows_kernel, out_shape=[pltpu.HBM(p.shape, F32), pltpu.HBM...  7.61 us
    all_to_all x1, starting transfers between devices, per_device(): held = lax.all_to_all(pieces, 'row', 0, 0, tiled=True)  7.02 us
  transfers between devices with their start and end apart: 11, of which 7 were waited for; matrix products, arithmetic and copies ran while one was open for 7% of the time, Pallas kernels for 21%

profile of v3, /device:TPU:8, one launch (start us, length us, event | category | flops | bytes accessed | tf_op | source)
XLA Modules:
  0.0 124.6 jit_solution(10490543818689779795)
XLA Ops:
  0.0 1.3 %slice_select_fusion = f32[1024,256]{1,0:T(8,128)S(1)} fusion(f32[1024,1024]{1,0:T(8,128)} %a_hbm.1, pred[]{:T(512)S(6)} %lt.10), kind=kLoop, calls=%fused_computation.1 | loop fusion | flops 262144 | bytes 2097153 | tf_op jit(solution)/shard_map/jit(_where)/select_n | solution.py:333
  1.3 5.2 %collective-permute-start.3 = (f32[1024,256]{1,0:T(8,128)S(1)}, f32[1024,256]{1,0:T(8,128)S(1)}, u32[]{:S(2)}, u32[]{:S(2)}) collective-permute-start(f32[1024,256]{1,0:T(8,128)S(1)} %slice_select_fusion), channel_id=1, source_target_pairs={{0,8},{1,9},{16,24},{17,25},{32,34},{33,35},{48,50},{49,51},{64,68... | collective-permute-start | bytes 3145736 | tf_op jit(solution)/shard_map/ppermute | solution.py:318
  6.5 1.0 slice.25
  7.5 17.5 %all_to_all.15 = f32[16,16,256]{2,1,0:T(8,128)S(1)} all-to-all(f32[16,16,256]{2,1,0:T(8,128)S(1)} %bitcast.22), channel_id=1, replica_groups=mesh['row'=16,'col'=16] {'row'}, dimensions={0} | all-to-all | bytes 524288 | tf_op jit(solution)/shard_map/all_to_all | solution.py:329
  25.0 1.4 %collective-permute-start = (f32[32,256]{1,0:T(8,128)S(1)}, f32[32,256]{1,0:T(8,128)S(1)}, u32[]{:S(2)}, u32[]{:S(2)}) collective-permute-start(f32[32,256]{1,0:T(8,128)S(1)} %bitcast.24), channel_id=1, source_target_pairs={{0,10},{1,11},{16,26},{17,27},{32,42},{33,43},{48,58},{49,59},{64,... | collective-permute-start | bytes 98312 | tf_op jit(solution)/shard_map/ppermute | solution.py:318
  26.4 1.6 %collective-permute-done = f32[32,256]{1,0:T(8,128)S(1)} collective-permute-done((f32[32,256]{1,0:T(8,128)S(1)}, f32[32,256]{1,0:T(8,128)S(1)}, u32[]{:S(2)}, u32[]{:S(2)}) %collective-permute-start) | collective-permute-done | bytes 32800 | tf_op jit(solution)/shard_map/ppermute | solution.py:318
  28.0 1.3 %collective-permute-start.1 = (f32[32,256]{1,0:T(8,128)S(1)}, f32[32,256]{1,0:T(8,128)S(1)}, u32[]{:S(2)}, u32[]{:S(2)}) collective-permute-start(f32[32,256]{1,0:T(8,128)S(1)} %bitcast_add_fusion), channel_id=1, source_target_pairs={{0,12},{1,13},{10,4},{11,5},{16,28},{17,29},{26,20},{27,21},{32,44... | collective-permute-start | bytes 98312 | tf_op jit(solution)/shard_map/ppermute | solution.py:318
  29.3 1.6 %collective-permute-done.1 = f32[32,256]{1,0:T(8,128)S(1)} collective-permute-done((f32[32,256]{1,0:T(8,128)S(1)}, f32[32,256]{1,0:T(8,128)S(1)}, u32[]{:S(2)}, u32[]{:S(2)}) %collective-permute-start.1) | collective-permute-done | bytes 32800 | tf_op jit(solution)/shard_map/ppermute | solution.py:318
  30.8 1.3 %collective-permute-start.2 = (f32[32,256]{1,0:T(8,128)S(1)}, f32[32,256]{1,0:T(8,128)S(1)}, u32[]{:S(2)}, u32[]{:S(2)}) collective-permute-start(f32[32,256]{1,0:T(8,128)S(1)} %add.26), channel_id=1, source_target_pairs={{0,14},{1,15},{12,6},{13,7},{10,8},{11,9},{4,2},{5,3},{16,30},{17,... | collective-permute-start | bytes 98312 | tf_op jit(solution)/shard_map/ppermute | solution.py:318
  32.1 0.7 pad_add_fusion.x_ref
  32.8 0.9 collective-permute-done.2
  33.7 1.4 %fusion = f32[1024,256]{1,0:T(8,128)S(1)} fusion(f32[1024,256]{1,0:T(8,128)S(1)} %collective-permute-done.3, f32[1024,1024]{1,0:T(8,128)} %a_hbm.1, pred[]{:T(512)S(6)} %lt.10), kind=kLoop, calls=%fused_computation.8 | loop fusion | flops 524288 | bytes 3145729 | tf_op jit(solution)/shard_map/add | solution.py:334
  35.1 6.4 %collective-permute-start.4 = (f32[1024,256]{1,0:T(8,128)S(1)}, f32[1024,256]{1,0:T(8,128)S(1)}, u32[]{:S(2)}, u32[]{:S(2)}) collective-permute-start(f32[1024,256]{1,0:T(8,128)S(1)} %fusion), channel_id=1, source_target_pairs={{0,12},{1,13},{8,4},{9,5},{16,28},{17,29},{24,20},{25,21},{32,44},... | collective-permute-start | bytes 3145736 | tf_op jit(solution)/shard_map/ppermute | solution.py:318
  41.6 1.2 %pad_maximum_fusion = f32[16,96,256]{2,1,0:T(8,128)} fusion(f32[16,32,256]{2,1,0:T(8,128)S(1)} %broadcast_in_dim.23, f32[16,64,256]{2,1,0:T(8,128)S(1)} %bitcast.21), kind=kLoop, calls=%fused_computation | loop fusion | flops 393216 | bytes 3145728 | tf_op jit(solution)/shard_map/concatenate | solution.py:338
  42.9 7.0 %all-to-all-start.1 = ((f32[16,96,256]{2,1,0:T(8,128)}), f32[16,96,256]{2,1,0:T(8,128)}, u32[]{:S(2)}, u32[]{:S(2)}) async-start(f32[16,96,256]{2,1,0:T(8,128)} %pad_maximum_fusion), calls=%async_computation.1 | async-start | bytes 3145728 | tf_op jit(solution)/shard_map/all_to_all | solution.py:339
  49.9 1.2 meanwhile.1.pos_ref
  51.1 8.7 %collective-permute-done.4 = f32[1024,256]{1,0:T(8,128)S(1)} collective-permute-done((f32[1024,256]{1,0:T(8,128)S(1)}, f32[1024,256]{1,0:T(8,128)S(1)}, u32[]{:S(2)}, u32[]{:S(2)}) %collective-permute-start.4) | collective-permute-done | bytes 1048608 | tf_op jit(solution)/shard_map/ppermute | solution.py:318
  59.8 8.6 %all-to-all-done.1 = f32[16,96,256]{2,1,0:T(8,128)} async-done(((f32[16,96,256]{2,1,0:T(8,128)}), f32[16,96,256]{2,1,0:T(8,128)}, u32[]{:S(2)}, u32[]{:S(2)}) %all-to-all-start.1) | async-done | bytes 1572896 | tf_op jit(solution)/shard_map/all_to_all | solution.py:339
  68.4 1.1 slice.32
  69.6 0.9 dynamic-slice_bitcast_fusion
  70.5 0.6 collective-permute-start.5
  71.1 1.1 add.31
  72.2 4.5 %collective-permute-start.7 = (f32[1024,256]{1,0:T(8,128)}, f32[1024,256]{1,0:T(8,128)}, u32[]{:S(2)}, u32[]{:S(2)}) collective-permute-start(f32[1024,256]{1,0:T(8,128)} %add.31), channel_id=1, source_target_pairs={{0,14},{1,15},{12,10},{13,11},{8,6},{9,7},{4,2},{5,3},{16,30},{17,... | collective-permute-start | bytes 3145736 | tf_op jit(solution)/shard_map/ppermute | solution.py:318
  76.7 1.6 %broadcast_in_dim.25 = f32[16,2,4,16,256]{4,3,2,1,0:T(8,128)} broadcast(f32[2,4,16,256]{3,2,1,0:T(8,128)S(1)} %maximum_bitcast_fusion), dimensions={1,2,3,4} | broadcast | bytes 2228224 | tf_op jit(solution)/shard_map/broadcast_in_dim | solution.py:350
  78.3 5.3 %all-to-all-start.2 = ((f32[16,2,4,16,256]{4,3,2,1,0:T(8,128)}), f32[16,2,4,16,256]{4,3,2,1,0:T(8,128)S(1)}, u32[]{:S(2)}, u32[]{:S(2)}) async-start(f32[16,2,4,16,256]{4,3,2,1,0:T(8,128)} %broadcast_in_dim.25), calls=%async_computation.2 | async-start | bytes 4194304 | tf_op jit(solution)/shard_map/all_to_all | solution.py:350
  83.6 17.7 %factor_lead.1 = (f32[512,512]{1,0:T(8,128)S(1)}, f32[512,512]{1,0:T(8,128)S(1)}) custom-call(s32[2]{0:T(128)S(1)} %copy-done, f32[16,2,16,256]{3,2,1,0:T(8,128)S(1)} %bitcast.19, f32[16,2,16,256]{3,2,1,0:T(8,128)S(1)} %collective-permute-done.6.theirs_ref), custom_call_target="tpu_custom_call" | custom-call | flops 15000000512 | bytes 4000000 | tf_op jit(solution)/shard_map/factor_lead/pallas_call | solution.py:140
  101.3 1.7 %add.32.mine_ref = f32[1024,256]{1,0:T(8,128)S(1)} add(f32[1024,256]{1,0:T(8,128)} %add.31, f32[1024,256]{1,0:T(8,128)} %collective-permute-done.7) | non-fusion elementwise | flops 262144 | bytes 3145728 | tf_op jit(solution)/shard_map/add | solution.py:353
  103.0 0.3 collective-permute-start.8
  103.3 2.6 %collective-permute-done.8.other_ref = f32[1024,256]{1,0:T(8,128)S(1)} collective-permute-done((f32[1024,256]{1,0:T(8,128)S(1)}, f32[1024,256]{1,0:T(8,128)S(1)}, u32[]{:S(2)}, u32[]{:S(2)}) %collective-permute-start.8) | collective-permute-done | bytes 1048608 | tf_op jit(solution)/shard_map/ppermute | solution.py:354
  106.0 7.6 %solve_rows.1 = (f32[1024,256]{1,0:T(8,128)}, bf16[1024,1536]{1,0:T(8,128)(2,1)}) custom-call(s32[2]{0:T(128)S(1)} %copy-done, f32[1024,256]{1,0:T(8,128)S(1)} %add.32.mine_ref, f32[1024,256]{1,0:T(8,128)S(1)} %collective-permute-done.8.other_ref, f32[512,512]{1,0:T(8,128)S(1)} %get-tuple-element.35.l_ref, f32[512,512]{1,0:T(8,128)S(1)} %get-tuple-element.36.w_ref), custom_call_target="tpu_custom_call" | custom-call | flops 8999999488 | bytes 5000000 | tf_op jit(solution)/shard_map/solve_rows/pallas_call | solution.py:207
  113.6 1.4 %all-to-all-done.2.gc_ref = f32[16,2,4,16,256]{4,3,2,1,0:T(8,128)S(1)} async-done(((f32[16,2,4,16,256]{4,3,2,1,0:T(8,128)}), f32[16,2,4,16,256]{4,3,2,1,0:T(8,128)S(1)}, u32[]{:S(2)}, u32[]{:S(2)}) %all-to-all-start.2) | async-done | bytes 2097184 | tf_op jit(solution)/shard_map/all_to_all | solution.py:350
  115.0 9.4 %update.1 = f32[1024,1024]{1,0:T(8,128)} custom-call(s32[2]{0:T(128)S(1)} %copy-done, f32[1024,1024]{1,0:T(8,128)} %a_hbm.1, f32[1024,256]{1,0:T(8,128)} %get-tuple-element.37.p_hbm, bf16[1024,1536]{1,0:T(8,128)(2,1)} %get-tuple-element.38.q_hbm, f32[16,2,4,16,256]{4,3,2,1,0:T(8,128)S(1)} %all-to-all-done.2.gc_ref), custom_call_target="tpu_custom_call" | custom-call | flops 8000000000 | bytes 13000000 | tf_op jit(solution)/shard_map/update/pallas_call | solution.py:279
  (14 shorter events, 0.3 us)
Async XLA Ops:
  1.3 32.4 %collective-permute-start.3 = (f32[1024,256]{1,0:T(8,128)S(1)}, f32[1024,256]{1,0:T(8,128)S(1)}, u32[]{:S(2)}, u32[]{:S(2)}) collective-permute-start(f32[1024,256]{1,0:T(8,128)S(1)} %slice_select_fusion), channel_id=1, source_target_pairs={{0,8},{1,9},{16,24},{17,25},{32,34},{33,35},{48,50},{49,51},{64,68... | collective-permute-start | bytes 3145736 | tf_op jit(solution)/shard_map/ppermute | solution.py:318
  25.0 3.0 %collective-permute-start = (f32[32,256]{1,0:T(8,128)S(1)}, f32[32,256]{1,0:T(8,128)S(1)}, u32[]{:S(2)}, u32[]{:S(2)}) collective-permute-start(f32[32,256]{1,0:T(8,128)S(1)} %bitcast.24), channel_id=1, source_target_pairs={{0,10},{1,11},{16,26},{17,27},{32,42},{33,43},{48,58},{49,59},{64,... | collective-permute-start | bytes 98312 | tf_op jit(solution)/shard_map/ppermute | solution.py:318
  28.0 2.9 %collective-permute-start.1 = (f32[32,256]{1,0:T(8,128)S(1)}, f32[32,256]{1,0:T(8,128)S(1)}, u32[]{:S(2)}, u32[]{:S(2)}) collective-permute-start(f32[32,256]{1,0:T(8,128)S(1)} %bitcast_add_fusion), channel_id=1, source_target_pairs={{0,12},{1,13},{10,4},{11,5},{16,28},{17,29},{26,20},{27,21},{32,44... | collective-permute-start | bytes 98312 | tf_op jit(solution)/shard_map/ppermute | solution.py:318
  30.8 2.9 %collective-permute-start.2 = (f32[32,256]{1,0:T(8,128)S(1)}, f32[32,256]{1,0:T(8,128)S(1)}, u32[]{:S(2)}, u32[]{:S(2)}) collective-permute-start(f32[32,256]{1,0:T(8,128)S(1)} %add.26), channel_id=1, source_target_pairs={{0,14},{1,15},{12,6},{13,7},{10,8},{11,9},{4,2},{5,3},{16,30},{17,... | collective-permute-start | bytes 98312 | tf_op jit(solution)/shard_map/ppermute | solution.py:318
  35.1 24.7 %collective-permute-start.4 = (f32[1024,256]{1,0:T(8,128)S(1)}, f32[1024,256]{1,0:T(8,128)S(1)}, u32[]{:S(2)}, u32[]{:S(2)}) collective-permute-start(f32[1024,256]{1,0:T(8,128)S(1)} %fusion), channel_id=1, source_target_pairs={{0,12},{1,13},{8,4},{9,5},{16,28},{17,29},{24,20},{25,21},{32,44},... | collective-permute-start | bytes 3145736 | tf_op jit(solution)/shard_map/ppermute | solution.py:318
  42.9 25.6 %all-to-all-start.1 = ((f32[16,96,256]{2,1,0:T(8,128)}), f32[16,96,256]{2,1,0:T(8,128)}, u32[]{:S(2)}, u32[]{:S(2)}) async-start(f32[16,96,256]{2,1,0:T(8,128)} %pad_maximum_fusion), calls=%async_computation.1 | async-start | bytes 3145728 | tf_op jit(solution)/shard_map/all_to_all | solution.py:339
  69.5 2.7 %collective-permute-start.6 = (f32[16,2,16,256]{3,2,1,0:T(8,128)S(1)}, f32[16,2,16,256]{3,2,1,0:T(8,128)S(1)}, u32[]{:S(2)}, u32[]{:S(2)}) collective-permute-start(f32[16,2,16,256]{3,2,1,0:T(8,128)S(1)} %bitcast.18), channel_id=1, source_target_pairs={{0,1},{1,0},{2,3},{3,2},{4,5},{5,4},{6,7},{7,6},{8,9},{9,8},{10,11... | collective-permute-start | bytes 1572872 | tf_op jit(solution)/shard_map/ppermute | solution.py:345
  70.5 1.7 %collective-permute-start.5 = (f32[64,256]{1,0:T(8,128)S(1)}, f32[64,256]{1,0:T(8,128)S(1)}, u32[]{:S(2)}, u32[]{:S(2)}) collective-permute-start(f32[64,256]{1,0:T(8,128)S(1)} %get-tuple-element.41), channel_id=1, source_target_pairs={{0,1},{1,0},{2,3},{3,2},{4,5},{5,4},{6,7},{7,6},{8,9},{9,8},{10,11... | collective-permute-start | bytes 196616 | tf_op jit(solution)/shard_map/ppermute | solution.py:347
  72.2 29.1 %collective-permute-start.7 = (f32[1024,256]{1,0:T(8,128)}, f32[1024,256]{1,0:T(8,128)}, u32[]{:S(2)}, u32[]{:S(2)}) collective-permute-start(f32[1024,256]{1,0:T(8,128)} %add.31), channel_id=1, source_target_pairs={{0,14},{1,15},{12,10},{13,11},{8,6},{9,7},{4,2},{5,3},{16,30},{17,... | collective-permute-start | bytes 3145736 | tf_op jit(solution)/shard_map/ppermute | solution.py:318
  78.3 5.3 %copy-start = (s32[2]{0:T(128)S(1)}, s32[2]{0:T(128)}, u32[]{:S(2)}) copy-start(s32[2]{0:T(128)} %meanwhile.1.pos_ref) | copy-start | bytes 28
  78.3 36.7 %all-to-all-start.2 = ((f32[16,2,4,16,256]{4,3,2,1,0:T(8,128)}), f32[16,2,4,16,256]{4,3,2,1,0:T(8,128)S(1)}, u32[]{:S(2)}, u32[]{:S(2)}) async-start(f32[16,2,4,16,256]{4,3,2,1,0:T(8,128)} %broadcast_in_dim.25), calls=%async_computation.2 | async-start | bytes 4194304 | tf_op jit(solution)/shard_map/all_to_all | solution.py:350
  103.0 3.0 %collective-permute-start.8 = (f32[1024,256]{1,0:T(8,128)S(1)}, f32[1024,256]{1,0:T(8,128)S(1)}, u32[]{:S(2)}, u32[]{:S(2)}) collective-permute-start(f32[1024,256]{1,0:T(8,128)S(1)} %add.32.mine_ref), channel_id=1, source_target_pairs={{0,1},{1,0},{2,3},{3,2},{4,5},{5,4},{6,7},{7,6},{8,9},{9,8},{10,11... | collective-permute-start | bytes 3145736 | tf_op jit(solution)/shard_map/ppermute | solution.py:354

commit v4 on v3

--- a/solution.py
+++ b/solution.py
@@ -194,8 +194,12 @@
             p = jnp.where(r == 0, jnp.where(c == 0, l_ref[:NB, :NB], zero), p)
             p = jnp.where(r == 1, jnp.where(c == 0, l_ref[NB:, :NB], l_ref[NB:, NB:]), p)
         p_ref[at, :] = p
-    copies.append(pltpu.make_async_copy(p_ref, p_hbm, p_sem))
-    copies[-1].start()
+    @pl.when(c < 2)
+    def _():
+        copy = pltpu.make_async_copy(p_ref, p_hbm, p_sem)
+        copy.start()
+        copy.wait()
+
     for copy in copies:
         copy.wait()
 
@@ -221,54 +225,75 @@
     )(pos, mine, other, *factors)
 
 
-def update_kernel(pos_ref, a_hbm, p_hbm, q_hbm, gc_ref, o_hbm, a_ref, p_ref, q_ref, g_ref, o_ref, sems):
+def update_kernel(pos_ref, a_hbm, p_hbm, q_hbm, gc_ref, o_hbm, a_ref, q_ref, g_ref, o_ref, load_sems, store_sems, panel_sem):
     r = pos_ref[0]
     c = pos_ref[1]
     n = 2 * NB
     order = (3, 2, 1, 0)
-    rows = [slice(k * NB, (k + 1) * NB) for k in range(4)]
-    loads = {}
+    part = [slice(k * NB, (k + 1) * NB) for k in range(4)]
+    loads = {
+        k: [
+            pltpu.make_async_copy(q_hbm.at[part[k]], q_ref.at[part[k]], load_sems.at[0, k]),
+            pltpu.make_async_copy(a_hbm.at[part[k]], a_ref.at[part[k]], load_sems.at[1, k]),
+        ]
+        for k in order
+    }
     for k in order:
-        loads[k] = [
-            pltpu.make_async_copy(q_hbm.at[rows[k]], q_ref.at[rows[k]], sems.at[0, k]),
-            pltpu.make_async_copy(a_hbm.at[rows[k]], a_ref.at[rows[k]], sems.at[1, k]),
-            pltpu.make_async_copy(p_hbm.at[rows[k]], p_ref.at[rows[k]], sems.at[2, k]),
-        ]
         for copy in loads[k]:
             copy.start()
+    panel = pltpu.make_async_copy(p_hbm, o_ref.at[:, :NB], panel_sem)
+
+    @pl.when(c < 2)
+    def _():
+        panel.start()
+
+    def block(k, m):
+        small = dot_nt_16(q_ref[part[k], :], g_ref[part[m], :])
+        small += dot_nt_16(q_ref[part[k], :2 * n], g_ref[part[m], n:])
+        main = dot_nt_16(q_ref[part[k], :n], g_ref[part[m], 2 * n:])
+        o_ref[part[k], part[m]] = a_ref[part[k], part[m]] - (small + main)
+
+    def clear(k, m):
+        o_ref[part[k], part[m]] = jnp.zeros((NB, NB), F32)
 
     core = c % 2
-    for h, lane in enumerate((core, 1 - core)):
-        for m in range(4):
+    for m in range(4):
+        for h, lane in enumerate((core, 1 - core)):
             hi, mid, lo = split3(gc_ref[:, lane, m].reshape(NB, NB))
-            for k, part in enumerate((lo, mid, hi)):
-                g_ref[rows[m], k * n + h * NB:k * n + (h + 1) * NB] = part.astype(BF16)
+            for k, piece in enumerate((lo, mid, hi)):
+                g_ref[part[m], k * n + h * NB:k * n + (h + 1) * NB] = piece.astype(BF16)
+        for k in range(m):
+            clear(k, m)
 
     stores = []
     for k in order:
         for copy in loads[k]:
             copy.wait()
-        row = r + 16 * k
-        for m in range(4):
-            col = c + 16 * m
-
-            @pl.when(row < col)
+        for m in range(1, k):
+            block(k, m)
+
+        @pl.when(c >= 2)
+        def _():
+            if k > 0:
+                block(k, 0)
+
+        if k == 3:
+            @pl.when(c < 2)
             def _():
-                o_ref[rows[k], rows[m]] = jnp.zeros((NB, NB), F32)
-
-            @pl.when(row >= col)
-            def _():
-                small = dot_nt_16(q_ref[rows[k], :], g_ref[rows[m], :])
-                small += dot_nt_16(q_ref[rows[k], :2 * n], g_ref[rows[m], n:])
-                o_ref[rows[k], rows[m]] = a_ref[rows[k], rows[m]] - (
-                    small + dot_nt_16(q_ref[rows[k], :n], g_ref[rows[m], 2 * n:])
-                )
-
-        @pl.when(c < 2)
+                panel.wait()
+
+        inside = r >= c if k > 0 else (r >= c) & (c >= 2)
+        outside = r < c if k > 0 else (r < c) & (c >= 2)
+
+        @pl.when(inside)
         def _():
-            o_ref[rows[k], :NB] = p_ref[rows[k], :]
-
-        stores.append(pltpu.make_async_copy(o_ref.at[rows[k]], o_hbm.at[rows[k]], sems.at[3, k]))
+            block(k, k)
+
+        @pl.when(outside)
+        def _():
+            clear(k, k)
+
+        stores.append(pltpu.make_async_copy(o_ref.at[part[k]], o_hbm.at[part[k]], store_sems.at[k]))
         stores[-1].start()
     for copy in stores:
         copy.wait()
@@ -283,11 +308,12 @@
         out_specs=hbm,
         scratch_shapes=[
             pltpu.VMEM(a.shape, F32),
-            pltpu.VMEM(p.shape, F32),
             pltpu.VMEM(q.shape, BF16),
             pltpu.VMEM(q.shape, BF16),
             pltpu.VMEM(a.shape, F32),
-            pltpu.SemaphoreType.DMA((4, 4)),
+            pltpu.SemaphoreType.DMA((2, 4)),
+            pltpu.SemaphoreType.DMA((4,)),
+            pltpu.SemaphoreType.DMA(()),
         ],
         compiler_params=pltpu.CompilerParams(vmem_limit_bytes=32 * 2**20),
         cost_estimate=pl.CostEstimate(flops=8_000_000_000, bytes_accessed=13_000_000, transcendentals=0),
@@ -310,7 +336,7 @@
 )
 
 
-LEAD = (((0, 5),), ((0, 6), (5, 2)), ((0, 7), (6, 3), (5, 4), (2, 1)))
+LEAD = (((0, 5),), ((0, 7), (5, 3)), ((0, 1), (7, 6), (5, 4), (3, 2)))
 
 
 def along_z(x, moves):

time: 125 us -> 123 us (0.984)
  Pallas kernels: 35.9 us -> 34 us
    pallas_call x1, Pallas kernels: 9.43 us -> 7.53 us  [update(): pl.pallas_call(update_kernel, out_shape=jax.ShapeDtypeStruct(a.shape, F32...]
  transfers between devices with their start and end apart: 11 -> 11, of which waited for: 7 -> 7; matrix products, arithmetic and copies ran while one was open for 7% -> 7% of each run, Pallas kernels for 21% -> 22%
where the time goes in v4:
time: 123 us; the launch traced here: 122 us
  Pallas kernels  34 us (28%)
  starting transfers between devices  33.5 us (27%)
  waiting for transfers between devices  25 us (20%)
  blocking collectives  17.5 us (14%)
  other arithmetic  7.38 us (6%)
  local copies, waits for them, and re-layouts  4.63 us (4%)
    ppermute x6, starting transfers between devices, along_z(): return lax.ppermute(x, ('row', 'col'), pairs)  19.4 us
    pallas_call x1, Pallas kernels, factor(): pl.pallas_call(factor_kernel, out_shape=[both] * 2, in_specs=[SMEM, VMEM,...  17.7 us
    all_to_all x1, blocking collectives, per_device(): lax.all_to_all(x[:NB].reshape(16, 16, NB), 'row', 0, 0, tiled=True)[0:2]  17.5 us
    ppermute x6, waiting for transfers between devices, along_z(): return lax.ppermute(x, ('row', 'col'), pairs)  12.5 us
    all_to_all x1, waiting for transfers between devices, per_device(): held = lax.all_to_all(pieces, 'row', 0, 0, tiled=True)  8.53 us
    pallas_call x1, Pallas kernels, solve_rows(): pl.pallas_call(rows_kernel, out_shape=[pltpu.HBM(p.shape, F32), pltpu.HBM...  7.61 us
    pallas_call x1, Pallas kernels, update(): pl.pallas_call(update_kernel, out_shape=jax.ShapeDtypeStruct(a.shape, F32...  7.53 us
    all_to_all x1, starting transfers between devices, per_device(): held = lax.all_to_all(pieces, 'row', 0, 0, tiled=True)  7.02 us
  transfers between devices with their start and end apart: 11, of which 7 were waited for; matrix products, arithmetic and copies ran while one was open for 7% of the time, Pallas kernels for 22%

profile of v4, /device:TPU:8, one launch (start us, length us, event | category | flops | bytes accessed | tf_op | source)
XLA Modules:
  0.0 122.3 jit_solution(3907687820360804258)
XLA Ops:
  0.0 1.3 %slice_select_fusion = f32[1024,256]{1,0:T(8,128)S(1)} fusion(f32[1024,1024]{1,0:T(8,128)} %a_hbm.1, pred[]{:T(512)S(6)} %lt.10), kind=kLoop, calls=%fused_computation.1 | loop fusion | flops 262144 | bytes 2097153 | tf_op jit(solution)/shard_map/jit(_where)/select_n | solution.py:359
  1.3 5.2 %collective-permute-start.3 = (f32[1024,256]{1,0:T(8,128)S(1)}, f32[1024,256]{1,0:T(8,128)S(1)}, u32[]{:S(2)}, u32[]{:S(2)}) collective-permute-start(f32[1024,256]{1,0:T(8,128)S(1)} %slice_select_fusion), channel_id=1, source_target_pairs={{0,8},{1,9},{16,24},{17,25},{32,34},{33,35},{48,50},{49,51},{64,68... | collective-permute-start | bytes 3145736 | tf_op jit(solution)/shard_map/ppermute | solution.py:344
  6.5 1.0 slice.25
  7.5 17.5 %all_to_all.15 = f32[16,16,256]{2,1,0:T(8,128)S(1)} all-to-all(f32[16,16,256]{2,1,0:T(8,128)S(1)} %bitcast.22), channel_id=1, replica_groups=mesh['row'=16,'col'=16] {'row'}, dimensions={0} | all-to-all | bytes 524288 | tf_op jit(solution)/shard_map/all_to_all | solution.py:355
  25.0 1.4 %collective-permute-start = (f32[32,256]{1,0:T(8,128)S(1)}, f32[32,256]{1,0:T(8,128)S(1)}, u32[]{:S(2)}, u32[]{:S(2)}) collective-permute-start(f32[32,256]{1,0:T(8,128)S(1)} %bitcast.24), channel_id=1, source_target_pairs={{0,10},{1,11},{16,26},{17,27},{32,42},{33,43},{48,58},{49,59},{64,... | collective-permute-start | bytes 98312 | tf_op jit(solution)/shard_map/ppermute | solution.py:344
  26.4 1.6 %collective-permute-done = f32[32,256]{1,0:T(8,128)S(1)} collective-permute-done((f32[32,256]{1,0:T(8,128)S(1)}, f32[32,256]{1,0:T(8,128)S(1)}, u32[]{:S(2)}, u32[]{:S(2)}) %collective-permute-start) | collective-permute-done | bytes 32800 | tf_op jit(solution)/shard_map/ppermute | solution.py:344
  28.0 1.3 %collective-permute-start.1 = (f32[32,256]{1,0:T(8,128)S(1)}, f32[32,256]{1,0:T(8,128)S(1)}, u32[]{:S(2)}, u32[]{:S(2)}) collective-permute-start(f32[32,256]{1,0:T(8,128)S(1)} %bitcast_add_fusion), channel_id=1, source_target_pairs={{0,14},{1,15},{10,6},{11,7},{16,30},{17,31},{26,22},{27,23},{32,46... | collective-permute-start | bytes 98312 | tf_op jit(solution)/shard_map/ppermute | solution.py:344
  29.3 1.6 %collective-permute-done.1 = f32[32,256]{1,0:T(8,128)S(1)} collective-permute-done((f32[32,256]{1,0:T(8,128)S(1)}, f32[32,256]{1,0:T(8,128)S(1)}, u32[]{:S(2)}, u32[]{:S(2)}) %collective-permute-start.1) | collective-permute-done | bytes 32800 | tf_op jit(solution)/shard_map/ppermute | solution.py:344
  30.8 1.3 %collective-permute-start.2 = (f32[32,256]{1,0:T(8,128)S(1)}, f32[32,256]{1,0:T(8,128)S(1)}, u32[]{:S(2)}, u32[]{:S(2)}) collective-permute-start(f32[32,256]{1,0:T(8,128)S(1)} %add.26), channel_id=1, source_target_pairs={{0,2},{1,3},{14,12},{15,13},{10,8},{11,9},{6,4},{7,5},{16,18},{17,... | collective-permute-start | bytes 98312 | tf_op jit(solution)/shard_map/ppermute | solution.py:344
  32.1 0.7 pad_add_fusion.x_ref
  32.8 0.9 collective-permute-done.2
  33.7 1.4 %fusion = f32[1024,256]{1,0:T(8,128)S(1)} fusion(f32[1024,256]{1,0:T(8,128)S(1)} %collective-permute-done.3, f32[1024,1024]{1,0:T(8,128)} %a_hbm.1, pred[]{:T(512)S(6)} %lt.10), kind=kLoop, calls=%fused_computation.8 | loop fusion | flops 524288 | bytes 3145729 | tf_op jit(solution)/shard_map/add | solution.py:360
  35.1 7.3 %collective-permute-start.4 = (f32[1024,256]{1,0:T(8,128)S(1)}, f32[1024,256]{1,0:T(8,128)S(1)}, u32[]{:S(2)}, u32[]{:S(2)}) collective-permute-start(f32[1024,256]{1,0:T(8,128)S(1)} %fusion), channel_id=1, source_target_pairs={{0,12},{1,13},{8,4},{9,5},{16,28},{17,29},{24,20},{25,21},{32,44},... | collective-permute-start | bytes 3145736 | tf_op jit(solution)/shard_map/ppermute | solution.py:344
  42.5 1.2 %pad_maximum_fusion = f32[16,96,256]{2,1,0:T(8,128)} fusion(f32[16,32,256]{2,1,0:T(8,128)S(1)} %broadcast_in_dim.23, f32[16,64,256]{2,1,0:T(8,128)S(1)} %bitcast.21), kind=kLoop, calls=%fused_computation | loop fusion | flops 393216 | bytes 3145728 | tf_op jit(solution)/shard_map/concatenate | solution.py:364
  43.7 7.0 %all-to-all-start.1 = ((f32[16,96,256]{2,1,0:T(8,128)}), f32[16,96,256]{2,1,0:T(8,128)}, u32[]{:S(2)}, u32[]{:S(2)}) async-start(f32[16,96,256]{2,1,0:T(8,128)} %pad_maximum_fusion), calls=%async_computation.1 | async-start | bytes 3145728 | tf_op jit(solution)/shard_map/all_to_all | solution.py:365
  50.7 1.2 meanwhile.1.pos_ref
  51.9 8.4 %collective-permute-done.4 = f32[1024,256]{1,0:T(8,128)S(1)} collective-permute-done((f32[1024,256]{1,0:T(8,128)S(1)}, f32[1024,256]{1,0:T(8,128)S(1)}, u32[]{:S(2)}, u32[]{:S(2)}) %collective-permute-start.4) | collective-permute-done | bytes 1048608 | tf_op jit(solution)/shard_map/ppermute | solution.py:344
  60.4 8.5 %all-to-all-done.1 = f32[16,96,256]{2,1,0:T(8,128)} async-done(((f32[16,96,256]{2,1,0:T(8,128)}), f32[16,96,256]{2,1,0:T(8,128)}, u32[]{:S(2)}, u32[]{:S(2)}) %all-to-all-start.1) | async-done | bytes 1572896 | tf_op jit(solution)/shard_map/all_to_all | solution.py:365
  68.9 1.1 slice.32
  70.1 0.9 dynamic-slice_bitcast_fusion
  71.0 0.6 collective-permute-start.5
  71.5 1.1 add.31
  72.7 3.0 %collective-permute-start.7 = (f32[1024,256]{1,0:T(8,128)}, f32[1024,256]{1,0:T(8,128)}, u32[]{:S(2)}, u32[]{:S(2)}) collective-permute-start(f32[1024,256]{1,0:T(8,128)} %add.31), channel_id=1, source_target_pairs={{0,14},{1,15},{12,10},{13,11},{8,6},{9,7},{4,2},{5,3},{16,30},{17,... | collective-permute-start | bytes 3145736 | tf_op jit(solution)/shard_map/ppermute | solution.py:344
  75.6 1.6 %broadcast_in_dim.25 = f32[16,2,4,16,256]{4,3,2,1,0:T(8,128)} broadcast(f32[2,4,16,256]{3,2,1,0:T(8,128)S(1)} %maximum_bitcast_fusion), dimensions={1,2,3,4} | broadcast | bytes 2228224 | tf_op jit(solution)/shard_map/broadcast_in_dim | solution.py:376
  77.2 6.1 %all-to-all-start.2 = ((f32[16,2,4,16,256]{4,3,2,1,0:T(8,128)}), f32[16,2,4,16,256]{4,3,2,1,0:T(8,128)S(1)}, u32[]{:S(2)}, u32[]{:S(2)}) async-start(f32[16,2,4,16,256]{4,3,2,1,0:T(8,128)} %broadcast_in_dim.25), calls=%async_computation.2 | async-start | bytes 4194304 | tf_op jit(solution)/shard_map/all_to_all | solution.py:376
  83.3 17.7 %factor_lead.1 = (f32[512,512]{1,0:T(8,128)S(1)}, f32[512,512]{1,0:T(8,128)S(1)}) custom-call(s32[2]{0:T(128)S(1)} %copy-done, f32[16,2,16,256]{3,2,1,0:T(8,128)S(1)} %bitcast.19, f32[16,2,16,256]{3,2,1,0:T(8,128)S(1)} %collective-permute-done.6.theirs_ref), custom_call_target="tpu_custom_call" | custom-call | flops 15000000512 | bytes 4000000 | tf_op jit(solution)/shard_map/factor_lead/pallas_call | solution.py:140
  101.0 1.7 %add.32.mine_ref = f32[1024,256]{1,0:T(8,128)S(1)} add(f32[1024,256]{1,0:T(8,128)} %add.31, f32[1024,256]{1,0:T(8,128)} %collective-permute-done.7) | non-fusion elementwise | flops 262144 | bytes 3145728 | tf_op jit(solution)/shard_map/add | solution.py:379
  102.7 0.3 collective-permute-start.8
  103.0 2.6 %collective-permute-done.8.other_ref = f32[1024,256]{1,0:T(8,128)S(1)} collective-permute-done((f32[1024,256]{1,0:T(8,128)S(1)}, f32[1024,256]{1,0:T(8,128)S(1)}, u32[]{:S(2)}, u32[]{:S(2)}) %collective-permute-start.8) | collective-permute-done | bytes 1048608 | tf_op jit(solution)/shard_map/ppermute | solution.py:380
  105.6 7.6 %solve_rows.1 = (f32[1024,256]{1,0:T(8,128)}, bf16[1024,1536]{1,0:T(8,128)(2,1)}) custom-call(s32[2]{0:T(128)S(1)} %copy-done, f32[1024,256]{1,0:T(8,128)S(1)} %add.32.mine_ref, f32[1024,256]{1,0:T(8,128)S(1)} %collective-permute-done.8.other_ref, f32[512,512]{1,0:T(8,128)S(1)} %get-tuple-element.35.l_ref, f32[512,512]{1,0:T(8,128)S(1)} %get-tuple-element.36.w_ref), custom_call_target="tpu_custom_call" | custom-call | flops 8999999488 | bytes 5000000 | tf_op jit(solution)/shard_map/solve_rows/pallas_call | solution.py:211
  113.3 1.4 %all-to-all-done.2.gc_ref = f32[16,2,4,16,256]{4,3,2,1,0:T(8,128)S(1)} async-done(((f32[16,2,4,16,256]{4,3,2,1,0:T(8,128)}), f32[16,2,4,16,256]{4,3,2,1,0:T(8,128)S(1)}, u32[]{:S(2)}, u32[]{:S(2)}) %all-to-all-start.2) | async-done | bytes 2097184 | tf_op jit(solution)/shard_map/all_to_all | solution.py:376
  114.6 7.5 %update.1 = f32[1024,1024]{1,0:T(8,128)} custom-call(s32[2]{0:T(128)S(1)} %copy-done, f32[1024,1024]{1,0:T(8,128)} %a_hbm.1, f32[1024,256]{1,0:T(8,128)} %get-tuple-element.37.p_hbm, bf16[1024,1536]{1,0:T(8,128)(2,1)} %get-tuple-element.38.q_hbm, f32[16,2,4,16,256]{4,3,2,1,0:T(8,128)S(1)} %all-to-all-done.2.gc_ref), custom_call_target="tpu_custom_call" | custom-call | flops 8000000000 | bytes 13000000 | tf_op jit(solution)/shard_map/update/pallas_call | solution.py:304
  (14 shorter events, 0.3 us)
Async XLA Ops:
  1.3 32.4 %collective-permute-start.3 = (f32[1024,256]{1,0:T(8,128)S(1)}, f32[1024,256]{1,0:T(8,128)S(1)}, u32[]{:S(2)}, u32[]{:S(2)}) collective-permute-start(f32[1024,256]{1,0:T(8,128)S(1)} %slice_select_fusion), channel_id=1, source_target_pairs={{0,8},{1,9},{16,24},{17,25},{32,34},{33,35},{48,50},{49,51},{64,68... | collective-permute-start | bytes 3145736 | tf_op jit(solution)/shard_map/ppermute | solution.py:344
  25.0 3.0 %collective-permute-start = (f32[32,256]{1,0:T(8,128)S(1)}, f32[32,256]{1,0:T(8,128)S(1)}, u32[]{:S(2)}, u32[]{:S(2)}) collective-permute-start(f32[32,256]{1,0:T(8,128)S(1)} %bitcast.24), channel_id=1, source_target_pairs={{0,10},{1,11},{16,26},{17,27},{32,42},{33,43},{48,58},{49,59},{64,... | collective-permute-start | bytes 98312 | tf_op jit(solution)/shard_map/ppermute | solution.py:344
  28.0 2.9 %collective-permute-start.1 = (f32[32,256]{1,0:T(8,128)S(1)}, f32[32,256]{1,0:T(8,128)S(1)}, u32[]{:S(2)}, u32[]{:S(2)}) collective-permute-start(f32[32,256]{1,0:T(8,128)S(1)} %bitcast_add_fusion), channel_id=1, source_target_pairs={{0,14},{1,15},{10,6},{11,7},{16,30},{17,31},{26,22},{27,23},{32,46... | collective-permute-start | bytes 98312 | tf_op jit(solution)/shard_map/ppermute | solution.py:344
  30.8 2.9 %collective-permute-start.2 = (f32[32,256]{1,0:T(8,128)S(1)}, f32[32,256]{1,0:T(8,128)S(1)}, u32[]{:S(2)}, u32[]{:S(2)}) collective-permute-start(f32[32,256]{1,0:T(8,128)S(1)} %add.26), channel_id=1, source_target_pairs={{0,2},{1,3},{14,12},{15,13},{10,8},{11,9},{6,4},{7,5},{16,18},{17,... | collective-permute-start | bytes 98312 | tf_op jit(solution)/shard_map/ppermute | solution.py:344
  35.1 25.3 %collective-permute-start.4 = (f32[1024,256]{1,0:T(8,128)S(1)}, f32[1024,256]{1,0:T(8,128)S(1)}, u32[]{:S(2)}, u32[]{:S(2)}) collective-permute-start(f32[1024,256]{1,0:T(8,128)S(1)} %fusion), channel_id=1, source_target_pairs={{0,12},{1,13},{8,4},{9,5},{16,28},{17,29},{24,20},{25,21},{32,44},... | collective-permute-start | bytes 3145736 | tf_op jit(solution)/shard_map/ppermute | solution.py:344
  43.7 25.2 %all-to-all-start.1 = ((f32[16,96,256]{2,1,0:T(8,128)}), f32[16,96,256]{2,1,0:T(8,128)}, u32[]{:S(2)}, u32[]{:S(2)}) async-start(f32[16,96,256]{2,1,0:T(8,128)} %pad_maximum_fusion), calls=%async_computation.1 | async-start | bytes 3145728 | tf_op jit(solution)/shard_map/all_to_all | solution.py:365
  70.0 2.7 %collective-permute-start.6 = (f32[16,2,16,256]{3,2,1,0:T(8,128)S(1)}, f32[16,2,16,256]{3,2,1,0:T(8,128)S(1)}, u32[]{:S(2)}, u32[]{:S(2)}) collective-permute-start(f32[16,2,16,256]{3,2,1,0:T(8,128)S(1)} %bitcast.18), channel_id=1, source_target_pairs={{0,1},{1,0},{2,3},{3,2},{4,5},{5,4},{6,7},{7,6},{8,9},{9,8},{10,11... | collective-permute-start | bytes 1572872 | tf_op jit(solution)/shard_map/ppermute | solution.py:371
  71.0 1.7 %collective-permute-start.5 = (f32[64,256]{1,0:T(8,128)S(1)}, f32[64,256]{1,0:T(8,128)S(1)}, u32[]{:S(2)}, u32[]{:S(2)}) collective-permute-start(f32[64,256]{1,0:T(8,128)S(1)} %get-tuple-element.41), channel_id=1, source_target_pairs={{0,1},{1,0},{2,3},{3,2},{4,5},{5,4},{6,7},{7,6},{8,9},{9,8},{10,11... | collective-permute-start | bytes 196616 | tf_op jit(solution)/shard_map/ppermute | solution.py:373
  72.7 28.3 %collective-permute-start.7 = (f32[1024,256]{1,0:T(8,128)}, f32[1024,256]{1,0:T(8,128)}, u32[]{:S(2)}, u32[]{:S(2)}) collective-permute-start(f32[1024,256]{1,0:T(8,128)} %add.31), channel_id=1, source_target_pairs={{0,14},{1,15},{12,10},{13,11},{8,6},{9,7},{4,2},{5,3},{16,30},{17,... | collective-permute-start | bytes 3145736 | tf_op jit(solution)/shard_map/ppermute | solution.py:344
  77.2 6.1 %copy-start = (s32[2]{0:T(128)S(1)}, s32[2]{0:T(128)}, u32[]{:S(2)}) copy-start(s32[2]{0:T(128)} %meanwhile.1.pos_ref) | copy-start | bytes 28
  77.2 37.4 %all-to-all-start.2 = ((f32[16,2,4,16,256]{4,3,2,1,0:T(8,128)}), f32[16,2,4,16,256]{4,3,2,1,0:T(8,128)S(1)}, u32[]{:S(2)}, u32[]{:S(2)}) async-start(f32[16,2,4,16,256]{4,3,2,1,0:T(8,128)} %broadcast_in_dim.25), calls=%async_computation.2 | async-start | bytes 4194304 | tf_op jit(solution)/shard_map/all_to_all | solution.py:376
  102.7 3.0 %collective-permute-start.8 = (f32[1024,256]{1,0:T(8,128)S(1)}, f32[1024,256]{1,0:T(8,128)S(1)}, u32[]{:S(2)}, u32[]{:S(2)}) collective-permute-start(f32[1024,256]{1,0:T(8,128)S(1)} %add.32.mine_ref), channel_id=1, source_target_pairs={{0,1},{1,0},{2,3},{3,2},{4,5},{5,4},{6,7},{7,6},{8,9},{9,8},{10,11... | collective-permute-start | bytes 3145736 | tf_op jit(solution)/shard_map/ppermute | solution.py:380

commit v5 on v4

--- a/solution.py
+++ b/solution.py
@@ -148,7 +148,7 @@
             pltpu.VMEM((HB, 2 * HB), F32),
         ],
         compiler_params=pltpu.CompilerParams(vmem_limit_bytes=16 * 2**20),
-        cost_estimate=pl.CostEstimate(flops=15_000_000_000, bytes_accessed=4_000_000, transcendentals=0),
+        cost_estimate=pl.CostEstimate(flops=1_000_000, bytes_accessed=4_000_000, transcendentals=0),
         name="factor_lead",
     )(pos, mine, theirs)
 
@@ -220,7 +220,7 @@
             pltpu.SemaphoreType.DMA((4,)),
         ],
         compiler_params=pltpu.CompilerParams(vmem_limit_bytes=20 * 2**20),
-        cost_estimate=pl.CostEstimate(flops=9_000_000_000, bytes_accessed=5_000_000, transcendentals=0),
+        cost_estimate=pl.CostEstimate(flops=1_000_000, bytes_accessed=5_000_000, transcendentals=0),
         name="solve_rows",
     )(pos, mine, other, *factors)
 
@@ -363,9 +363,10 @@
     pieces = panel.reshape(4, 16, 16, NB).transpose(1, 0, 2, 3).reshape(16, 64, NB)
     pieces = jnp.concatenate([pieces, jnp.broadcast_to(lead[None], (16, 32, NB))], axis=1)
     held = lax.all_to_all(pieces, "row", 0, 0, tiled=True)
-    arrived = along_z(panel, lambda d: TREE[1][d])
-    held, arrived, pos = lax.optimization_barrier((held, arrived, meanwhile(pos)))
+    arrived, pos = lax.optimization_barrier((along_z(panel, lambda d: TREE[1][d]), meanwhile(pos)))
     panel += arrived
+    arrived = along_z(panel, lambda d: TREE[2][d])
+    held, panel, pos = lax.optimization_barrier((held, panel, pos))
 
     lead = held[:, 64:].reshape(16, 2, 16, NB)
     theirs = lax.ppermute(lead, "col", swap)
@@ -374,7 +375,6 @@
     mine, other, lead, theirs, panel = lax.optimization_barrier((mine, other, lead, theirs, panel))
     gc = jnp.stack([mine, other]).reshape(2, 4, 16, NB)
     gc = lax.all_to_all(jnp.broadcast_to(gc[None], (16, 2, 4, 16, NB)), "row", 0, 0, tiled=True)
-    arrived = along_z(panel, lambda d: TREE[2][d])
     *factors, arrived = lax.optimization_barrier((*factor(pos, lead, theirs), arrived))
     panel += arrived
     p, q = solve_rows(pos, panel, lax.ppermute(panel, "col", swap), factors)

time: 123 us -> 120 us (0.976)
  waiting for transfers between devices: 25 us -> 22.3 us
  local copies, waits for them, and re-layouts: 4.63 us -> 2.73 us
    all_to_all x1, waiting for transfers between devices: 8.53 us -> 6.89 us  [per_device(): held = lax.all_to_all(pieces, 'row', 0, 0, tiled=True)]
where the time goes in v5:
time: 120 us
  starting transfers between devices  34.5 us (29%)
  Pallas kernels  33.8 us (28%)
  waiting for transfers between devices  22.3 us (19%)
  blocking collectives  17.5 us (15%)
  other arithmetic  8.56 us (7%)
  local copies, waits for them, and re-layouts  2.73 us (2%)
    ppermute x6, starting transfers between devices, along_z(): return lax.ppermute(x, ('row', 'col'), pairs)  20.5 us
    pallas_call x1, Pallas kernels, factor(): pl.pallas_call(factor_kernel, out_shape=[both] * 2, in_specs=[SMEM, VMEM,...  17.7 us
    all_to_all x1, blocking collectives, per_device(): lax.all_to_all(x[:NB].reshape(16, 16, NB), 'row', 0, 0, tiled=True)[0:2]  17.5 us
    ppermute x6, waiting for transfers between devices, along_z(): return lax.ppermute(x, ('row', 'col'), pairs)  11.6 us
    pallas_call x1, Pallas kernels, update(): pl.pallas_call(update_kernel, out_shape=jax.ShapeDtypeStruct(a.shape, F32...  7.52 us
    pallas_call x1, Pallas kernels, solve_rows(): pl.pallas_call(rows_kernel, out_shape=[pltpu.HBM(p.shape, F32), pltpu.HBM...  7.39 us
    all_to_all x1, starting transfers between devices, per_device(): held = lax.all_to_all(pieces, 'row', 0, 0, tiled=True)  7.02 us
    all_to_all x1, waiting for transfers between devices, per_device(): held = lax.all_to_all(pieces, 'row', 0, 0, tiled=True)  6.89 us
  transfers between devices with their start and end apart: 11, of which 7 were waited for; matrix products, arithmetic and copies ran while one was open for 7% of the time, Pallas kernels for 22%

profile of v5, /device:TPU:8, one launch (start us, length us, event | category | flops | bytes accessed | tf_op | source)
XLA Modules:
  0.0 119.7 jit_solution(1031302579200309612)
XLA Ops:
  0.0 1.3 %slice_select_fusion = f32[1024,256]{1,0:T(8,128)S(1)} fusion(f32[1024,1024]{1,0:T(8,128)} %a_hbm.1, pred[]{:T(512)S(6)} %lt.10), kind=kLoop, calls=%fused_computation.1 | loop fusion | flops 262144 | bytes 2097153 | tf_op jit(solution)/shard_map/jit(_where)/select_n | solution.py:359
  1.3 5.2 %collective-permute-start.3 = (f32[1024,256]{1,0:T(8,128)S(1)}, f32[1024,256]{1,0:T(8,128)S(1)}, u32[]{:S(2)}, u32[]{:S(2)}) collective-permute-start(f32[1024,256]{1,0:T(8,128)S(1)} %slice_select_fusion), channel_id=1, source_target_pairs={{0,8},{1,9},{16,24},{17,25},{32,34},{33,35},{48,50},{49,51},{64,68... | collective-permute-start | bytes 3145736 | tf_op jit(solution)/shard_map/ppermute | solution.py:344
  6.5 1.0 slice.25
  7.5 17.5 %all_to_all.15 = f32[16,16,256]{2,1,0:T(8,128)S(1)} all-to-all(f32[16,16,256]{2,1,0:T(8,128)S(1)} %bitcast.22), channel_id=1, replica_groups=mesh['row'=16,'col'=16] {'row'}, dimensions={0} | all-to-all | bytes 524288 | tf_op jit(solution)/shard_map/all_to_all | solution.py:355
  25.0 1.4 %collective-permute-start = (f32[32,256]{1,0:T(8,128)S(1)}, f32[32,256]{1,0:T(8,128)S(1)}, u32[]{:S(2)}, u32[]{:S(2)}) collective-permute-start(f32[32,256]{1,0:T(8,128)S(1)} %bitcast.24), channel_id=1, source_target_pairs={{0,10},{1,11},{16,26},{17,27},{32,42},{33,43},{48,58},{49,59},{64,... | collective-permute-start | bytes 98312 | tf_op jit(solution)/shard_map/ppermute | solution.py:344
  26.4 1.6 %collective-permute-done = f32[32,256]{1,0:T(8,128)S(1)} collective-permute-done((f32[32,256]{1,0:T(8,128)S(1)}, f32[32,256]{1,0:T(8,128)S(1)}, u32[]{:S(2)}, u32[]{:S(2)}) %collective-permute-start) | collective-permute-done | bytes 32800 | tf_op jit(solution)/shard_map/ppermute | solution.py:344
  28.0 1.3 %collective-permute-start.1 = (f32[32,256]{1,0:T(8,128)S(1)}, f32[32,256]{1,0:T(8,128)S(1)}, u32[]{:S(2)}, u32[]{:S(2)}) collective-permute-start(f32[32,256]{1,0:T(8,128)S(1)} %bitcast_add_fusion), channel_id=1, source_target_pairs={{0,14},{1,15},{10,6},{11,7},{16,30},{17,31},{26,22},{27,23},{32,46... | collective-permute-start | bytes 98312 | tf_op jit(solution)/shard_map/ppermute | solution.py:344
  29.3 1.6 %collective-permute-done.1 = f32[32,256]{1,0:T(8,128)S(1)} collective-permute-done((f32[32,256]{1,0:T(8,128)S(1)}, f32[32,256]{1,0:T(8,128)S(1)}, u32[]{:S(2)}, u32[]{:S(2)}) %collective-permute-start.1) | collective-permute-done | bytes 32800 | tf_op jit(solution)/shard_map/ppermute | solution.py:344
  30.8 1.3 %collective-permute-start.2 = (f32[32,256]{1,0:T(8,128)S(1)}, f32[32,256]{1,0:T(8,128)S(1)}, u32[]{:S(2)}, u32[]{:S(2)}) collective-permute-start(f32[32,256]{1,0:T(8,128)S(1)} %add.26), channel_id=1, source_target_pairs={{0,2},{1,3},{14,12},{15,13},{10,8},{11,9},{6,4},{7,5},{16,18},{17,... | collective-permute-start | bytes 98312 | tf_op jit(solution)/shard_map/ppermute | solution.py:344
  32.1 0.6 pad_add_fusion.x_ref
  32.7 1.0 collective-permute-done.2
  33.7 1.4 %fusion = f32[1024,256]{1,0:T(8,128)S(1)} fusion(f32[1024,256]{1,0:T(8,128)S(1)} %collective-permute-done.3, f32[1024,1024]{1,0:T(8,128)} %a_hbm.1, pred[]{:T(512)S(6)} %lt.10), kind=kLoop, calls=%fused_computation.8 | loop fusion | flops 524288 | bytes 3145729 | tf_op jit(solution)/shard_map/add | solution.py:360
  35.1 8.2 %collective-permute-start.4 = (f32[1024,256]{1,0:T(8,128)S(1)}, f32[1024,256]{1,0:T(8,128)}, u32[]{:S(2)}, u32[]{:S(2)}) collective-permute-start(f32[1024,256]{1,0:T(8,128)S(1)} %fusion), channel_id=1, source_target_pairs={{0,12},{1,13},{8,4},{9,5},{16,28},{17,29},{24,20},{25,21},{32,44},... | collective-permute-start | bytes 3145736 | tf_op jit(solution)/shard_map/ppermute | solution.py:344
  43.3 0.1 copy.2
  43.4 1.2 %pad_maximum_fusion = f32[16,96,256]{2,1,0:T(8,128)} fusion(f32[16,32,256]{2,1,0:T(8,128)S(1)} %broadcast_in_dim.23, f32[16,64,256]{2,1,0:T(8,128)S(1)} %bitcast.21), kind=kLoop, calls=%fused_computation | loop fusion | flops 393216 | bytes 3145728 | tf_op jit(solution)/shard_map/concatenate | solution.py:364
  44.6 7.0 %all-to-all-start.1 = ((f32[16,96,256]{2,1,0:T(8,128)}), f32[16,96,256]{2,1,0:T(8,128)S(1)}, u32[]{:S(2)}, u32[]{:S(2)}) async-start(f32[16,96,256]{2,1,0:T(8,128)} %pad_maximum_fusion), calls=%async_computation.1 | async-start | bytes 3145728 | tf_op jit(solution)/shard_map/all_to_all | solution.py:365
  51.7 1.2 meanwhile.1.pos_ref
  52.9 7.5 %collective-permute-done.4 = f32[1024,256]{1,0:T(8,128)} collective-permute-done((f32[1024,256]{1,0:T(8,128)S(1)}, f32[1024,256]{1,0:T(8,128)}, u32[]{:S(2)}, u32[]{:S(2)}) %collective-permute-start.4) | collective-permute-done | bytes 1048608 | tf_op jit(solution)/shard_map/ppermute | solution.py:344
  60.4 2.3 %add.29 = f32[1024,256]{1,0:T(8,128)} add(f32[1024,256]{1,0:T(8,128)S(1)} %fusion, f32[1024,256]{1,0:T(8,128)} %collective-permute-done.4) | non-fusion elementwise | flops 262144 | bytes 3145728 | tf_op jit(solution)/shard_map/add | solution.py:367
  62.7 6.9 %all-to-all-done.1 = f32[16,96,256]{2,1,0:T(8,128)S(1)} async-done(((f32[16,96,256]{2,1,0:T(8,128)}), f32[16,96,256]{2,1,0:T(8,128)S(1)}, u32[]{:S(2)}, u32[]{:S(2)}) %all-to-all-start.1) | async-done | bytes 1572896 | tf_op jit(solution)/shard_map/all_to_all | solution.py:365
  69.6 0.1 collective-permute-start.6
  69.8 0.6 collective-permute-start.5
  70.3 3.1 %collective-permute-start.7 = (f32[1024,256]{1,0:T(8,128)}, f32[1024,256]{1,0:T(8,128)}, u32[]{:S(2)}, u32[]{:S(2)}) collective-permute-start(f32[1024,256]{1,0:T(8,128)} %add.29), channel_id=1, source_target_pairs={{0,14},{1,15},{12,10},{13,11},{8,6},{9,7},{4,2},{5,3},{16,30},{17,... | collective-permute-start | bytes 3145736 | tf_op jit(solution)/shard_map/ppermute | solution.py:344
  73.4 1.6 %broadcast_in_dim.25 = f32[16,2,4,16,256]{4,3,2,1,0:T(8,128)} broadcast(f32[2,4,16,256]{3,2,1,0:T(8,128)S(1)} %maximum_bitcast_fusion), dimensions={1,2,3,4} | broadcast | bytes 2228224 | tf_op jit(solution)/shard_map/broadcast_in_dim | solution.py:377
  75.0 6.1 %all-to-all-start.2 = ((f32[16,2,4,16,256]{4,3,2,1,0:T(8,128)}), f32[16,2,4,16,256]{4,3,2,1,0:T(8,128)S(1)}, u32[]{:S(2)}, u32[]{:S(2)}) async-start(f32[16,2,4,16,256]{4,3,2,1,0:T(8,128)} %broadcast_in_dim.25), calls=%async_computation.2 | async-start | bytes 4194304 | tf_op jit(solution)/shard_map/all_to_all | solution.py:377
  81.1 17.7 %factor_lead.1 = (f32[512,512]{1,0:T(8,128)S(1)}, f32[512,512]{1,0:T(8,128)S(1)}) custom-call(s32[2]{0:T(128)S(1)} %copy-done, f32[16,2,16,256]{3,2,1,0:T(8,128)S(1)} %bitcast.19, f32[16,2,16,256]{3,2,1,0:T(8,128)S(1)} %collective-permute-done.6.theirs_ref), custom_call_target="tpu_custom_call" | custom-call | flops 1000000 | bytes 4000000 | tf_op jit(solution)/shard_map/factor_lead/pallas_call | solution.py:140
  98.8 1.7 %add.32.mine_ref = f32[1024,256]{1,0:T(8,128)S(1)} add(f32[1024,256]{1,0:T(8,128)} %add.29, f32[1024,256]{1,0:T(8,128)} %collective-permute-done.7) | non-fusion elementwise | flops 262144 | bytes 3145728 | tf_op jit(solution)/shard_map/add | solution.py:379
  100.5 0.3 collective-permute-start.8
  100.8 2.6 %collective-permute-done.8.other_ref = f32[1024,256]{1,0:T(8,128)S(1)} collective-permute-done((f32[1024,256]{1,0:T(8,128)S(1)}, f32[1024,256]{1,0:T(8,128)S(1)}, u32[]{:S(2)}, u32[]{:S(2)}) %collective-permute-start.8) | collective-permute-done | bytes 1048608 | tf_op jit(solution)/shard_map/ppermute | solution.py:380
  103.4 7.4 %solve_rows.1 = (f32[1024,256]{1,0:T(8,128)}, bf16[1024,1536]{1,0:T(8,128)(2,1)}) custom-call(s32[2]{0:T(128)S(1)} %copy-done, f32[1024,256]{1,0:T(8,128)S(1)} %add.32.mine_ref, f32[1024,256]{1,0:T(8,128)S(1)} %collective-permute-done.8.other_ref, f32[512,512]{1,0:T(8,128)S(1)} %get-tuple-element.39.l_ref, f32[512,512]{1,0:T(8,128)S(1)} %get-tuple-element.40.w_ref), custom_call_target="tpu_custom_call" | custom-call | flops 1000000 | bytes 5000000 | tf_op jit(solution)/shard_map/solve_rows/pallas_call | solution.py:211
  110.8 1.2 all-to-all-done.2.gc_ref
  112.0 7.5 %update.1 = f32[1024,1024]{1,0:T(8,128)} custom-call(s32[2]{0:T(128)S(1)} %copy-done, f32[1024,1024]{1,0:T(8,128)} %a_hbm.1, f32[1024,256]{1,0:T(8,128)} %get-tuple-element.41.p_hbm, bf16[1024,1536]{1,0:T(8,128)(2,1)} %get-tuple-element.42.q_hbm, f32[16,2,4,16,256]{4,3,2,1,0:T(8,128)S(1)} %all-to-all-done.2.gc_ref), custom_call_target="tpu_custom_call" | custom-call | flops 8000000000 | bytes 13000000 | tf_op jit(solution)/shard_map/update/pallas_call | solution.py:304
  (14 shorter events, 0.1 us)
Async XLA Ops:
  1.3 32.4 %collective-permute-start.3 = (f32[1024,256]{1,0:T(8,128)S(1)}, f32[1024,256]{1,0:T(8,128)S(1)}, u32[]{:S(2)}, u32[]{:S(2)}) collective-permute-start(f32[1024,256]{1,0:T(8,128)S(1)} %slice_select_fusion), channel_id=1, source_target_pairs={{0,8},{1,9},{16,24},{17,25},{32,34},{33,35},{48,50},{49,51},{64,68... | collective-permute-start | bytes 3145736 | tf_op jit(solution)/shard_map/ppermute | solution.py:344
  25.0 3.0 %collective-permute-start = (f32[32,256]{1,0:T(8,128)S(1)}, f32[32,256]{1,0:T(8,128)S(1)}, u32[]{:S(2)}, u32[]{:S(2)}) collective-permute-start(f32[32,256]{1,0:T(8,128)S(1)} %bitcast.24), channel_id=1, source_target_pairs={{0,10},{1,11},{16,26},{17,27},{32,42},{33,43},{48,58},{49,59},{64,... | collective-permute-start | bytes 98312 | tf_op jit(solution)/shard_map/ppermute | solution.py:344
  28.0 2.9 %collective-permute-start.1 = (f32[32,256]{1,0:T(8,128)S(1)}, f32[32,256]{1,0:T(8,128)S(1)}, u32[]{:S(2)}, u32[]{:S(2)}) collective-permute-start(f32[32,256]{1,0:T(8,128)S(1)} %bitcast_add_fusion), channel_id=1, source_target_pairs={{0,14},{1,15},{10,6},{11,7},{16,30},{17,31},{26,22},{27,23},{32,46... | collective-permute-start | bytes 98312 | tf_op jit(solution)/shard_map/ppermute | solution.py:344
  30.8 2.9 %collective-permute-start.2 = (f32[32,256]{1,0:T(8,128)S(1)}, f32[32,256]{1,0:T(8,128)S(1)}, u32[]{:S(2)}, u32[]{:S(2)}) collective-permute-start(f32[32,256]{1,0:T(8,128)S(1)} %add.26), channel_id=1, source_target_pairs={{0,2},{1,3},{14,12},{15,13},{10,8},{11,9},{6,4},{7,5},{16,18},{17,... | collective-permute-start | bytes 98312 | tf_op jit(solution)/shard_map/ppermute | solution.py:344
  35.1 25.3 %collective-permute-start.4 = (f32[1024,256]{1,0:T(8,128)S(1)}, f32[1024,256]{1,0:T(8,128)}, u32[]{:S(2)}, u32[]{:S(2)}) collective-permute-start(f32[1024,256]{1,0:T(8,128)S(1)} %fusion), channel_id=1, source_target_pairs={{0,12},{1,13},{8,4},{9,5},{16,28},{17,29},{24,20},{25,21},{32,44},... | collective-permute-start | bytes 3145736 | tf_op jit(solution)/shard_map/ppermute | solution.py:344
  44.6 24.9 %all-to-all-start.1 = ((f32[16,96,256]{2,1,0:T(8,128)}), f32[16,96,256]{2,1,0:T(8,128)S(1)}, u32[]{:S(2)}, u32[]{:S(2)}) async-start(f32[16,96,256]{2,1,0:T(8,128)} %pad_maximum_fusion), calls=%async_computation.1 | async-start | bytes 3145728 | tf_op jit(solution)/shard_map/all_to_all | solution.py:365
  69.6 3.8 %collective-permute-start.6 = (f32[16,2,16,256]{3,2,1,0:T(8,128)S(1)}, f32[16,2,16,256]{3,2,1,0:T(8,128)S(1)}, u32[]{:S(2)}, u32[]{:S(2)}) collective-permute-start(f32[16,2,16,256]{3,2,1,0:T(8,128)S(1)} %bitcast.18), channel_id=1, source_target_pairs={{0,1},{1,0},{2,3},{3,2},{4,5},{5,4},{6,7},{7,6},{8,9},{9,8},{10,11... | collective-permute-start | bytes 1572872 | tf_op jit(solution)/shard_map/ppermute | solution.py:372
  69.8 3.7 %collective-permute-start.5 = (f32[64,256]{1,0:T(8,128)S(1)}, f32[64,256]{1,0:T(8,128)S(1)}, u32[]{:S(2)}, u32[]{:S(2)}) collective-permute-start(f32[64,256]{1,0:T(8,128)S(1)} %get-tuple-element.45), channel_id=1, source_target_pairs={{0,1},{1,0},{2,3},{3,2},{4,5},{5,4},{6,7},{7,6},{8,9},{9,8},{10,11... | collective-permute-start | bytes 196616 | tf_op jit(solution)/shard_map/ppermute | solution.py:374
  70.3 28.4 %collective-permute-start.7 = (f32[1024,256]{1,0:T(8,128)}, f32[1024,256]{1,0:T(8,128)}, u32[]{:S(2)}, u32[]{:S(2)}) collective-permute-start(f32[1024,256]{1,0:T(8,128)} %add.29), channel_id=1, source_target_pairs={{0,14},{1,15},{12,10},{13,11},{8,6},{9,7},{4,2},{5,3},{16,30},{17,... | collective-permute-start | bytes 3145736 | tf_op jit(solution)/shard_map/ppermute | solution.py:344
  75.0 6.1 %copy-start = (s32[2]{0:T(128)S(1)}, s32[2]{0:T(128)}, u32[]{:S(2)}) copy-start(s32[2]{0:T(128)} %meanwhile.1.pos_ref) | copy-start | bytes 28
  75.0 37.0 %all-to-all-start.2 = ((f32[16,2,4,16,256]{4,3,2,1,0:T(8,128)}), f32[16,2,4,16,256]{4,3,2,1,0:T(8,128)S(1)}, u32[]{:S(2)}, u32[]{:S(2)}) async-start(f32[16,2,4,16,256]{4,3,2,1,0:T(8,128)} %broadcast_in_dim.25), calls=%async_computation.2 | async-start | bytes 4194304 | tf_op jit(solution)/shard_map/all_to_all | solution.py:377
  100.5 3.0 %collective-permute-start.8 = (f32[1024,256]{1,0:T(8,128)S(1)}, f32[1024,256]{1,0:T(8,128)S(1)}, u32[]{:S(2)}, u32[]{:S(2)}) collective-permute-start(f32[1024,256]{1,0:T(8,128)S(1)} %add.32.mine_ref), channel_id=1, source_target_pairs={{0,1},{1,0},{2,3},{3,2},{4,5},{5,4},{6,7},{7,6},{8,9},{9,8},{10,11... | collective-permute-start | bytes 3145736 | tf_op jit(solution)/shard_map/ppermute | solution.py:380

commit v6 on v5

--- a/solution.py
+++ b/solution.py
@@ -174,6 +174,7 @@
     n = 2 * NB
     lane0 = c % 2 == 0
     copies = []
+    panels = []
     for k in range(4):
         at = slice(k * NB, (k + 1) * NB)
         mine = mine_ref[at, :]
@@ -194,14 +195,15 @@
             p = jnp.where(r == 0, jnp.where(c == 0, l_ref[:NB, :NB], zero), p)
             p = jnp.where(r == 1, jnp.where(c == 0, l_ref[NB:, :NB], l_ref[NB:, NB:]), p)
         p_ref[at, :] = p
+        panels.append(pltpu.make_async_copy(p_ref.at[at], p_hbm.at[at], p_sem.at[k]))
+        pl.when(c < 2)(panels[-1].start)
+    for copy in copies:
+        copy.wait()
+
     @pl.when(c < 2)
     def _():
-        copy = pltpu.make_async_copy(p_ref, p_hbm, p_sem)
-        copy.start()
-        copy.wait()
-
-    for copy in copies:
-        copy.wait()
+        for copy in panels:
+            copy.wait()
 
 
 def solve_rows(pos, mine, other, factors):
@@ -216,7 +218,7 @@
         scratch_shapes=[
             pltpu.VMEM(p.shape, F32),
             pltpu.VMEM(q.shape, BF16),
-            pltpu.SemaphoreType.DMA(()),
+            pltpu.SemaphoreType.DMA((4,)),
             pltpu.SemaphoreType.DMA((4,)),
         ],
         compiler_params=pltpu.CompilerParams(vmem_limit_bytes=20 * 2**20),
@@ -238,14 +240,17 @@
         ]
         for k in order
     }
-    for k in order:
-        for copy in loads[k]:
-            copy.start()
+    for copy in loads[3]:
+        copy.start()
     panel = pltpu.make_async_copy(p_hbm, o_ref.at[:, :NB], panel_sem)
 
     @pl.when(c < 2)
     def _():
         panel.start()
+
+    for k in order[1:]:
+        for copy in loads[k]:
+            copy.start()
 
     def block(k, m):
         small = dot_nt_16(q_ref[part[k], :], g_ref[part[m], :])
@@ -256,12 +261,16 @@
     def clear(k, m):
         o_ref[part[k], part[m]] = jnp.zeros((NB, NB), F32)
 
-    core = c % 2
-    for m in range(4):
+    def split(m):
+        core = c % 2
         for h, lane in enumerate((core, 1 - core)):
             hi, mid, lo = split3(gc_ref[:, lane, m].reshape(NB, NB))
             for k, piece in enumerate((lo, mid, hi)):
                 g_ref[part[m], k * n + h * NB:k * n + (h + 1) * NB] = piece.astype(BF16)
+
+    pl.when(c >= 2)(lambda: split(0))
+    for m in range(1, 4):
+        split(m)
         for k in range(m):
             clear(k, m)
 

time: 120 us -> 121 us (level)
  no operation moved by 1% of the time
where the time goes in v6:
time: 121 us; the launch traced here: 120 us
  starting transfers between devices  34.5 us (29%)
  Pallas kernels  34.1 us (28%)
  waiting for transfers between devices  22.3 us (18%)
  blocking collectives  17.5 us (14%)
  other arithmetic  8.56 us (7%)
  local copies, waits for them, and re-layouts  2.73 us (2%)
    ppermute x6, starting transfers between devices, along_z(): return lax.ppermute(x, ('row', 'col'), pairs)  20.5 us
    pallas_call x1, Pallas kernels, factor(): pl.pallas_call(factor_kernel, out_shape=[both] * 2, in_specs=[SMEM, VMEM,...  17.7 us
    all_to_all x1, blocking collectives, per_device(): lax.all_to_all(x[:NB].reshape(16, 16, NB), 'row', 0, 0, tiled=True)[0:2]  17.5 us
    ppermute x6, waiting for transfers between devices, along_z(): return lax.ppermute(x, ('row', 'col'), pairs)  11.6 us
    pallas_call x1, Pallas kernels, update(): pl.pallas_call(update_kernel, out_shape=jax.ShapeDtypeStruct(a.shape, F32...  7.83 us
    pallas_call x1, Pallas kernels, solve_rows(): pl.pallas_call(rows_kernel, out_shape=[pltpu.HBM(p.shape, F32), pltpu.HBM...  7.43 us
    all_to_all x1, starting transfers between devices, per_device(): held = lax.all_to_all(pieces, 'row', 0, 0, tiled=True)  7.02 us
    all_to_all x1, waiting for transfers between devices, per_device(): held = lax.all_to_all(pieces, 'row', 0, 0, tiled=True)  6.89 us
  transfers between devices with their start and end apart: 11, of which 7 were waited for; matrix products, arithmetic and copies ran while one was open for 7% of the time, Pallas kernels for 22%

profile of v6, /device:TPU:8, one launch (start us, length us, event | category | flops | bytes accessed | tf_op | source)
XLA Modules:
  0.0 120.0 jit_solution(13483659776956531679)
XLA Ops:
  0.0 1.3 %slice_select_fusion = f32[1024,256]{1,0:T(8,128)S(1)} fusion(f32[1024,1024]{1,0:T(8,128)} %a_hbm.1, pred[]{:T(512)S(6)} %lt.10), kind=kLoop, calls=%fused_computation.1 | loop fusion | flops 262144 | bytes 2097153 | tf_op jit(solution)/shard_map/jit(_where)/select_n | solution.py:368
  1.3 5.2 %collective-permute-start.3 = (f32[1024,256]{1,0:T(8,128)S(1)}, f32[1024,256]{1,0:T(8,128)S(1)}, u32[]{:S(2)}, u32[]{:S(2)}) collective-permute-start(f32[1024,256]{1,0:T(8,128)S(1)} %slice_select_fusion), channel_id=1, source_target_pairs={{0,8},{1,9},{16,24},{17,25},{32,34},{33,35},{48,50},{49,51},{64,68... | collective-permute-start | bytes 3145736 | tf_op jit(solution)/shard_map/ppermute | solution.py:353
  6.5 1.0 slice.25
  7.5 17.5 %all_to_all.15 = f32[16,16,256]{2,1,0:T(8,128)S(1)} all-to-all(f32[16,16,256]{2,1,0:T(8,128)S(1)} %bitcast.22), channel_id=1, replica_groups=mesh['row'=16,'col'=16] {'row'}, dimensions={0} | all-to-all | bytes 524288 | tf_op jit(solution)/shard_map/all_to_all | solution.py:364
  25.0 1.4 %collective-permute-start = (f32[32,256]{1,0:T(8,128)S(1)}, f32[32,256]{1,0:T(8,128)S(1)}, u32[]{:S(2)}, u32[]{:S(2)}) collective-permute-start(f32[32,256]{1,0:T(8,128)S(1)} %bitcast.24), channel_id=1, source_target_pairs={{0,10},{1,11},{16,26},{17,27},{32,42},{33,43},{48,58},{49,59},{64,... | collective-permute-start | bytes 98312 | tf_op jit(solution)/shard_map/ppermute | solution.py:353
  26.4 1.6 %collective-permute-done = f32[32,256]{1,0:T(8,128)S(1)} collective-permute-done((f32[32,256]{1,0:T(8,128)S(1)}, f32[32,256]{1,0:T(8,128)S(1)}, u32[]{:S(2)}, u32[]{:S(2)}) %collective-permute-start) | collective-permute-done | bytes 32800 | tf_op jit(solution)/shard_map/ppermute | solution.py:353
  28.0 1.3 %collective-permute-start.1 = (f32[32,256]{1,0:T(8,128)S(1)}, f32[32,256]{1,0:T(8,128)S(1)}, u32[]{:S(2)}, u32[]{:S(2)}) collective-permute-start(f32[32,256]{1,0:T(8,128)S(1)} %bitcast_add_fusion), channel_id=1, source_target_pairs={{0,14},{1,15},{10,6},{11,7},{16,30},{17,31},{26,22},{27,23},{32,46... | collective-permute-start | bytes 98312 | tf_op jit(solution)/shard_map/ppermute | solution.py:353
  29.3 1.6 %collective-permute-done.1 = f32[32,256]{1,0:T(8,128)S(1)} collective-permute-done((f32[32,256]{1,0:T(8,128)S(1)}, f32[32,256]{1,0:T(8,128)S(1)}, u32[]{:S(2)}, u32[]{:S(2)}) %collective-permute-start.1) | collective-permute-done | bytes 32800 | tf_op jit(solution)/shard_map/ppermute | solution.py:353
  30.8 1.3 %collective-permute-start.2 = (f32[32,256]{1,0:T(8,128)S(1)}, f32[32,256]{1,0:T(8,128)S(1)}, u32[]{:S(2)}, u32[]{:S(2)}) collective-permute-start(f32[32,256]{1,0:T(8,128)S(1)} %add.26), channel_id=1, source_target_pairs={{0,2},{1,3},{14,12},{15,13},{10,8},{11,9},{6,4},{7,5},{16,18},{17,... | collective-permute-start | bytes 98312 | tf_op jit(solution)/shard_map/ppermute | solution.py:353
  32.1 0.6 pad_add_fusion.x_ref
  32.7 1.0 collective-permute-done.2
  33.7 1.4 %fusion = f32[1024,256]{1,0:T(8,128)S(1)} fusion(f32[1024,256]{1,0:T(8,128)S(1)} %collective-permute-done.3, f32[1024,1024]{1,0:T(8,128)} %a_hbm.1, pred[]{:T(512)S(6)} %lt.10), kind=kLoop, calls=%fused_computation.8 | loop fusion | flops 524288 | bytes 3145729 | tf_op jit(solution)/shard_map/add | solution.py:369
  35.1 8.2 %collective-permute-start.4 = (f32[1024,256]{1,0:T(8,128)S(1)}, f32[1024,256]{1,0:T(8,128)}, u32[]{:S(2)}, u32[]{:S(2)}) collective-permute-start(f32[1024,256]{1,0:T(8,128)S(1)} %fusion), channel_id=1, source_target_pairs={{0,12},{1,13},{8,4},{9,5},{16,28},{17,29},{24,20},{25,21},{32,44},... | collective-permute-start | bytes 3145736 | tf_op jit(solution)/shard_map/ppermute | solution.py:353
  43.3 0.1 copy.2
  43.4 1.2 %pad_maximum_fusion = f32[16,96,256]{2,1,0:T(8,128)} fusion(f32[16,32,256]{2,1,0:T(8,128)S(1)} %broadcast_in_dim.23, f32[16,64,256]{2,1,0:T(8,128)S(1)} %bitcast.21), kind=kLoop, calls=%fused_computation | loop fusion | flops 393216 | bytes 3145728 | tf_op jit(solution)/shard_map/concatenate | solution.py:373
  44.6 7.0 %all-to-all-start.1 = ((f32[16,96,256]{2,1,0:T(8,128)}), f32[16,96,256]{2,1,0:T(8,128)S(1)}, u32[]{:S(2)}, u32[]{:S(2)}) async-start(f32[16,96,256]{2,1,0:T(8,128)} %pad_maximum_fusion), calls=%async_computation.1 | async-start | bytes 3145728 | tf_op jit(solution)/shard_map/all_to_all | solution.py:374
  51.7 1.2 meanwhile.1.pos_ref
  52.9 7.5 %collective-permute-done.4 = f32[1024,256]{1,0:T(8,128)} collective-permute-done((f32[1024,256]{1,0:T(8,128)S(1)}, f32[1024,256]{1,0:T(8,128)}, u32[]{:S(2)}, u32[]{:S(2)}) %collective-permute-start.4) | collective-permute-done | bytes 1048608 | tf_op jit(solution)/shard_map/ppermute | solution.py:353
  60.4 2.3 %add.29 = f32[1024,256]{1,0:T(8,128)} add(f32[1024,256]{1,0:T(8,128)S(1)} %fusion, f32[1024,256]{1,0:T(8,128)} %collective-permute-done.4) | non-fusion elementwise | flops 262144 | bytes 3145728 | tf_op jit(solution)/shard_map/add | solution.py:376
  62.7 6.9 %all-to-all-done.1 = f32[16,96,256]{2,1,0:T(8,128)S(1)} async-done(((f32[16,96,256]{2,1,0:T(8,128)}), f32[16,96,256]{2,1,0:T(8,128)S(1)}, u32[]{:S(2)}, u32[]{:S(2)}) %all-to-all-start.1) | async-done | bytes 1572896 | tf_op jit(solution)/shard_map/all_to_all | solution.py:374
  69.6 0.1 collective-permute-start.6
  69.8 0.6 collective-permute-start.5
  70.3 3.1 %collective-permute-start.7 = (f32[1024,256]{1,0:T(8,128)}, f32[1024,256]{1,0:T(8,128)}, u32[]{:S(2)}, u32[]{:S(2)}) collective-permute-start(f32[1024,256]{1,0:T(8,128)} %add.29), channel_id=1, source_target_pairs={{0,14},{1,15},{12,10},{13,11},{8,6},{9,7},{4,2},{5,3},{16,30},{17,... | collective-permute-start | bytes 3145736 | tf_op jit(solution)/shard_map/ppermute | solution.py:353
  73.4 1.6 %broadcast_in_dim.25 = f32[16,2,4,16,256]{4,3,2,1,0:T(8,128)} broadcast(f32[2,4,16,256]{3,2,1,0:T(8,128)S(1)} %maximum_bitcast_fusion), dimensions={1,2,3,4} | broadcast | bytes 2228224 | tf_op jit(solution)/shard_map/broadcast_in_dim | solution.py:386
  75.0 6.1 %all-to-all-start.2 = ((f32[16,2,4,16,256]{4,3,2,1,0:T(8,128)}), f32[16,2,4,16,256]{4,3,2,1,0:T(8,128)S(1)}, u32[]{:S(2)}, u32[]{:S(2)}) async-start(f32[16,2,4,16,256]{4,3,2,1,0:T(8,128)} %broadcast_in_dim.25), calls=%async_computation.2 | async-start | bytes 4194304 | tf_op jit(solution)/shard_map/all_to_all | solution.py:386
  81.1 17.7 %factor_lead.1 = (f32[512,512]{1,0:T(8,128)S(1)}, f32[512,512]{1,0:T(8,128)S(1)}) custom-call(s32[2]{0:T(128)S(1)} %copy-done, f32[16,2,16,256]{3,2,1,0:T(8,128)S(1)} %bitcast.19, f32[16,2,16,256]{3,2,1,0:T(8,128)S(1)} %collective-permute-done.6.theirs_ref), custom_call_target="tpu_custom_call" | custom-call | flops 1000000 | bytes 4000000 | tf_op jit(solution)/shard_map/factor_lead/pallas_call | solution.py:140
  98.8 1.7 %add.32.mine_ref = f32[1024,256]{1,0:T(8,128)S(1)} add(f32[1024,256]{1,0:T(8,128)} %add.29, f32[1024,256]{1,0:T(8,128)} %collective-permute-done.7) | non-fusion elementwise | flops 262144 | bytes 3145728 | tf_op jit(solution)/shard_map/add | solution.py:388
  100.5 0.3 collective-permute-start.8
  100.8 2.6 %collective-permute-done.8.other_ref = f32[1024,256]{1,0:T(8,128)S(1)} collective-permute-done((f32[1024,256]{1,0:T(8,128)S(1)}, f32[1024,256]{1,0:T(8,128)S(1)}, u32[]{:S(2)}, u32[]{:S(2)}) %collective-permute-start.8) | collective-permute-done | bytes 1048608 | tf_op jit(solution)/shard_map/ppermute | solution.py:389
  103.4 7.4 %solve_rows.1 = (f32[1024,256]{1,0:T(8,128)}, bf16[1024,1536]{1,0:T(8,128)(2,1)}) custom-call(s32[2]{0:T(128)S(1)} %copy-done, f32[1024,256]{1,0:T(8,128)S(1)} %add.32.mine_ref, f32[1024,256]{1,0:T(8,128)S(1)} %collective-permute-done.8.other_ref, f32[512,512]{1,0:T(8,128)S(1)} %get-tuple-element.39.l_ref, f32[512,512]{1,0:T(8,128)S(1)} %get-tuple-element.40.w_ref), custom_call_target="tpu_custom_call" | custom-call | flops 1000000 | bytes 5000000 | tf_op jit(solution)/shard_map/solve_rows/pallas_call | solution.py:213
  110.9 1.1 all-to-all-done.2.gc_ref
  112.0 7.8 %update.1 = f32[1024,1024]{1,0:T(8,128)} custom-call(s32[2]{0:T(128)S(1)} %copy-done, f32[1024,1024]{1,0:T(8,128)} %a_hbm.1, f32[1024,256]{1,0:T(8,128)} %get-tuple-element.41.p_hbm, bf16[1024,1536]{1,0:T(8,128)(2,1)} %get-tuple-element.42.q_hbm, f32[16,2,4,16,256]{4,3,2,1,0:T(8,128)S(1)} %all-to-all-done.2.gc_ref), custom_call_target="tpu_custom_call" | custom-call | flops 8000000000 | bytes 13000000 | tf_op jit(solution)/shard_map/update/pallas_call | solution.py:313
  (14 shorter events, 0.1 us)
Async XLA Ops:
  1.3 32.4 %collective-permute-start.3 = (f32[1024,256]{1,0:T(8,128)S(1)}, f32[1024,256]{1,0:T(8,128)S(1)}, u32[]{:S(2)}, u32[]{:S(2)}) collective-permute-start(f32[1024,256]{1,0:T(8,128)S(1)} %slice_select_fusion), channel_id=1, source_target_pairs={{0,8},{1,9},{16,24},{17,25},{32,34},{33,35},{48,50},{49,51},{64,68... | collective-permute-start | bytes 3145736 | tf_op jit(solution)/shard_map/ppermute | solution.py:353
  25.0 3.0 %collective-permute-start = (f32[32,256]{1,0:T(8,128)S(1)}, f32[32,256]{1,0:T(8,128)S(1)}, u32[]{:S(2)}, u32[]{:S(2)}) collective-permute-start(f32[32,256]{1,0:T(8,128)S(1)} %bitcast.24), channel_id=1, source_target_pairs={{0,10},{1,11},{16,26},{17,27},{32,42},{33,43},{48,58},{49,59},{64,... | collective-permute-start | bytes 98312 | tf_op jit(solution)/shard_map/ppermute | solution.py:353
  28.0 2.9 %collective-permute-start.1 = (f32[32,256]{1,0:T(8,128)S(1)}, f32[32,256]{1,0:T(8,128)S(1)}, u32[]{:S(2)}, u32[]{:S(2)}) collective-permute-start(f32[32,256]{1,0:T(8,128)S(1)} %bitcast_add_fusion), channel_id=1, source_target_pairs={{0,14},{1,15},{10,6},{11,7},{16,30},{17,31},{26,22},{27,23},{32,46... | collective-permute-start | bytes 98312 | tf_op jit(solution)/shard_map/ppermute | solution.py:353
  30.8 2.9 %collective-permute-start.2 = (f32[32,256]{1,0:T(8,128)S(1)}, f32[32,256]{1,0:T(8,128)S(1)}, u32[]{:S(2)}, u32[]{:S(2)}) collective-permute-start(f32[32,256]{1,0:T(8,128)S(1)} %add.26), channel_id=1, source_target_pairs={{0,2},{1,3},{14,12},{15,13},{10,8},{11,9},{6,4},{7,5},{16,18},{17,... | collective-permute-start | bytes 98312 | tf_op jit(solution)/shard_map/ppermute | solution.py:353
  35.1 25.3 %collective-permute-start.4 = (f32[1024,256]{1,0:T(8,128)S(1)}, f32[1024,256]{1,0:T(8,128)}, u32[]{:S(2)}, u32[]{:S(2)}) collective-permute-start(f32[1024,256]{1,0:T(8,128)S(1)} %fusion), channel_id=1, source_target_pairs={{0,12},{1,13},{8,4},{9,5},{16,28},{17,29},{24,20},{25,21},{32,44},... | collective-permute-start | bytes 3145736 | tf_op jit(solution)/shard_map/ppermute | solution.py:353
  44.6 24.9 %all-to-all-start.1 = ((f32[16,96,256]{2,1,0:T(8,128)}), f32[16,96,256]{2,1,0:T(8,128)S(1)}, u32[]{:S(2)}, u32[]{:S(2)}) async-start(f32[16,96,256]{2,1,0:T(8,128)} %pad_maximum_fusion), calls=%async_computation.1 | async-start | bytes 3145728 | tf_op jit(solution)/shard_map/all_to_all | solution.py:374
  69.6 3.8 %collective-permute-start.6 = (f32[16,2,16,256]{3,2,1,0:T(8,128)S(1)}, f32[16,2,16,256]{3,2,1,0:T(8,128)S(1)}, u32[]{:S(2)}, u32[]{:S(2)}) collective-permute-start(f32[16,2,16,256]{3,2,1,0:T(8,128)S(1)} %bitcast.18), channel_id=1, source_target_pairs={{0,1},{1,0},{2,3},{3,2},{4,5},{5,4},{6,7},{7,6},{8,9},{9,8},{10,11... | collective-permute-start | bytes 1572872 | tf_op jit(solution)/shard_map/ppermute | solution.py:381
  69.8 3.7 %collective-permute-start.5 = (f32[64,256]{1,0:T(8,128)S(1)}, f32[64,256]{1,0:T(8,128)S(1)}, u32[]{:S(2)}, u32[]{:S(2)}) collective-permute-start(f32[64,256]{1,0:T(8,128)S(1)} %get-tuple-element.45), channel_id=1, source_target_pairs={{0,1},{1,0},{2,3},{3,2},{4,5},{5,4},{6,7},{7,6},{8,9},{9,8},{10,11... | collective-permute-start | bytes 196616 | tf_op jit(solution)/shard_map/ppermute | solution.py:383
  70.3 28.4 %collective-permute-start.7 = (f32[1024,256]{1,0:T(8,128)}, f32[1024,256]{1,0:T(8,128)}, u32[]{:S(2)}, u32[]{:S(2)}) collective-permute-start(f32[1024,256]{1,0:T(8,128)} %add.29), channel_id=1, source_target_pairs={{0,14},{1,15},{12,10},{13,11},{8,6},{9,7},{4,2},{5,3},{16,30},{17,... | collective-permute-start | bytes 3145736 | tf_op jit(solution)/shard_map/ppermute | solution.py:353
  75.0 6.1 %copy-start = (s32[2]{0:T(128)S(1)}, s32[2]{0:T(128)}, u32[]{:S(2)}) copy-start(s32[2]{0:T(128)} %meanwhile.1.pos_ref) | copy-start | bytes 28
  75.0 37.0 %all-to-all-start.2 = ((f32[16,2,4,16,256]{4,3,2,1,0:T(8,128)}), f32[16,2,4,16,256]{4,3,2,1,0:T(8,128)S(1)}, u32[]{:S(2)}, u32[]{:S(2)}) async-start(f32[16,2,4,16,256]{4,3,2,1,0:T(8,128)} %broadcast_in_dim.25), calls=%async_computation.2 | async-start | bytes 4194304 | tf_op jit(solution)/shard_map/all_to_all | solution.py:386
  100.5 3.0 %collective-permute-start.8 = (f32[1024,256]{1,0:T(8,128)S(1)}, f32[1024,256]{1,0:T(8,128)S(1)}, u32[]{:S(2)}, u32[]{:S(2)}) collective-permute-start(f32[1024,256]{1,0:T(8,128)S(1)} %add.32.mine_ref), channel_id=1, source_target_pairs={{0,1},{1,0},{2,3},{3,2},{4,5},{5,4},{6,7},{7,6},{8,9},{9,8},{10,11... | collective-permute-start | bytes 3145736 | tf_op jit(solution)/shard_map/ppermute | solution.py:389

commit v7 on v6

--- a/solution.py
+++ b/solution.py
@@ -268,9 +268,8 @@
             for k, piece in enumerate((lo, mid, hi)):
                 g_ref[part[m], k * n + h * NB:k * n + (h + 1) * NB] = piece.astype(BF16)
 
-    pl.when(c >= 2)(lambda: split(0))
+    split(1)
     for m in range(1, 4):
-        split(m)
         for k in range(m):
             clear(k, m)
 
@@ -280,9 +279,13 @@
             copy.wait()
         for m in range(1, k):
             block(k, m)
+            if k == 3:
+                split(m + 1)
 
         @pl.when(c >= 2)
         def _():
+            if k == 3:
+                split(0)
             if k > 0:
                 block(k, 0)
 

time: 121 us -> 120 us (level)
  no operation moved by 1% of the time
where the time goes in v7:
time: 120 us; the launch traced here: 119 us
  starting transfers between devices  34.5 us (29%)
  Pallas kernels  33.6 us (28%)
  waiting for transfers between devices  22.3 us (19%)
  blocking collectives  17.5 us (15%)
  other arithmetic  8.56 us (7%)
  local copies, waits for them, and re-layouts  2.73 us (2%)
    ppermute x6, starting transfers between devices, along_z(): return lax.ppermute(x, ('row', 'col'), pairs)  20.5 us
    pallas_call x1, Pallas kernels, factor(): pl.pallas_call(factor_kernel, out_shape=[both] * 2, in_specs=[SMEM, VMEM,...  17.7 us
    all_to_all x1, blocking collectives, per_device(): lax.all_to_all(x[:NB].reshape(16, 16, NB), 'row', 0, 0, tiled=True)[0:2]  17.5 us
    ppermute x6, waiting for transfers between devices, along_z(): return lax.ppermute(x, ('row', 'col'), pairs)  11.6 us
    pallas_call x1, Pallas kernels, solve_rows(): pl.pallas_call(rows_kernel, out_shape=[pltpu.HBM(p.shape, F32), pltpu.HBM...  7.43 us
    pallas_call x1, Pallas kernels, update(): pl.pallas_call(update_kernel, out_shape=jax.ShapeDtypeStruct(a.shape, F32...  7.29 us
    all_to_all x1, starting transfers between devices, per_device(): held = lax.all_to_all(pieces, 'row', 0, 0, tiled=True)  7.02 us
    all_to_all x1, waiting for transfers between devices, per_device(): held = lax.all_to_all(pieces, 'row', 0, 0, tiled=True)  6.89 us
  transfers between devices with their start and end apart: 11, of which 7 were waited for; matrix products, arithmetic and copies ran while one was open for 7% of the time, Pallas kernels for 22%

profile of v7, /device:TPU:8, one launch (start us, length us, event | category | flops | bytes accessed | tf_op | source)
XLA Modules:
  0.0 119.5 jit_solution(13103817114163209904)
XLA Ops:
  0.0 1.3 %slice_select_fusion = f32[1024,256]{1,0:T(8,128)S(1)} fusion(f32[1024,1024]{1,0:T(8,128)} %a_hbm.1, pred[]{:T(512)S(6)} %lt.10), kind=kLoop, calls=%fused_computation.1 | loop fusion | flops 262144 | bytes 2097153 | tf_op jit(solution)/shard_map/jit(_where)/select_n | solution.py:371
  1.3 5.2 %collective-permute-start.3 = (f32[1024,256]{1,0:T(8,128)S(1)}, f32[1024,256]{1,0:T(8,128)S(1)}, u32[]{:S(2)}, u32[]{:S(2)}) collective-permute-start(f32[1024,256]{1,0:T(8,128)S(1)} %slice_select_fusion), channel_id=1, source_target_pairs={{0,8},{1,9},{16,24},{17,25},{32,34},{33,35},{48,50},{49,51},{64,68... | collective-permute-start | bytes 3145736 | tf_op jit(solution)/shard_map/ppermute | solution.py:356
  6.5 1.0 slice.25
  7.5 17.5 %all_to_all.15 = f32[16,16,256]{2,1,0:T(8,128)S(1)} all-to-all(f32[16,16,256]{2,1,0:T(8,128)S(1)} %bitcast.22), channel_id=1, replica_groups=mesh['row'=16,'col'=16] {'row'}, dimensions={0} | all-to-all | bytes 524288 | tf_op jit(solution)/shard_map/all_to_all | solution.py:367
  25.0 1.4 %collective-permute-start = (f32[32,256]{1,0:T(8,128)S(1)}, f32[32,256]{1,0:T(8,128)S(1)}, u32[]{:S(2)}, u32[]{:S(2)}) collective-permute-start(f32[32,256]{1,0:T(8,128)S(1)} %bitcast.24), channel_id=1, source_target_pairs={{0,10},{1,11},{16,26},{17,27},{32,42},{33,43},{48,58},{49,59},{64,... | collective-permute-start | bytes 98312 | tf_op jit(solution)/shard_map/ppermute | solution.py:356
  26.4 1.6 %collective-permute-done = f32[32,256]{1,0:T(8,128)S(1)} collective-permute-done((f32[32,256]{1,0:T(8,128)S(1)}, f32[32,256]{1,0:T(8,128)S(1)}, u32[]{:S(2)}, u32[]{:S(2)}) %collective-permute-start) | collective-permute-done | bytes 32800 | tf_op jit(solution)/shard_map/ppermute | solution.py:356
  28.0 1.3 %collective-permute-start.1 = (f32[32,256]{1,0:T(8,128)S(1)}, f32[32,256]{1,0:T(8,128)S(1)}, u32[]{:S(2)}, u32[]{:S(2)}) collective-permute-start(f32[32,256]{1,0:T(8,128)S(1)} %bitcast_add_fusion), channel_id=1, source_target_pairs={{0,14},{1,15},{10,6},{11,7},{16,30},{17,31},{26,22},{27,23},{32,46... | collective-permute-start | bytes 98312 | tf_op jit(solution)/shard_map/ppermute | solution.py:356
  29.3 1.6 %collective-permute-done.1 = f32[32,256]{1,0:T(8,128)S(1)} collective-permute-done((f32[32,256]{1,0:T(8,128)S(1)}, f32[32,256]{1,0:T(8,128)S(1)}, u32[]{:S(2)}, u32[]{:S(2)}) %collective-permute-start.1) | collective-permute-done | bytes 32800 | tf_op jit(solution)/shard_map/ppermute | solution.py:356
  30.8 1.3 %collective-permute-start.2 = (f32[32,256]{1,0:T(8,128)S(1)}, f32[32,256]{1,0:T(8,128)S(1)}, u32[]{:S(2)}, u32[]{:S(2)}) collective-permute-start(f32[32,256]{1,0:T(8,128)S(1)} %add.26), channel_id=1, source_target_pairs={{0,2},{1,3},{14,12},{15,13},{10,8},{11,9},{6,4},{7,5},{16,18},{17,... | collective-permute-start | bytes 98312 | tf_op jit(solution)/shard_map/ppermute | solution.py:356
  32.1 0.6 pad_add_fusion.x_ref
  32.7 1.0 collective-permute-done.2
  33.7 1.4 %fusion = f32[1024,256]{1,0:T(8,128)S(1)} fusion(f32[1024,256]{1,0:T(8,128)S(1)} %collective-permute-done.3, f32[1024,1024]{1,0:T(8,128)} %a_hbm.1, pred[]{:T(512)S(6)} %lt.10), kind=kLoop, calls=%fused_computation.8 | loop fusion | flops 524288 | bytes 3145729 | tf_op jit(solution)/shard_map/add | solution.py:372
  35.1 8.2 %collective-permute-start.4 = (f32[1024,256]{1,0:T(8,128)S(1)}, f32[1024,256]{1,0:T(8,128)}, u32[]{:S(2)}, u32[]{:S(2)}) collective-permute-start(f32[1024,256]{1,0:T(8,128)S(1)} %fusion), channel_id=1, source_target_pairs={{0,12},{1,13},{8,4},{9,5},{16,28},{17,29},{24,20},{25,21},{32,44},... | collective-permute-start | bytes 3145736 | tf_op jit(solution)/shard_map/ppermute | solution.py:356
  43.3 0.1 copy.2
  43.4 1.2 %pad_maximum_fusion = f32[16,96,256]{2,1,0:T(8,128)} fusion(f32[16,32,256]{2,1,0:T(8,128)S(1)} %broadcast_in_dim.23, f32[16,64,256]{2,1,0:T(8,128)S(1)} %bitcast.21), kind=kLoop, calls=%fused_computation | loop fusion | flops 393216 | bytes 3145728 | tf_op jit(solution)/shard_map/concatenate | solution.py:376
  44.6 7.0 %all-to-all-start.1 = ((f32[16,96,256]{2,1,0:T(8,128)}), f32[16,96,256]{2,1,0:T(8,128)S(1)}, u32[]{:S(2)}, u32[]{:S(2)}) async-start(f32[16,96,256]{2,1,0:T(8,128)} %pad_maximum_fusion), calls=%async_computation.1 | async-start | bytes 3145728 | tf_op jit(solution)/shard_map/all_to_all | solution.py:377
  51.7 1.2 meanwhile.1.pos_ref
  52.9 7.5 %collective-permute-done.4 = f32[1024,256]{1,0:T(8,128)} collective-permute-done((f32[1024,256]{1,0:T(8,128)S(1)}, f32[1024,256]{1,0:T(8,128)}, u32[]{:S(2)}, u32[]{:S(2)}) %collective-permute-start.4) | collective-permute-done | bytes 1048608 | tf_op jit(solution)/shard_map/ppermute | solution.py:356
  60.4 2.3 %add.29 = f32[1024,256]{1,0:T(8,128)} add(f32[1024,256]{1,0:T(8,128)S(1)} %fusion, f32[1024,256]{1,0:T(8,128)} %collective-permute-done.4) | non-fusion elementwise | flops 262144 | bytes 3145728 | tf_op jit(solution)/shard_map/add | solution.py:379
  62.7 6.9 %all-to-all-done.1 = f32[16,96,256]{2,1,0:T(8,128)S(1)} async-done(((f32[16,96,256]{2,1,0:T(8,128)}), f32[16,96,256]{2,1,0:T(8,128)S(1)}, u32[]{:S(2)}, u32[]{:S(2)}) %all-to-all-start.1) | async-done | bytes 1572896 | tf_op jit(solution)/shard_map/all_to_all | solution.py:377
  69.6 0.1 collective-permute-start.6
  69.8 0.6 collective-permute-start.5
  70.3 3.1 %collective-permute-start.7 = (f32[1024,256]{1,0:T(8,128)}, f32[1024,256]{1,0:T(8,128)}, u32[]{:S(2)}, u32[]{:S(2)}) collective-permute-start(f32[1024,256]{1,0:T(8,128)} %add.29), channel_id=1, source_target_pairs={{0,14},{1,15},{12,10},{13,11},{8,6},{9,7},{4,2},{5,3},{16,30},{17,... | collective-permute-start | bytes 3145736 | tf_op jit(solution)/shard_map/ppermute | solution.py:356
  73.4 1.6 %broadcast_in_dim.25 = f32[16,2,4,16,256]{4,3,2,1,0:T(8,128)} broadcast(f32[2,4,16,256]{3,2,1,0:T(8,128)S(1)} %maximum_bitcast_fusion), dimensions={1,2,3,4} | broadcast | bytes 2228224 | tf_op jit(solution)/shard_map/broadcast_in_dim | solution.py:389
  75.0 6.1 %all-to-all-start.2 = ((f32[16,2,4,16,256]{4,3,2,1,0:T(8,128)}), f32[16,2,4,16,256]{4,3,2,1,0:T(8,128)S(1)}, u32[]{:S(2)}, u32[]{:S(2)}) async-start(f32[16,2,4,16,256]{4,3,2,1,0:T(8,128)} %broadcast_in_dim.25), calls=%async_computation.2 | async-start | bytes 4194304 | tf_op jit(solution)/shard_map/all_to_all | solution.py:389
  81.1 17.7 %factor_lead.1 = (f32[512,512]{1,0:T(8,128)S(1)}, f32[512,512]{1,0:T(8,128)S(1)}) custom-call(s32[2]{0:T(128)S(1)} %copy-done, f32[16,2,16,256]{3,2,1,0:T(8,128)S(1)} %bitcast.19, f32[16,2,16,256]{3,2,1,0:T(8,128)S(1)} %collective-permute-done.6.theirs_ref), custom_call_target="tpu_custom_call" | custom-call | flops 1000000 | bytes 4000000 | tf_op jit(solution)/shard_map/factor_lead/pallas_call | solution.py:140
  98.8 1.7 %add.32.mine_ref = f32[1024,256]{1,0:T(8,128)S(1)} add(f32[1024,256]{1,0:T(8,128)} %add.29, f32[1024,256]{1,0:T(8,128)} %collective-permute-done.7) | non-fusion elementwise | flops 262144 | bytes 3145728 | tf_op jit(solution)/shard_map/add | solution.py:391
  100.5 0.3 collective-permute-start.8
  100.8 2.6 %collective-permute-done.8.other_ref = f32[1024,256]{1,0:T(8,128)S(1)} collective-permute-done((f32[1024,256]{1,0:T(8,128)S(1)}, f32[1024,256]{1,0:T(8,128)S(1)}, u32[]{:S(2)}, u32[]{:S(2)}) %collective-permute-start.8) | collective-permute-done | bytes 1048608 | tf_op jit(solution)/shard_map/ppermute | solution.py:392
  103.4 7.4 %solve_rows.1 = (f32[1024,256]{1,0:T(8,128)}, bf16[1024,1536]{1,0:T(8,128)(2,1)}) custom-call(s32[2]{0:T(128)S(1)} %copy-done, f32[1024,256]{1,0:T(8,128)S(1)} %add.32.mine_ref, f32[1024,256]{1,0:T(8,128)S(1)} %collective-permute-done.8.other_ref, f32[512,512]{1,0:T(8,128)S(1)} %get-tuple-element.39.l_ref, f32[512,512]{1,0:T(8,128)S(1)} %get-tuple-element.40.w_ref), custom_call_target="tpu_custom_call" | custom-call | flops 1000000 | bytes 5000000 | tf_op jit(solution)/shard_map/solve_rows/pallas_call | solution.py:213
  110.9 1.1 all-to-all-done.2.gc_ref
  112.0 7.3 %update.1 = f32[1024,1024]{1,0:T(8,128)} custom-call(s32[2]{0:T(128)S(1)} %copy-done, f32[1024,1024]{1,0:T(8,128)} %a_hbm.1, f32[1024,256]{1,0:T(8,128)} %get-tuple-element.41.p_hbm, bf16[1024,1536]{1,0:T(8,128)(2,1)} %get-tuple-element.42.q_hbm, f32[16,2,4,16,256]{4,3,2,1,0:T(8,128)S(1)} %all-to-all-done.2.gc_ref), custom_call_target="tpu_custom_call" | custom-call | flops 8000000000 | bytes 13000000 | tf_op jit(solution)/shard_map/update/pallas_call | solution.py:316
  (14 shorter events, 0.1 us)
Async XLA Ops:
  1.3 32.4 %collective-permute-start.3 = (f32[1024,256]{1,0:T(8,128)S(1)}, f32[1024,256]{1,0:T(8,128)S(1)}, u32[]{:S(2)}, u32[]{:S(2)}) collective-permute-start(f32[1024,256]{1,0:T(8,128)S(1)} %slice_select_fusion), channel_id=1, source_target_pairs={{0,8},{1,9},{16,24},{17,25},{32,34},{33,35},{48,50},{49,51},{64,68... | collective-permute-start | bytes 3145736 | tf_op jit(solution)/shard_map/ppermute | solution.py:356
  25.0 3.0 %collective-permute-start = (f32[32,256]{1,0:T(8,128)S(1)}, f32[32,256]{1,0:T(8,128)S(1)}, u32[]{:S(2)}, u32[]{:S(2)}) collective-permute-start(f32[32,256]{1,0:T(8,128)S(1)} %bitcast.24), channel_id=1, source_target_pairs={{0,10},{1,11},{16,26},{17,27},{32,42},{33,43},{48,58},{49,59},{64,... | collective-permute-start | bytes 98312 | tf_op jit(solution)/shard_map/ppermute | solution.py:356
  28.0 2.9 %collective-permute-start.1 = (f32[32,256]{1,0:T(8,128)S(1)}, f32[32,256]{1,0:T(8,128)S(1)}, u32[]{:S(2)}, u32[]{:S(2)}) collective-permute-start(f32[32,256]{1,0:T(8,128)S(1)} %bitcast_add_fusion), channel_id=1, source_target_pairs={{0,14},{1,15},{10,6},{11,7},{16,30},{17,31},{26,22},{27,23},{32,46... | collective-permute-start | bytes 98312 | tf_op jit(solution)/shard_map/ppermute | solution.py:356
  30.8 2.9 %collective-permute-start.2 = (f32[32,256]{1,0:T(8,128)S(1)}, f32[32,256]{1,0:T(8,128)S(1)}, u32[]{:S(2)}, u32[]{:S(2)}) collective-permute-start(f32[32,256]{1,0:T(8,128)S(1)} %add.26), channel_id=1, source_target_pairs={{0,2},{1,3},{14,12},{15,13},{10,8},{11,9},{6,4},{7,5},{16,18},{17,... | collective-permute-start | bytes 98312 | tf_op jit(solution)/shard_map/ppermute | solution.py:356
  35.1 25.3 %collective-permute-start.4 = (f32[1024,256]{1,0:T(8,128)S(1)}, f32[1024,256]{1,0:T(8,128)}, u32[]{:S(2)}, u32[]{:S(2)}) collective-permute-start(f32[1024,256]{1,0:T(8,128)S(1)} %fusion), channel_id=1, source_target_pairs={{0,12},{1,13},{8,4},{9,5},{16,28},{17,29},{24,20},{25,21},{32,44},... | collective-permute-start | bytes 3145736 | tf_op jit(solution)/shard_map/ppermute | solution.py:356
  44.6 24.9 %all-to-all-start.1 = ((f32[16,96,256]{2,1,0:T(8,128)}), f32[16,96,256]{2,1,0:T(8,128)S(1)}, u32[]{:S(2)}, u32[]{:S(2)}) async-start(f32[16,96,256]{2,1,0:T(8,128)} %pad_maximum_fusion), calls=%async_computation.1 | async-start | bytes 3145728 | tf_op jit(solution)/shard_map/all_to_all | solution.py:377
  69.6 3.8 %collective-permute-start.6 = (f32[16,2,16,256]{3,2,1,0:T(8,128)S(1)}, f32[16,2,16,256]{3,2,1,0:T(8,128)S(1)}, u32[]{:S(2)}, u32[]{:S(2)}) collective-permute-start(f32[16,2,16,256]{3,2,1,0:T(8,128)S(1)} %bitcast.18), channel_id=1, source_target_pairs={{0,1},{1,0},{2,3},{3,2},{4,5},{5,4},{6,7},{7,6},{8,9},{9,8},{10,11... | collective-permute-start | bytes 1572872 | tf_op jit(solution)/shard_map/ppermute | solution.py:384
  69.8 3.7 %collective-permute-start.5 = (f32[64,256]{1,0:T(8,128)S(1)}, f32[64,256]{1,0:T(8,128)S(1)}, u32[]{:S(2)}, u32[]{:S(2)}) collective-permute-start(f32[64,256]{1,0:T(8,128)S(1)} %get-tuple-element.45), channel_id=1, source_target_pairs={{0,1},{1,0},{2,3},{3,2},{4,5},{5,4},{6,7},{7,6},{8,9},{9,8},{10,11... | collective-permute-start | bytes 196616 | tf_op jit(solution)/shard_map/ppermute | solution.py:386
  70.3 28.4 %collective-permute-start.7 = (f32[1024,256]{1,0:T(8,128)}, f32[1024,256]{1,0:T(8,128)}, u32[]{:S(2)}, u32[]{:S(2)}) collective-permute-start(f32[1024,256]{1,0:T(8,128)} %add.29), channel_id=1, source_target_pairs={{0,14},{1,15},{12,10},{13,11},{8,6},{9,7},{4,2},{5,3},{16,30},{17,... | collective-permute-start | bytes 3145736 | tf_op jit(solution)/shard_map/ppermute | solution.py:356
  75.0 6.1 %copy-start = (s32[2]{0:T(128)S(1)}, s32[2]{0:T(128)}, u32[]{:S(2)}) copy-start(s32[2]{0:T(128)} %meanwhile.1.pos_ref) | copy-start | bytes 28
  75.0 37.0 %all-to-all-start.2 = ((f32[16,2,4,16,256]{4,3,2,1,0:T(8,128)}), f32[16,2,4,16,256]{4,3,2,1,0:T(8,128)S(1)}, u32[]{:S(2)}, u32[]{:S(2)}) async-start(f32[16,2,4,16,256]{4,3,2,1,0:T(8,128)} %broadcast_in_dim.25), calls=%async_computation.2 | async-start | bytes 4194304 | tf_op jit(solution)/shard_map/all_to_all | solution.py:389
  100.5 3.0 %collective-permute-start.8 = (f32[1024,256]{1,0:T(8,128)S(1)}, f32[1024,256]{1,0:T(8,128)S(1)}, u32[]{:S(2)}, u32[]{:S(2)}) collective-permute-start(f32[1024,256]{1,0:T(8,128)S(1)} %add.32.mine_ref), channel_id=1, source_target_pairs={{0,1},{1,0},{2,3},{3,2},{4,5},{5,4},{6,7},{7,6},{8,9},{9,8},{10,11... | collective-permute-start | bytes 3145736 | tf_op jit(solution)/shard_map/ppermute | solution.py:392

commit v8 on v7

--- a/solution.py
+++ b/solution.py
@@ -128,7 +128,8 @@
         if k < 3:
             row = dot_nn(w, s_ref[lo:hi, hi:])
             s_ref[lo:hi, hi:] = row
-            s_ref[hi:, hi:] = s_ref[hi:, hi:] - dot_tn(row, row)
+            for at in range(hi, 2 * NB, HB):
+                s_ref[at:at + HB, at:] = s_ref[at:at + HB, at:] - dot_tn(row[:, at - hi:at - hi + HB], row[:, at - hi:])
             l_ref[hi:, lo:hi] = row.T
         if k % 2 == 1:
             w_ref[lo:hi, lo - HB:lo] = -dot_nn(w, dot_nn(l_ref[lo:hi, lo - HB:lo], w_ref[lo - HB:lo, lo - HB:lo]))

time: 120 us -> 120 us (level)
  no operation moved by 1% of the time
where the time goes in v8:
time: 120 us; the launch traced here: 119 us
  starting transfers between devices  34.5 us (29%)
  Pallas kernels  33.1 us (28%)
  waiting for transfers between devices  22.8 us (19%)
  blocking collectives  17.5 us (15%)
  other arithmetic  8.56 us (7%)
  local copies, waits for them, and re-layouts  2.73 us (2%)
    ppermute x6, starting transfers between devices, along_z(): return lax.ppermute(x, ('row', 'col'), pairs)  20.5 us
    all_to_all x1, blocking collectives, per_device(): lax.all_to_all(x[:NB].reshape(16, 16, NB), 'row', 0, 0, tiled=True)[0:2]  17.5 us
    pallas_call x1, Pallas kernels, factor(): pl.pallas_call(factor_kernel, out_shape=[both] * 2, in_specs=[SMEM, VMEM,...  17.2 us
    ppermute x6, waiting for transfers between devices, along_z(): return lax.ppermute(x, ('row', 'col'), pairs)  11.6 us
    pallas_call x1, Pallas kernels, solve_rows(): pl.pallas_call(rows_kernel, out_shape=[pltpu.HBM(p.shape, F32), pltpu.HBM...  7.44 us
    pallas_call x1, Pallas kernels, update(): pl.pallas_call(update_kernel, out_shape=jax.ShapeDtypeStruct(a.shape, F32...  7.29 us
    all_to_all x1, starting transfers between devices, per_device(): held = lax.all_to_all(pieces, 'row', 0, 0, tiled=True)  7.02 us
    all_to_all x1, waiting for transfers between devices, per_device(): held = lax.all_to_all(pieces, 'row', 0, 0, tiled=True)  6.89 us
  transfers between devices with their start and end apart: 11, of which 7 were waited for; matrix products, arithmetic and copies ran while one was open for 7% of the time, Pallas kernels for 22%

profile of v8, /device:TPU:8, one launch (start us, length us, event | category | flops | bytes accessed | tf_op | source)
XLA Modules:
  0.0 119.5 jit_solution(4051217480505953750)
XLA Ops:
  0.0 1.3 %slice_select_fusion = f32[1024,256]{1,0:T(8,128)S(1)} fusion(f32[1024,1024]{1,0:T(8,128)} %a_hbm.1, pred[]{:T(512)S(6)} %lt.10), kind=kLoop, calls=%fused_computation.1 | loop fusion | flops 262144 | bytes 2097153 | tf_op jit(solution)/shard_map/jit(_where)/select_n | solution.py:372
  1.3 5.2 %collective-permute-start.3 = (f32[1024,256]{1,0:T(8,128)S(1)}, f32[1024,256]{1,0:T(8,128)S(1)}, u32[]{:S(2)}, u32[]{:S(2)}) collective-permute-start(f32[1024,256]{1,0:T(8,128)S(1)} %slice_select_fusion), channel_id=1, source_target_pairs={{0,8},{1,9},{16,24},{17,25},{32,34},{33,35},{48,50},{49,51},{64,68... | collective-permute-start | bytes 3145736 | tf_op jit(solution)/shard_map/ppermute | solution.py:357
  6.5 1.0 slice.25
  7.5 17.5 %all_to_all.15 = f32[16,16,256]{2,1,0:T(8,128)S(1)} all-to-all(f32[16,16,256]{2,1,0:T(8,128)S(1)} %bitcast.22), channel_id=1, replica_groups=mesh['row'=16,'col'=16] {'row'}, dimensions={0} | all-to-all | bytes 524288 | tf_op jit(solution)/shard_map/all_to_all | solution.py:368
  25.0 1.4 %collective-permute-start = (f32[32,256]{1,0:T(8,128)S(1)}, f32[32,256]{1,0:T(8,128)S(1)}, u32[]{:S(2)}, u32[]{:S(2)}) collective-permute-start(f32[32,256]{1,0:T(8,128)S(1)} %bitcast.24), channel_id=1, source_target_pairs={{0,10},{1,11},{16,26},{17,27},{32,42},{33,43},{48,58},{49,59},{64,... | collective-permute-start | bytes 98312 | tf_op jit(solution)/shard_map/ppermute | solution.py:357
  26.4 1.6 %collective-permute-done = f32[32,256]{1,0:T(8,128)S(1)} collective-permute-done((f32[32,256]{1,0:T(8,128)S(1)}, f32[32,256]{1,0:T(8,128)S(1)}, u32[]{:S(2)}, u32[]{:S(2)}) %collective-permute-start) | collective-permute-done | bytes 32800 | tf_op jit(solution)/shard_map/ppermute | solution.py:357
  28.0 1.3 %collective-permute-start.1 = (f32[32,256]{1,0:T(8,128)S(1)}, f32[32,256]{1,0:T(8,128)S(1)}, u32[]{:S(2)}, u32[]{:S(2)}) collective-permute-start(f32[32,256]{1,0:T(8,128)S(1)} %bitcast_add_fusion), channel_id=1, source_target_pairs={{0,14},{1,15},{10,6},{11,7},{16,30},{17,31},{26,22},{27,23},{32,46... | collective-permute-start | bytes 98312 | tf_op jit(solution)/shard_map/ppermute | solution.py:357
  29.3 1.6 %collective-permute-done.1 = f32[32,256]{1,0:T(8,128)S(1)} collective-permute-done((f32[32,256]{1,0:T(8,128)S(1)}, f32[32,256]{1,0:T(8,128)S(1)}, u32[]{:S(2)}, u32[]{:S(2)}) %collective-permute-start.1) | collective-permute-done | bytes 32800 | tf_op jit(solution)/shard_map/ppermute | solution.py:357
  30.8 1.3 %collective-permute-start.2 = (f32[32,256]{1,0:T(8,128)S(1)}, f32[32,256]{1,0:T(8,128)S(1)}, u32[]{:S(2)}, u32[]{:S(2)}) collective-permute-start(f32[32,256]{1,0:T(8,128)S(1)} %add.26), channel_id=1, source_target_pairs={{0,2},{1,3},{14,12},{15,13},{10,8},{11,9},{6,4},{7,5},{16,18},{17,... | collective-permute-start | bytes 98312 | tf_op jit(solution)/shard_map/ppermute | solution.py:357
  32.1 0.6 pad_add_fusion.x_ref
  32.7 1.0 collective-permute-done.2
  33.7 1.4 %fusion = f32[1024,256]{1,0:T(8,128)S(1)} fusion(f32[1024,256]{1,0:T(8,128)S(1)} %collective-permute-done.3, f32[1024,1024]{1,0:T(8,128)} %a_hbm.1, pred[]{:T(512)S(6)} %lt.10), kind=kLoop, calls=%fused_computation.8 | loop fusion | flops 524288 | bytes 3145729 | tf_op jit(solution)/shard_map/add | solution.py:373
  35.1 8.2 %collective-permute-start.4 = (f32[1024,256]{1,0:T(8,128)S(1)}, f32[1024,256]{1,0:T(8,128)}, u32[]{:S(2)}, u32[]{:S(2)}) collective-permute-start(f32[1024,256]{1,0:T(8,128)S(1)} %fusion), channel_id=1, source_target_pairs={{0,12},{1,13},{8,4},{9,5},{16,28},{17,29},{24,20},{25,21},{32,44},... | collective-permute-start | bytes 3145736 | tf_op jit(solution)/shard_map/ppermute | solution.py:357
  43.3 0.1 copy.2
  43.4 1.2 %pad_maximum_fusion = f32[16,96,256]{2,1,0:T(8,128)} fusion(f32[16,32,256]{2,1,0:T(8,128)S(1)} %broadcast_in_dim.23, f32[16,64,256]{2,1,0:T(8,128)S(1)} %bitcast.21), kind=kLoop, calls=%fused_computation | loop fusion | flops 393216 | bytes 3145728 | tf_op jit(solution)/shard_map/concatenate | solution.py:377
  44.6 7.0 %all-to-all-start.1 = ((f32[16,96,256]{2,1,0:T(8,128)}), f32[16,96,256]{2,1,0:T(8,128)S(1)}, u32[]{:S(2)}, u32[]{:S(2)}) async-start(f32[16,96,256]{2,1,0:T(8,128)} %pad_maximum_fusion), calls=%async_computation.1 | async-start | bytes 3145728 | tf_op jit(solution)/shard_map/all_to_all | solution.py:378
  51.7 1.2 meanwhile.1.pos_ref
  52.9 7.5 %collective-permute-done.4 = f32[1024,256]{1,0:T(8,128)} collective-permute-done((f32[1024,256]{1,0:T(8,128)S(1)}, f32[1024,256]{1,0:T(8,128)}, u32[]{:S(2)}, u32[]{:S(2)}) %collective-permute-start.4) | collective-permute-done | bytes 1048608 | tf_op jit(solution)/shard_map/ppermute | solution.py:357
  60.4 2.3 %add.29 = f32[1024,256]{1,0:T(8,128)} add(f32[1024,256]{1,0:T(8,128)S(1)} %fusion, f32[1024,256]{1,0:T(8,128)} %collective-permute-done.4) | non-fusion elementwise | flops 262144 | bytes 3145728 | tf_op jit(solution)/shard_map/add | solution.py:380
  62.7 6.9 %all-to-all-done.1 = f32[16,96,256]{2,1,0:T(8,128)S(1)} async-done(((f32[16,96,256]{2,1,0:T(8,128)}), f32[16,96,256]{2,1,0:T(8,128)S(1)}, u32[]{:S(2)}, u32[]{:S(2)}) %all-to-all-start.1) | async-done | bytes 1572896 | tf_op jit(solution)/shard_map/all_to_all | solution.py:378
  69.6 0.1 collective-permute-start.6
  69.8 0.6 collective-permute-start.5
  70.3 3.1 %collective-permute-start.7 = (f32[1024,256]{1,0:T(8,128)}, f32[1024,256]{1,0:T(8,128)}, u32[]{:S(2)}, u32[]{:S(2)}) collective-permute-start(f32[1024,256]{1,0:T(8,128)} %add.29), channel_id=1, source_target_pairs={{0,14},{1,15},{12,10},{13,11},{8,6},{9,7},{4,2},{5,3},{16,30},{17,... | collective-permute-start | bytes 3145736 | tf_op jit(solution)/shard_map/ppermute | solution.py:357
  73.4 1.6 %broadcast_in_dim.25 = f32[16,2,4,16,256]{4,3,2,1,0:T(8,128)} broadcast(f32[2,4,16,256]{3,2,1,0:T(8,128)S(1)} %maximum_bitcast_fusion), dimensions={1,2,3,4} | broadcast | bytes 2228224 | tf_op jit(solution)/shard_map/broadcast_in_dim | solution.py:390
  75.0 6.1 %all-to-all-start.2 = ((f32[16,2,4,16,256]{4,3,2,1,0:T(8,128)}), f32[16,2,4,16,256]{4,3,2,1,0:T(8,128)S(1)}, u32[]{:S(2)}, u32[]{:S(2)}) async-start(f32[16,2,4,16,256]{4,3,2,1,0:T(8,128)} %broadcast_in_dim.25), calls=%async_computation.2 | async-start | bytes 4194304 | tf_op jit(solution)/shard_map/all_to_all | solution.py:390
  81.1 17.2 %factor_lead.1 = (f32[512,512]{1,0:T(8,128)S(1)}, f32[512,512]{1,0:T(8,128)S(1)}) custom-call(s32[2]{0:T(128)S(1)} %copy-done, f32[16,2,16,256]{3,2,1,0:T(8,128)S(1)} %bitcast.19, f32[16,2,16,256]{3,2,1,0:T(8,128)S(1)} %collective-permute-done.6.theirs_ref), custom_call_target="tpu_custom_call" | custom-call | flops 1000000 | bytes 4000000 | tf_op jit(solution)/shard_map/factor_lead/pallas_call | solution.py:141
  98.3 1.7 %add.32.mine_ref = f32[1024,256]{1,0:T(8,128)S(1)} add(f32[1024,256]{1,0:T(8,128)} %add.29, f32[1024,256]{1,0:T(8,128)} %collective-permute-done.7) | non-fusion elementwise | flops 262144 | bytes 3145728 | tf_op jit(solution)/shard_map/add | solution.py:392
  100.0 0.3 collective-permute-start.8
  100.3 2.6 %collective-permute-done.8.other_ref = f32[1024,256]{1,0:T(8,128)S(1)} collective-permute-done((f32[1024,256]{1,0:T(8,128)S(1)}, f32[1024,256]{1,0:T(8,128)S(1)}, u32[]{:S(2)}, u32[]{:S(2)}) %collective-permute-start.8) | collective-permute-done | bytes 1048608 | tf_op jit(solution)/shard_map/ppermute | solution.py:393
  102.9 7.4 %solve_rows.1 = (f32[1024,256]{1,0:T(8,128)}, bf16[1024,1536]{1,0:T(8,128)(2,1)}) custom-call(s32[2]{0:T(128)S(1)} %copy-done, f32[1024,256]{1,0:T(8,128)S(1)} %add.32.mine_ref, f32[1024,256]{1,0:T(8,128)S(1)} %collective-permute-done.8.other_ref, f32[512,512]{1,0:T(8,128)S(1)} %get-tuple-element.39.l_ref, f32[512,512]{1,0:T(8,128)S(1)} %get-tuple-element.40.w_ref), custom_call_target="tpu_custom_call" | custom-call | flops 1000000 | bytes 5000000 | tf_op jit(solution)/shard_map/solve_rows/pallas_call | solution.py:214
  110.4 1.6 %all-to-all-done.2.gc_ref = f32[16,2,4,16,256]{4,3,2,1,0:T(8,128)S(1)} async-done(((f32[16,2,4,16,256]{4,3,2,1,0:T(8,128)}), f32[16,2,4,16,256]{4,3,2,1,0:T(8,128)S(1)}, u32[]{:S(2)}, u32[]{:S(2)}) %all-to-all-start.2) | async-done | bytes 2097184 | tf_op jit(solution)/shard_map/all_to_all | solution.py:390
  112.0 7.3 %update.1 = f32[1024,1024]{1,0:T(8,128)} custom-call(s32[2]{0:T(128)S(1)} %copy-done, f32[1024,1024]{1,0:T(8,128)} %a_hbm.1, f32[1024,256]{1,0:T(8,128)} %get-tuple-element.41.p_hbm, bf16[1024,1536]{1,0:T(8,128)(2,1)} %get-tuple-element.42.q_hbm, f32[16,2,4,16,256]{4,3,2,1,0:T(8,128)S(1)} %all-to-all-done.2.gc_ref), custom_call_target="tpu_custom_call" | custom-call | flops 8000000000 | bytes 13000000 | tf_op jit(solution)/shard_map/update/pallas_call | solution.py:317
  (14 shorter events, 0.1 us)
Async XLA Ops:
  1.3 32.4 %collective-permute-start.3 = (f32[1024,256]{1,0:T(8,128)S(1)}, f32[1024,256]{1,0:T(8,128)S(1)}, u32[]{:S(2)}, u32[]{:S(2)}) collective-permute-start(f32[1024,256]{1,0:T(8,128)S(1)} %slice_select_fusion), channel_id=1, source_target_pairs={{0,8},{1,9},{16,24},{17,25},{32,34},{33,35},{48,50},{49,51},{64,68... | collective-permute-start | bytes 3145736 | tf_op jit(solution)/shard_map/ppermute | solution.py:357
  25.0 3.0 %collective-permute-start = (f32[32,256]{1,0:T(8,128)S(1)}, f32[32,256]{1,0:T(8,128)S(1)}, u32[]{:S(2)}, u32[]{:S(2)}) collective-permute-start(f32[32,256]{1,0:T(8,128)S(1)} %bitcast.24), channel_id=1, source_target_pairs={{0,10},{1,11},{16,26},{17,27},{32,42},{33,43},{48,58},{49,59},{64,... | collective-permute-start | bytes 98312 | tf_op jit(solution)/shard_map/ppermute | solution.py:357
  28.0 2.9 %collective-permute-start.1 = (f32[32,256]{1,0:T(8,128)S(1)}, f32[32,256]{1,0:T(8,128)S(1)}, u32[]{:S(2)}, u32[]{:S(2)}) collective-permute-start(f32[32,256]{1,0:T(8,128)S(1)} %bitcast_add_fusion), channel_id=1, source_target_pairs={{0,14},{1,15},{10,6},{11,7},{16,30},{17,31},{26,22},{27,23},{32,46... | collective-permute-start | bytes 98312 | tf_op jit(solution)/shard_map/ppermute | solution.py:357
  30.8 2.9 %collective-permute-start.2 = (f32[32,256]{1,0:T(8,128)S(1)}, f32[32,256]{1,0:T(8,128)S(1)}, u32[]{:S(2)}, u32[]{:S(2)}) collective-permute-start(f32[32,256]{1,0:T(8,128)S(1)} %add.26), channel_id=1, source_target_pairs={{0,2},{1,3},{14,12},{15,13},{10,8},{11,9},{6,4},{7,5},{16,18},{17,... | collective-permute-start | bytes 98312 | tf_op jit(solution)/shard_map/ppermute | solution.py:357
  35.1 25.3 %collective-permute-start.4 = (f32[1024,256]{1,0:T(8,128)S(1)}, f32[1024,256]{1,0:T(8,128)}, u32[]{:S(2)}, u32[]{:S(2)}) collective-permute-start(f32[1024,256]{1,0:T(8,128)S(1)} %fusion), channel_id=1, source_target_pairs={{0,12},{1,13},{8,4},{9,5},{16,28},{17,29},{24,20},{25,21},{32,44},... | collective-permute-start | bytes 3145736 | tf_op jit(solution)/shard_map/ppermute | solution.py:357
  44.6 24.9 %all-to-all-start.1 = ((f32[16,96,256]{2,1,0:T(8,128)}), f32[16,96,256]{2,1,0:T(8,128)S(1)}, u32[]{:S(2)}, u32[]{:S(2)}) async-start(f32[16,96,256]{2,1,0:T(8,128)} %pad_maximum_fusion), calls=%async_computation.1 | async-start | bytes 3145728 | tf_op jit(solution)/shard_map/all_to_all | solution.py:378
  69.6 3.8 %collective-permute-start.6 = (f32[16,2,16,256]{3,2,1,0:T(8,128)S(1)}, f32[16,2,16,256]{3,2,1,0:T(8,128)S(1)}, u32[]{:S(2)}, u32[]{:S(2)}) collective-permute-start(f32[16,2,16,256]{3,2,1,0:T(8,128)S(1)} %bitcast.18), channel_id=1, source_target_pairs={{0,1},{1,0},{2,3},{3,2},{4,5},{5,4},{6,7},{7,6},{8,9},{9,8},{10,11... | collective-permute-start | bytes 1572872 | tf_op jit(solution)/shard_map/ppermute | solution.py:385
  69.8 3.7 %collective-permute-start.5 = (f32[64,256]{1,0:T(8,128)S(1)}, f32[64,256]{1,0:T(8,128)S(1)}, u32[]{:S(2)}, u32[]{:S(2)}) collective-permute-start(f32[64,256]{1,0:T(8,128)S(1)} %get-tuple-element.45), channel_id=1, source_target_pairs={{0,1},{1,0},{2,3},{3,2},{4,5},{5,4},{6,7},{7,6},{8,9},{9,8},{10,11... | collective-permute-start | bytes 196616 | tf_op jit(solution)/shard_map/ppermute | solution.py:387
  70.3 28.0 %collective-permute-start.7 = (f32[1024,256]{1,0:T(8,128)}, f32[1024,256]{1,0:T(8,128)}, u32[]{:S(2)}, u32[]{:S(2)}) collective-permute-start(f32[1024,256]{1,0:T(8,128)} %add.29), channel_id=1, source_target_pairs={{0,14},{1,15},{12,10},{13,11},{8,6},{9,7},{4,2},{5,3},{16,30},{17,... | collective-permute-start | bytes 3145736 | tf_op jit(solution)/shard_map/ppermute | solution.py:357
  75.0 6.1 %copy-start = (s32[2]{0:T(128)S(1)}, s32[2]{0:T(128)}, u32[]{:S(2)}) copy-start(s32[2]{0:T(128)} %meanwhile.1.pos_ref) | copy-start | bytes 28
  75.0 37.0 %all-to-all-start.2 = ((f32[16,2,4,16,256]{4,3,2,1,0:T(8,128)}), f32[16,2,4,16,256]{4,3,2,1,0:T(8,128)S(1)}, u32[]{:S(2)}, u32[]{:S(2)}) async-start(f32[16,2,4,16,256]{4,3,2,1,0:T(8,128)} %broadcast_in_dim.25), calls=%async_computation.2 | async-start | bytes 4194304 | tf_op jit(solution)/shard_map/all_to_all | solution.py:390
  100.0 3.0 %collective-permute-start.8 = (f32[1024,256]{1,0:T(8,128)S(1)}, f32[1024,256]{1,0:T(8,128)S(1)}, u32[]{:S(2)}, u32[]{:S(2)}) collective-permute-start(f32[1024,256]{1,0:T(8,128)S(1)} %add.32.mine_ref), channel_id=1, source_target_pairs={{0,1},{1,0},{2,3},{3,2},{4,5},{5,4},{6,7},{7,6},{8,9},{9,8},{10,11... | collective-permute-start | bytes 3145736 | tf_op jit(solution)/shard_map/ppermute | solution.py:393
